TPU v7x, 256 devices: a whole 4x4x8 slice. The times are simulated.
256 devices in a mesh: band: 32 (over z_hi, x, core), grid: 8 (over y, z_lo).
Axes of the slice: x: 4, y: 4, z: 8 (z_hi: 4, z_lo: 2; z = z_hi * 2 + z_lo), core: 2. Of those that a mesh axis runs over, the one named last changes fastest.
Arguments:
- orbitals: float32 [64, 72, 5184], P('band', 'grid'), may hold values from -4 to 4
- block_owner: int32 [2], replicated, may hold values from 0 to 31
Outputs:
- exchange_field: float32 [64, 72, 5184], P('band', 'grid')
- block_field: float32 [2, 2, 72, 5184], P(None, None, 'grid', 'band')
All inputs are finite; a program needn't handle non-finite values.
Results may differ from a plain program's by a relative error of at most 0.00023.
Values sent between devices are 32-bit elements; how exact they have to be, the bound alone decides.
No kernel may reach another device: no remote copies, remote signals or barrier semaphores. Data moves between devices by JAX's collectives and lax.ppermute only.
A program may use at most 64 MiB of HBM per device.

v0:
```python
import math

import jax
import jax.numpy as jnp
from jax import lax
from jax.sharding import PartitionSpec as P

GRID = 72
BLK = 2
NBLK = 2


def broadcast(x, axis, root):
    mine = lax.axis_index(axis) == root
    return lax.psum(jnp.where(mine, x, jnp.zeros_like(x)), axis)


def contract(values, table, form):
    return jnp.einsum(form, values, table, precision=lax.Precision.HIGHEST)


def folded_freqs(points, edge_cells):
    return jnp.where(points > edge_cells // 2, points - edge_cells, points)


def on_device(orbitals, block_owner):
    local_count = orbitals.shape[0]
    slab_planes = orbitals.shape[1]
    edge_cells = GRID
    half_cells = edge_cells // 2 + 1
    orbital_grid = orbitals.reshape(local_count, slab_planes, edge_cells, edge_cells)
    columns = edge_cells // lax.axis_size("grid")
    scale = math.sqrt(edge_cells**3 / (local_count * lax.axis_size("band")))
    points = jnp.arange(edge_cells, dtype=jnp.int32)
    angle = (
        2.0
        * math.pi
        / edge_cells
        * (points[:, None] * points[None, :] % edge_cells).astype(jnp.float32)
    )
    cos_full = jnp.cos(angle)
    sin_full = jnp.sin(angle)
    cos_half = cos_full[:, :half_cells]
    sin_half = sin_full[:, :half_cells]
    edge_freq = (points[:half_cells] == 0) | (points[:half_cells] == edge_cells // 2)
    weights = jnp.where(edge_freq, 1.0, 2.0).astype(jnp.float32) / float(edge_cells**3)
    inv_cos = weights[:, None] * cos_full[:half_cells, :]
    inv_sin = weights[:, None] * sin_full[:half_cells, :]
    folded_all = folded_freqs(points, edge_cells)
    folded_last = folded_all[:half_cells]
    first_table = jnp.stack([cos_half, -sin_half], axis=0)
    forward_table = jnp.stack(
        [jnp.stack([cos_full, -sin_full], axis=0), jnp.stack([sin_full, cos_full], axis=0)], axis=0
    )
    inverse_table = jnp.stack(
        [jnp.stack([cos_full, sin_full], axis=0), jnp.stack([-sin_full, cos_full], axis=0)], axis=0
    )
    final_table = jnp.stack([inv_cos, -inv_sin], axis=0)
    field = jnp.zeros((local_count, slab_planes, edge_cells, edge_cells), jnp.float32)
    collected = []
    for block_index in range(NBLK):
        blocks = broadcast(orbital_grid, "band", block_owner[block_index])
        members = blocks.shape[0]
        pair_density = (orbital_grid[:, None] * blocks[None]).reshape(
            local_count * members, slab_planes, edge_cells, edge_cells
        )
        section_one = contract(pair_density, first_table, "pxyn,dnk->dpxyk")
        form_mid = "cpxnk,cdnu->dpxuk"
        section_two = contract(section_one, forward_table, form_mid)
        form = "cpxyk,cdxu->dpuyk"
        spectrum = contract(
            lax.all_to_all(section_two, "grid", split_axis=3, concat_axis=2, tiled=True),
            forward_table,
            form,
        )
        rows = lax.axis_index("grid") * columns + jnp.arange(columns, dtype=jnp.int32)
        folded_rows = folded_freqs(rows, edge_cells)
        squared = (
            folded_all[:, None, None] ** 2
            + folded_rows[None, :, None] ** 2
            + folded_last[None, None, :] ** 2
        )
        kernel = jnp.where(
            squared > 0, scale / jnp.maximum(squared, 1).astype(jnp.float32), jnp.float32(0.0)
        )
        spectrum = spectrum * kernel[None, None]
        reverted = contract(spectrum, inverse_table, form)
        section_three = lax.all_to_all(reverted, "grid", split_axis=2, concat_axis=3, tiled=True)
        section_four = contract(section_three, inverse_table, form_mid)
        potential = contract(section_four, final_table, "cpxyk,ckn->pxyn").reshape(
            local_count, members, slab_planes, edge_cells, edge_cells
        )
        own_field = -jnp.sum(potential * blocks[None], axis=1)
        block_terms = -jnp.sum(potential * orbital_grid[:, None], axis=0)
        own_field, terms = (own_field, block_terms)
        field = field + own_field
        share_members = terms.shape[0]
        collected.append(
            lax.psum_scatter(
                terms.reshape(share_members, slab_planes, edge_cells * edge_cells),
                "band",
                scatter_dimension=2,
                tiled=True,
            )
        )
    shares = jnp.concatenate(collected, axis=0)
    exchange_field = field.reshape(local_count, slab_planes, edge_cells * edge_cells)
    block_field = shares.reshape(NBLK, BLK, slab_planes, shares.shape[-1])
    return (exchange_field, block_field)


def solution(mesh):
    return jax.shard_map(
        on_device,
        mesh=mesh,
        in_specs=(P("band", "grid", None), P()),
        out_specs=(P("band", "grid", None), P(None, None, "grid", "band")),
        check_vma=False,
    )
```

profile of v0, /device:TPU:2, one launch (start us, length us, event | category | flops | bytes accessed | tf_op | source)
XLA Modules:
  0.0 728.1 jit_solution(15574379052038561861)
XLA Ops:
  13.4 281.6 %all-reduce.9.cloned.1.call-done = (f32[2,9,72,72]{3,2,0,1:T(8,128)}, f32[2,9,72,72]{3,2,0,1:T(8,128)}) async-done(((f32[2,9,72,72]{3,2,0,1:T(8,128)}, f32[2,9,72,72]{3,2,0,1:T(8,128)}), (f32[2,9,72,72]{3,2,0,1:T(8,128)}, f32[2,9,72,72]{3,2,0,1:T(8,128)})) %all-reduce.9.cloned.1.call-update) | async-done | bytes 746512 | tf_op jit(solution)/shard_map/psum | solution.py:15
  297.6 3.6 fusion.67
  303.8 2.9 copy.88
  306.7 4.0 reshape.200
  310.7 5.5 all-to-all-start
  316.3 3.6 fusion.66
  322.5 2.9 copy.100
  325.4 4.0 reshape.204
  329.4 6.3 all-to-all-start.2
  337.1 4.4 reduce
  341.6 3.2 reshape.201
  345.6 5.0 fusion.8
  350.7 2.6 fusion.22
  353.3 2.9 copy.93
  356.2 4.0 reshape.202
  360.2 5.9 all-to-all-start.1
  366.1 4.4 reduce.2
  370.6 3.2 reshape.205
  374.6 5.0 fusion.5
  379.6 2.6 fusion.25
  382.2 2.9 copy.105
  385.2 4.0 reshape.206
  389.2 5.8 all-to-all-start.3
  395.4 4.4 reduce.1
  399.8 3.2 reshape.203
  403.7 6.1 fusion.2
  409.8 4.4 reduce.3
  414.2 3.2 reshape.207
  418.5 5.0 fusion
  423.5 4.3 fusion.12
  427.9 4.5 fusion.10
  438.6 280.2 %all-reduce.7.cloned.1.call-done = (f32[2,9,5184]{2,0,1:T(2,128)}, f32[2,9,5184]{2,0,1:T(2,128)}) async-done(((f32[2,9,5184]{2,0,1:T(2,128)}, f32[2,9,5184]{2,0,1:T(2,128)}), (f32[2,9,5184]{2,0,1:T(2,128)}, f32[2,9,5184]{2,0,1:T(2,128)})) %all-reduce.7.cloned.1.call-update) | async-done | bytes 746512
  (88 shorter events, 25.6 us)
Async XLA Ops:
  7.2 287.8 %all-reduce.9.cloned.1.call-start = ((), (), s32[]{:S(2)}) async-start(), calls=%async_computation.5 | async-start | bytes 2654208 | tf_op jit(solution)/shard_map/psum | solution.py:15
  12.8 284.7 %copy-start.10 = (f32[72,72]{0,1:T(8,128)}, f32[72,72]{0,1:T(8,128)S(1)}, u32[]{:S(2)}) copy-start(f32[72,72]{0,1:T(8,128)S(1)} %fusion.59) | copy-start | bytes 62212
  13.0 284.6 %copy-start.12 = (f32[72,72]{0,1:T(8,128)}, f32[72,72]{0,1:T(8,128)S(1)}, u32[]{:S(2)}) copy-start(f32[72,72]{0,1:T(8,128)S(1)} %fusion.58) | copy-start | bytes 62212
  13.4 287.8 %copy-start.4 = (f32[1,2,72,72]{3,2,0,1:T(8,128)}, f32[1,2,72,72]{3,2,0,1:T(8,128)S(1)}, u32[]{:S(2)}) copy-start(f32[1,2,72,72]{3,2,0,1:T(8,128)S(1)} %get-tuple-element.28) | copy-start | bytes 124420
  13.4 284.2 %copy-start.14 = (f32[1,72,37]{1,2,0:T(8,128)}, f32[1,72,37]{1,2,0:T(8,128)S(1)}, u32[]{:S(2)}) copy-start(f32[1,72,37]{1,2,0:T(8,128)S(1)} %get-tuple-element.34) | copy-start | bytes 31972
  13.4 284.1 %copy-start.16 = (f32[1,72,37]{1,2,0:T(8,128)}, f32[1,72,37]{1,2,0:T(8,128)S(1)}, u32[]{:S(2)}) copy-start(f32[1,72,37]{1,2,0:T(8,128)S(1)} %get-tuple-element.35) | copy-start | bytes 31972
  310.7 5.5 copy-start.1
  310.7 5.6 copy-start.15
  310.7 5.6 copy-start.17
  310.7 18.7 %all-to-all-start = ((f32[8,1,23976]{2,1,0:T(1,128)}), f32[8,1,23976]{2,1,0:T(1,128)}, u32[]{:S(2)}, u32[]{:S(2)}) async-start(f32[8,1,23976]{2,1,0:T(1,128)} %reshape.200), calls=%async_computation | async-start | bytes 1540096 | tf_op jit(solution)/shard_map/all_to_all | solution.py:72
  316.2 3.7 copy-start.5
  329.4 30.8 %all-to-all-start.2 = ((f32[8,1,23976]{2,1,0:T(1,128)}), f32[8,1,23976]{2,1,0:T(1,128)}, u32[]{:S(2)}, u32[]{:S(2)}) async-start(f32[8,1,23976]{2,1,0:T(1,128)} %reshape.204), calls=%async_computation.2 | async-start | bytes 1540096 | tf_op jit(solution)/shard_map/all_to_all | solution.py:72
  344.8 0.9 copy-start.6
  345.6 5.0 copy-start.8
  360.2 29.0 %all-to-all-start.1 = ((f32[8,1,23976]{2,1,0:T(1,128)}), f32[8,1,23976]{2,1,0:T(1,128)}, u32[]{:S(2)}, u32[]{:S(2)}) async-start(f32[8,1,23976]{2,1,0:T(1,128)} %reshape.202), calls=%async_computation.1 | async-start | bytes 1540096 | tf_op jit(solution)/shard_map/all_to_all | solution.py:88
  373.7 0.9 copy-start.7
  374.6 5.0 copy-start.9
  389.2 6.1 copy-start.11
  389.2 6.1 copy-start.13
  389.2 20.6 %all-to-all-start.3 = ((f32[8,1,23976]{2,1,0:T(1,128)}), f32[8,1,23976]{2,1,0:T(1,128)}, u32[]{:S(2)}, u32[]{:S(2)}) async-start(f32[8,1,23976]{2,1,0:T(1,128)} %reshape.206), calls=%async_computation.3 | async-start | bytes 1540096 | tf_op jit(solution)/shard_map/all_to_all | solution.py:88
  395.0 323.7 %all-reduce.7.cloned.1.call-start = ((), (), s32[]{:S(2)}) async-start(), calls=%async_computation.4 | async-start | bytes 1511424
  418.5 5.0 copy-start
  427.8 4.5 copy-start.2
  427.8 4.5 copy-start.3
  434.5 1.4 copy-start.18
Sparse Core Ops, SparseCore 0:
  12.8 282.1 all-reduce.8
  436.0 282.7 all-reduce.6
where the time goes:
time: 741 us; the launch traced here: 728 us
  waiting for transfers between devices  562 us (76%)
  local copies, waits for them, and re-layouts  54.4 us (7%)
  matrix products  47.5 us (6%)
  starting transfers between devices  23.9 us (3%)
  other arithmetic  23.8 us (3%)
  between operations  16.7 us (2%)
    psum x1, waiting for transfers between devices, broadcast(): return lax.psum(jnp.where(mine, x, jnp.zeros_like(x)), axis)  282 us
    unnamed x3, waiting for transfers between devices  280 us
    dot_general x12, matrix products, contract(): return jnp.einsum(form, values, table, precision=lax.Precision.HIGHEST)  47.5 us
    unnamed x50, local copies, waits for them, and re-layouts  32.5 us
  transfers between devices with their start and end apart: 6, of which 2 were waited for; matrix products, arithmetic and copies ran while one was open for 11% of the time, Pallas kernels for 0%

commit v1 on v0

v1 whole, which is shorter than its diff:
```python
import math

import jax
import jax.numpy as jnp
import numpy as np
from jax import lax
from jax.experimental import pallas as pl
from jax.experimental.pallas import tpu as pltpu
from jax.sharding import PartitionSpec as P

GRID = 72
HALF = GRID // 2 + 1
KX = 40
PLANE = GRID * GRID
TILES = 41
LANES = 128
SLAB = 9
TAIL = 8 * TILES
ROWS = 384
XR = 80
BAND = 32
CHUNK = 2 * ROWS // BAND
SHARE = PLANE // BAND
PACK = 56
F32 = jnp.float32
BF16 = jnp.bfloat16
PARAMS = pltpu.CompilerParams(vmem_limit_bytes=48 * 1024 * 1024)


def split_np(table):
    high = table.astype(jnp.bfloat16)
    low = (table - high.astype(np.float64)).astype(jnp.bfloat16)
    return high, low


def tables():
    k = np.arange(GRID)
    ang = 2.0 * np.pi / GRID * ((k[:, None] * k[None, :]) % GRID)
    cos, sin = np.cos(ang), np.sin(ang)
    place = np.arange(GRID)
    plane = np.where(place < 64, SLAB * (place // 8) + place % 8, SLAB * (place - 64) + 8)
    forward_x = np.zeros((2 * KX, XR))
    forward_x[:HALF, :GRID] = cos[:HALF][:, plane]
    forward_x[KX : KX + HALF, :GRID] = -sin[:HALF][:, plane]
    weight = np.where((k[:HALF] == 0) | (k[:HALF] == GRID // 2), 1.0, 2.0) / GRID**3
    inverse_x = np.zeros((XR, 2 * KX))
    inverse_x[:GRID, :HALF] = (weight[:, None] * cos[:HALF][:, plane]).T
    inverse_x[:GRID, KX : KX + HALF] = -(weight[:, None] * sin[:HALF][:, plane]).T
    along_z = np.zeros((LANES, 2 * LANES))
    along_z[:GRID, :GRID] = cos
    along_z[:GRID, LANES : LANES + GRID] = sin
    forward_y = np.block([[cos, sin], [-sin, cos]])
    inverse_y = np.block([[cos, -sin], [sin, cos]])

    def left(table):
        high, low = split_np(table)
        return np.concatenate([high, high, low], axis=1)

    z_high, z_low = split_np(along_z)
    z_two = np.concatenate([z_high, z_high], axis=0)
    fold = np.where(k > GRID // 2, k - GRID, k).astype(np.float64)
    squares = np.ones((GRID, LANES))
    squares[:, :GRID] = fold[:, None] ** 2 + fold[None, :] ** 2
    return (
        left(forward_x),
        left(inverse_x),
        z_two,
        z_low,
        left(forward_y),
        left(inverse_y),
        squares.astype(np.float32),
    )


def split(x):
    high = x.astype(BF16)
    low = (x - high.astype(F32)).astype(BF16)
    return high, low


def left_dot(table, x):
    high, low = split(x)
    return jnp.dot(table, jnp.concatenate([high, low, high], axis=0), preferred_element_type=F32)


def right_dot(x, two, low_table):
    high, low = split(x)
    both = jnp.concatenate([high, low], axis=1)
    return jnp.dot(both, two, preferred_element_type=F32) + jnp.dot(
        high, low_table, preferred_element_type=F32
    )


def pack_kernel(orb_ref, out_ref):
    for o in range(2):
        out_ref[o, TAIL:ROWS, :] = jnp.zeros((ROWS - TAIL, LANES), F32)
        for t in range(TILES):
            wide = min(LANES, PLANE - t * LANES)
            if wide < LANES:
                out_ref[o, 8 * t : 8 * t + 8, :] = jnp.zeros((8, LANES), F32)
            cols = slice(t * LANES, t * LANES + wide)
            out_ref[o, 8 * t : 8 * t + 8, :wide] = orb_ref[o, 0:8, cols]
            out_ref[o, TAIL + t : TAIL + t + 1, :wide] = orb_ref[o, 8:9, cols]


def pack(orbitals):
    return pl.pallas_call(
        pack_kernel,
        out_shape=jax.ShapeDtypeStruct((2, ROWS, LANES), F32),
        compiler_params=PARAMS,
    )(orbitals)


def field_kernel(
    scale,
    den_ref,
    fx_ref,
    ix_ref,
    ztwo_ref,
    zlow_ref,
    fy_ref,
    iy_ref,
    sq_ref,
    out_ref,
    wide_ref,
    col_ref,
    re_ref,
    im_ref,
):
    lane = lax.broadcasted_iota(jnp.int32, (XR, LANES), 1)

    wide_ref[GRID:XR, :] = jnp.zeros((XR - GRID, TILES * LANES), F32)
    for t in range(TILES):
        cols = slice(t * LANES, (t + 1) * LANES)
        for s in range(8):
            wide_ref[8 * s : 8 * s + 8, cols] = den_ref[s, 8 * t : 8 * t + 8, :]
            wide_ref[64 + s : 65 + s, cols] = den_ref[s, TAIL + t : TAIL + t + 1, :]
    for t in range(0, TILES, 4):
        cols = slice(t * LANES, min(t + 4, TILES) * LANES)
        wide_ref[:, cols] = left_dot(fx_ref[...], wide_ref[:, cols])

    for y in range(GRID):
        t, off = divmod(y * GRID, LANES)
        value = wide_ref[:, t * LANES : (t + 1) * LANES]
        if off:
            value = pltpu.roll(value, LANES - off, 1)
            if off + GRID > LANES:
                after = pltpu.roll(wide_ref[:, (t + 1) * LANES : (t + 2) * LANES], LANES - off, 1)
                value = jnp.where(lane < LANES - off, value, after)
        col_ref[y * XR : (y + 1) * XR, :] = value

    def forward_z(j, carry):
        base = pl.multiple_of(j * 8 * XR, 8 * XR)
        both = right_dot(col_ref[pl.ds(base, 8 * XR), :], ztwo_ref[...], zlow_ref[...])
        base = pl.multiple_of(j * 8 * KX, 8 * KX)
        for y in range(8):
            real = both[y * XR : y * XR + KX]
            imag = both[y * XR + KX : (y + 1) * XR]
            rows = pl.ds(base + y * KX, KX)
            re_ref[rows, :] = real[:, :LANES] + imag[:, LANES:]
            im_ref[rows, :] = imag[:, :LANES] - real[:, LANES:]
        return carry

    lax.fori_loop(0, GRID // 8, forward_z, 0)

    def along_y(j, carry):
        parts = []
        for q in range(2):
            rows = pl.ds(2 * j + q, GRID, stride=KX)
            parts.append(jnp.concatenate([re_ref[rows, :], im_ref[rows, :]], axis=0))
        spec = left_dot(fy_ref[...], jnp.concatenate(parts, axis=1))
        factors = []
        for q in range(2):
            kx = (2 * j + q).astype(F32)
            square = sq_ref[...] + kx * kx
            factor = jnp.where(square > 0, scale / jnp.maximum(square, 1.0), 0.0)
            factors.append(jnp.concatenate([factor, factor], axis=0))
        spec = spec * jnp.concatenate(factors, axis=1)
        back = left_dot(iy_ref[...], spec)
        for q in range(2):
            rows = pl.ds(2 * j + q, GRID, stride=KX)
            cols = slice(q * LANES, (q + 1) * LANES)
            re_ref[rows, :] = back[:GRID, cols]
            im_ref[rows, :] = back[GRID:, cols]
        return carry

    lax.fori_loop(0, (HALF + 1) // 2, along_y, 0)

    def inverse_z(j, carry):
        base = pl.multiple_of(j * 8 * KX, 8 * KX)
        rows = pl.ds(base, 8 * KX)
        real = right_dot(re_ref[rows, :], ztwo_ref[...], zlow_ref[...])
        imag = right_dot(im_ref[rows, :], ztwo_ref[...], zlow_ref[...])
        new_re = real[:, :LANES] - imag[:, LANES:]
        new_im = real[:, LANES:] + imag[:, :LANES]
        base = pl.multiple_of(j * 8 * XR, 8 * XR)
        for y in range(8):
            col_ref[pl.ds(base + y * XR, KX), :] = new_re[y * KX : (y + 1) * KX]
            col_ref[pl.ds(base + y * XR + KX, KX), :] = new_im[y * KX : (y + 1) * KX]
        return carry

    lax.fori_loop(0, GRID // 8, inverse_z, 0)

    for t in range(TILES):
        value = jnp.zeros((XR, LANES), F32)
        for y in range(GRID):
            at = y * GRID - t * LANES
            if at >= LANES or at + GRID <= 0:
                continue
            piece = col_ref[y * XR : (y + 1) * XR, :]
            if at % LANES:
                piece = pltpu.roll(piece, at % LANES, 1)
            keep = (lane >= at) & (lane < at + GRID)
            value = jnp.where(keep, piece, value)
        wide_ref[:, t * LANES : (t + 1) * LANES] = value
    for t in range(0, TILES, 4):
        last = min(t + 4, TILES)
        cols = slice(t * LANES, last * LANES)
        pot = left_dot(ix_ref[...], wide_ref[:, cols])
        for u in range(t, last):
            part = pot[:, (u - t) * LANES : (u - t + 1) * LANES]
            for s in range(8):
                out_ref[s, 8 * u : 8 * u + 8, :] = part[8 * s : 8 * s + 8]
                out_ref[s, TAIL + u : TAIL + u + 1, :] = part[64 + s : 65 + s]
    for s in range(8):
        out_ref[s, TAIL + TILES : ROWS, :] = jnp.zeros((ROWS - TAIL - TILES, LANES), F32)


def potentials(densities, scale):
    def body(*refs):
        field_kernel(scale, *refs)

    return pl.pallas_call(
        body,
        out_shape=jax.ShapeDtypeStruct((8, ROWS, LANES), F32),
        scratch_shapes=[
            pltpu.VMEM((XR, TILES * LANES), F32),
            pltpu.VMEM((GRID * XR, LANES), F32),
            pltpu.VMEM((GRID * KX, LANES), F32),
            pltpu.VMEM((GRID * KX, LANES), F32),
        ],
        compiler_params=PARAMS,
    )(densities, *[jnp.asarray(t) for t in tables()])


def sums_kernel(pot_ref, orb_ref, blk_ref, field_ref, share_ref, wide_ref):
    wide_ref[32:40, :] = jnp.zeros((8, TILES * LANES), F32)
    for i in range(2):
        for t in range(TILES + 1):
            tail = t == TILES
            rows = slice(TAIL, ROWS) if tail else slice(8 * t, 8 * t + 8)
            total = blk_ref[0, rows, :] * pot_ref[4 * i, rows, :]
            for b in range(1, 4):
                total = total + blk_ref[b, rows, :] * pot_ref[4 * i + b, rows, :]
            total = -total
            if tail:
                for u in range(TILES):
                    wide = min(LANES, PLANE - u * LANES)
                    field_ref[i, 8:9, u * LANES : u * LANES + wide] = total[u : u + 1, :wide]
            else:
                wide = min(LANES, PLANE - t * LANES)
                field_ref[i, 0:8, t * LANES : t * LANES + wide] = total[:, :wide]
    for b in range(4):
        for t in range(TILES + 1):
            tail = t == TILES
            rows = slice(TAIL, ROWS) if tail else slice(8 * t, 8 * t + 8)
            total = -(
                orb_ref[0, rows, :] * pot_ref[b, rows, :]
                + orb_ref[1, rows, :] * pot_ref[4 + b, rows, :]
            )
            if tail:
                for u in range(TILES):
                    wide_ref[32 + b : 33 + b, u * LANES : (u + 1) * LANES] = total[u : u + 1]
            else:
                wide_ref[8 * b : 8 * b + 8, t * LANES : (t + 1) * LANES] = total
    lane = lax.broadcasted_iota(jnp.int32, (40, LANES), 1)
    rest = SHARE - LANES

    def cut(start):
        t, off = divmod(start, LANES)
        value = wide_ref[:, t * LANES : (t + 1) * LANES]
        if off:
            value = pltpu.roll(value, LANES - off, 1)
            if t + 1 < TILES:
                after = pltpu.roll(wide_ref[:, (t + 1) * LANES : (t + 2) * LANES], LANES - off, 1)
                value = jnp.where(lane < LANES - off, value, after)
        return value

    for r in range(BAND):
        share_ref[r, 0:40, :] = cut(r * SHARE)
        more = cut(r * SHARE + LANES)
        low, mid, top = more[0:16], more[16:32], more[32:40]
        mid = pltpu.roll(mid, rest, 1)
        top = jnp.concatenate([pltpu.roll(top, 2 * rest, 1), jnp.zeros((8, LANES), F32)], axis=0)
        where = lane[:16]
        share_ref[r, 40:56, :] = jnp.where(
            where < rest, low, jnp.where(where < 2 * rest, mid, top)
        )


def sums(pot, packed, blocks):
    return pl.pallas_call(
        sums_kernel,
        out_shape=(
            jax.ShapeDtypeStruct((2, SLAB, PLANE), F32),
            jax.ShapeDtypeStruct((BAND, PACK, LANES), F32),
        ),
        scratch_shapes=[pltpu.VMEM((40, TILES * LANES), F32)],
        compiler_params=PARAMS,
    )(pot, packed, blocks)


def share_kernel(part_ref, out_ref):
    total = part_ref[0]
    for r in range(1, BAND):
        total = total + part_ref[r]
    rest = SHARE - LANES
    tail = total[40:56]
    tails = [tail, pltpu.roll(tail, LANES - rest, 1), pltpu.roll(tail, LANES - 2 * rest, 1)]
    for b in range(4):
        at = (b // 2, b % 2)
        out_ref[at[0], at[1], 0:8, :LANES] = total[8 * b : 8 * b + 8]
        more = tails[b // 2][8 * (b % 2) : 8 * (b % 2) + 8]
        out_ref[at[0], at[1], 0:8, LANES:SHARE] = more[:, :rest]
        out_ref[at[0], at[1], 8:9, :LANES] = total[32 + b : 33 + b]
        out_ref[at[0], at[1], 8:9, LANES:SHARE] = tails[2][b : b + 1, :rest]


def share(parts):
    return pl.pallas_call(
        share_kernel,
        out_shape=jax.ShapeDtypeStruct((2, 2, SLAB, SHARE), F32),
        compiler_params=PARAMS,
    )(parts)


def on_device(orbitals, block_owner):
    scale = math.sqrt(GRID**3 / (2 * BAND))
    packed = pack(orbitals)
    pieces = lax.all_to_all(packed.reshape(BAND, CHUNK, LANES), "band", 0, 0)
    mine = jnp.take(pieces, block_owner, axis=0, mode="clip")
    spread = jnp.broadcast_to(mine[None], (BAND, 2, CHUNK, LANES))
    gathered = lax.all_to_all(spread, "band", 0, 0)
    blocks = gathered.transpose(1, 0, 2, 3).reshape(4, ROWS, LANES)
    densities = (packed[:, None] * blocks[None]).reshape(8, ROWS, LANES)
    whole = lax.all_to_all(densities, "grid", 0, 0)
    pot = potentials(whole, scale)
    pot = lax.all_to_all(pot, "grid", 0, 0)
    field, shares = sums(pot, packed, blocks)
    block_field = share(lax.all_to_all(shares, "band", 0, 0))
    return field, block_field


def solution(mesh):
    return jax.shard_map(
        on_device,
        mesh=mesh,
        in_specs=(P("band", "grid", None), P()),
        out_specs=(P("band", "grid", None), P(None, None, "grid", "band")),
        check_vma=False,
    )
```

time: 741 us -> 164 us (0.22); the launches traced: 728 us -> 161 us
  waiting for transfers between devices: 562 us -> 37.7 us
  blocking collectives: 0 us -> 76.5 us
  local copies, waits for them, and re-layouts: 54.4 us -> 3.34 us
  matrix products: 47.5 us -> 0 us
  other arithmetic: 23.8 us -> 1.11 us
  Pallas kernels: 0 us -> 22.6 us
  between operations: 16.7 us -> 0.79 us
    psum x1 -> x0, waiting for transfers between devices: 282 us -> none  [broadcast(): return lax.psum(jnp.where(mine, x, jnp.zeros_like(x)), axis)]
    unnamed x3 -> x0, waiting for transfers between devices: 280 us -> none
    all_to_all x0 -> x3, blocking collectives: none -> 76.5 us  [the longest x1 27.3 us: on_device(): gathered = lax.all_to_all(spread, 'band', 0, 0)]
    dot_general x12 -> x0, matrix products: 47.5 us -> none  [contract(): return jnp.einsum(form, values, table, precision=lax.Precision.HIGHEST)]
    all_to_all x4 -> x2, waiting for transfers between devices: 0.01 us -> 37.7 us  [the longest x1 23.6 us: on_device(): block_field = share(lax.all_to_all(shares, 'band', 0, 0))]
    unnamed x50 -> x19, local copies, waits for them, and re-layouts: 32.5 us -> 2.69 us
    pallas_call x0 -> x4, Pallas kernels: none -> 22.6 us  [the longest x1 17.1 us: potentials(): pl.pallas_call(body, out_shape=jax.ShapeDtypeStruct((8, ROWS, LANES), F32...]
    all_to_all x4 -> x0, other arithmetic: 17.7 us -> none  [the longest x2 8.88 us: on_device(): lax.all_to_all(section_two, 'grid', split_axis=3, concat_axis=2, tiled=True)]
  transfers between devices with their start and end apart: 6 -> 2, of which waited for: 2 -> 2; matrix products, arithmetic and copies ran while one was open for 11% -> 1% of each run, Pallas kernels for 0% -> 0%
where the time goes in v1:
time: 164 us; the launch traced here: 161 us
  blocking collectives  76.5 us (47%)
  waiting for transfers between devices  37.7 us (23%)
  Pallas kernels  22.6 us (14%)
  starting transfers between devices  18.7 us (11%)
  local copies, waits for them, and re-layouts  3.34 us (2%)
    all_to_all x1, blocking collectives, on_device(): gathered = lax.all_to_all(spread, 'band', 0, 0)  27.3 us
    all_to_all x1, blocking collectives, on_device(): whole = lax.all_to_all(densities, 'grid', 0, 0)  26.4 us
    all_to_all x1, waiting for transfers between devices, on_device(): block_field = share(lax.all_to_all(shares, 'band', 0, 0))  23.6 us
    all_to_all x1, blocking collectives, on_device(): pot = lax.all_to_all(pot, 'grid', 0, 0)  22.8 us
    pallas_call x1, Pallas kernels, potentials(): pl.pallas_call(body, out_shape=jax.ShapeDtypeStruct((8, ROWS, LANES), F32...  17.1 us
    all_to_all x1, waiting for transfers between devices, on_device(): pieces = lax.all_to_all(packed.reshape(BAND, CHUNK, LANES), 'band', 0, 0)  14.2 us
    all_to_all x1, starting transfers between devices, on_device(): pieces = lax.all_to_all(packed.reshape(BAND, CHUNK, LANES), 'band', 0, 0)  11.6 us
    all_to_all x1, starting transfers between devices, on_device(): block_field = share(lax.all_to_all(shares, 'band', 0, 0))  7.08 us
  transfers between devices with their start and end apart: 2, of which 2 were waited for; matrix products, arithmetic and copies ran while one was open for 1% of the time, Pallas kernels for 0%

profile of v1, /device:TPU:2, one launch (start us, length us, event | category | flops | bytes accessed | tf_op | source)
XLA Modules:
  0.0 160.8 jit_solution(684775070243761334)
XLA Ops:
  0.6 0.0 copy-start.7
  0.6 1.1 copy.14.orb_ref
  1.7 0.8 shard_map.104.orb_ref
  2.5 11.6 %all-to-all-start = ((f32[32,24,128]{2,1,0:T(8,128)}), f32[32,24,128]{2,1,0:T(8,128)S(1)}, u32[]{:S(2)}, u32[]{:S(2)}) async-start(f32[32,24,128]{2,1,0:T(8,128)} %bitcast), calls=%async_computation | async-start | bytes 786432 | tf_op jit(solution)/shard_map/all_to_all | solution.py:340
  14.1 0.0 copy-done.7
  14.2 14.2 %all-to-all-done = f32[32,24,128]{2,1,0:T(8,128)S(1)} async-done(((f32[32,24,128]{2,1,0:T(8,128)}), f32[32,24,128]{2,1,0:T(8,128)S(1)}, u32[]{:S(2)}, u32[]{:S(2)}) %all-to-all-start) | async-done | bytes 393248 | tf_op jit(solution)/shard_map/all_to_all | solution.py:340
  28.3 0.5 gather_fusion
  28.9 0.1 broadcast_in_dim.12
  28.9 27.3 %all_to_all.25 = f32[32,2,24,128]{3,2,1,0:T(8,128)S(1)} all-to-all(f32[32,2,24,128]{3,2,1,0:T(8,128)S(1)} %broadcast_in_dim.12), channel_id=1, replica_groups=mesh['band'=32,'grid'=8] {'band'}, dimensions={0} | all-to-all | bytes 1572864 | tf_op jit(solution)/shard_map/all_to_all | solution.py:343
  56.2 0.1 copy.15
  56.3 1.1 broadcast_multiply_fusion
  57.4 0.0 copy-start
  57.4 0.0 copy-start.1
  57.4 0.0 copy-start.2
  57.4 0.0 copy-start.3
  57.4 0.0 copy-start.4
  57.5 0.0 copy-start.5
  57.5 0.0 copy-start.6
  57.5 26.4 %all_to_all.26.refs_0_ = f32[8,384,128]{2,1,0:T(8,128)S(1)} all-to-all(f32[8,384,128]{2,1,0:T(8,128)S(1)} %bitcast.6), channel_id=1, replica_groups=mesh['band'=32,'grid'=8] {'grid'}, dimensions={0} | all-to-all | bytes 3145728 | tf_op jit(solution)/shard_map/all_to_all | solution.py:346
  83.9 0.0 copy-done
  83.9 0.0 copy-done.3
  83.9 0.0 copy-done.4
  83.9 0.0 copy-done.5
  84.0 0.0 copy-done.6
  84.0 17.1 %shard_map.105 = f32[8,384,128]{2,1,0:T(8,128)S(1)} custom-call(f32[8,384,128]{2,1,0:T(8,128)S(1)} %all_to_all.26.refs_0_, bf16[80,240]{1,0:T(8,128)(2,1)S(1)} %copy-done.5, bf16[80,240]{1,0:T(8,128)(2,1)S(1)} %copy-done.4, bf16[256,256]{1,0:T(8,128)(2,1)S(1)} %copy-done.2, bf16[128,256]{1,0:T(8,128)(2,1)S(1)} %copy-done.3, bf16[144,432]{1,0:T(8,128)(2,1)S(1)} %copy-done.1, ...), custom_call_target="tpu_custom_call" | custom-call | tf_op jit(solution)/shard_map/pallas_call | solution.py:233
  101.1 22.8 %all_to_all.27.pot_ref = f32[8,384,128]{2,1,0:T(8,128)S(1)} all-to-all(f32[8,384,128]{2,1,0:T(8,128)S(1)} %shard_map.105), channel_id=1, replica_groups=mesh['band'=32,'grid'=8] {'grid'}, dimensions={0} | all-to-all | bytes 3145728 | tf_op jit(solution)/shard_map/all_to_all | solution.py:348
  123.9 4.6 %shard_map.106 = (f32[2,9,5184]{2,1,0:T(8,128)S(1)}, f32[32,56,128]{2,1,0:T(8,128)}) custom-call(f32[8,384,128]{2,1,0:T(8,128)S(1)} %all_to_all.27.pot_ref, f32[2,384,128]{2,1,0:T(8,128)} %shard_map.104.orb_ref, f32[4,384,128]{2,1,0:T(8,128)S(1)} %bitcast.5), custom_call_target="tpu_custom_call" | custom-call | tf_op jit(solution)/shard_map/pallas_call | solution.py:302
  128.4 7.1 %all-to-all-start.4 = ((f32[32,56,128]{2,1,0:T(8,128)}), f32[32,56,128]{2,1,0:T(8,128)S(1)}, u32[]{:S(2)}, u32[]{:S(2)}) async-start(f32[32,56,128]{2,1,0:T(8,128)} %get-tuple-element.5), calls=%async_computation.4 | async-start | bytes 1835008 | tf_op jit(solution)/shard_map/all_to_all | solution.py:350
  135.5 0.9 copy.16
  136.4 23.6 %all-to-all-done.4.part_ref = f32[32,56,128]{2,1,0:T(8,128)S(1)} async-done(((f32[32,56,128]{2,1,0:T(8,128)}), f32[32,56,128]{2,1,0:T(8,128)S(1)}, u32[]{:S(2)}, u32[]{:S(2)}) %all-to-all-start.4) | async-done | bytes 917536 | tf_op jit(solution)/shard_map/all_to_all | solution.py:350
  160.0 0.1 shard_map.107
  160.1 0.6 copy.17
  (3 shorter events, 0.0 us)
Async XLA Ops:
  0.6 13.5 %copy-start.7 = (s32[2]{0:T(128)S(1)}, s32[2]{0:T(128)}, u32[]{:S(2)}) copy-start(s32[2]{0:T(128)} %param.10) | copy-start | bytes 28
  2.5 25.8 %all-to-all-start = ((f32[32,24,128]{2,1,0:T(8,128)}), f32[32,24,128]{2,1,0:T(8,128)S(1)}, u32[]{:S(2)}, u32[]{:S(2)}) async-start(f32[32,24,128]{2,1,0:T(8,128)} %bitcast), calls=%async_computation | async-start | bytes 786432 | tf_op jit(solution)/shard_map/all_to_all | solution.py:340
  57.4 26.5 %copy-start = (bf16[144,432]{1,0:T(8,128)(2,1)S(1)}, bf16[144,432]{1,0:T(8,128)(2,1)}, u32[]{:S(2)}) copy-start(bf16[144,432]{1,0:T(8,128)(2,1)} %constant.19.clone.refs_6_) | copy-start | bytes 373252
  57.4 26.5 %copy-start.1 = (bf16[144,432]{1,0:T(8,128)(2,1)S(1)}, bf16[144,432]{1,0:T(8,128)(2,1)}, u32[]{:S(2)}) copy-start(bf16[144,432]{1,0:T(8,128)(2,1)} %constant.18.clone.refs_5_) | copy-start | bytes 373252
  57.4 26.5 %copy-start.2 = (bf16[256,256]{1,0:T(8,128)(2,1)S(1)}, bf16[256,256]{1,0:T(8,128)(2,1)}, u32[]{:S(2)}) copy-start(bf16[256,256]{1,0:T(8,128)(2,1)} %constant.16.clone.refs_3_) | copy-start | bytes 393220
  57.4 26.5 %copy-start.3 = (bf16[128,256]{1,0:T(8,128)(2,1)S(1)}, bf16[128,256]{1,0:T(8,128)(2,1)}, u32[]{:S(2)}) copy-start(bf16[128,256]{1,0:T(8,128)(2,1)} %constant.17.clone.refs_4_) | copy-start | bytes 196612
  57.4 26.5 %copy-start.4 = (bf16[80,240]{1,0:T(8,128)(2,1)S(1)}, bf16[80,240]{1,0:T(8,128)(2,1)}, u32[]{:S(2)}) copy-start(bf16[80,240]{1,0:T(8,128)(2,1)} %constant.15.clone.refs_2_) | copy-start | bytes 115204
  57.5 26.5 %copy-start.5 = (bf16[80,240]{1,0:T(8,128)(2,1)S(1)}, bf16[80,240]{1,0:T(8,128)(2,1)}, u32[]{:S(2)}) copy-start(bf16[80,240]{1,0:T(8,128)(2,1)} %constant.14.clone.refs_1_) | copy-start | bytes 115204
  57.5 26.5 %copy-start.6 = (f32[72,128]{1,0:T(8,128)S(1)}, f32[72,128]{1,0:T(8,128)}, u32[]{:S(2)}) copy-start(f32[72,128]{1,0:T(8,128)} %constant.20.clone.refs_7_) | copy-start | bytes 110596
  128.4 31.6 %all-to-all-start.4 = ((f32[32,56,128]{2,1,0:T(8,128)}), f32[32,56,128]{2,1,0:T(8,128)S(1)}, u32[]{:S(2)}, u32[]{:S(2)}) async-start(f32[32,56,128]{2,1,0:T(8,128)} %get-tuple-element.5), calls=%async_computation.4 | async-start | bytes 1835008 | tf_op jit(solution)/shard_map/all_to_all | solution.py:350

commit v2 on v1

--- a/solution.py
+++ b/solution.py
@@ -19,9 +19,12 @@
 ROWS = 384
 XR = 80
 BAND = 32
-CHUNK = 2 * ROWS // BAND
+QUARTER = ROWS // 4
+PIECE = ROWS // 8
 SHARE = PLANE // BAND
-PACK = 56
+REST = SHARE - LANES
+PACK = 96
+PART = 24
 F32 = jnp.float32
 BF16 = jnp.bfloat16
 PARAMS = pltpu.CompilerParams(vmem_limit_bytes=48 * 1024 * 1024)
@@ -91,7 +94,35 @@
     )
 
 
-def pack_kernel(orb_ref, out_ref):
+def pick(index, choices):
+    value = choices[0]
+    for d in range(1, len(choices)):
+        value = jnp.where(index == d, choices[d], value)
+    return value
+
+
+def shape(*dims):
+    return jax.ShapeDtypeStruct(dims, F32)
+
+
+def call(kernel, out_shape, info, *arrays, scratch=(), flops=0):
+    specs = [pl.BlockSpec(memory_space=pltpu.SMEM)]
+    specs += [pl.BlockSpec(memory_space=pltpu.VMEM) for _ in arrays]
+    size = sum(a.size for a in arrays) * 4
+    return pl.pallas_call(
+        kernel,
+        in_specs=specs,
+        out_shape=out_shape,
+        scratch_shapes=list(scratch),
+        compiler_params=PARAMS,
+        cost_estimate=pl.CostEstimate(flops=flops, bytes_accessed=2 * size, transcendentals=0),
+    )(info, *arrays)
+
+
+MY_X, MY_C, MY_Z, X_STEP, C_OWN, Z_STEP = 0, 1, 2, 3, 5, 7
+
+
+def pack_kernel(info, orb_ref, out_ref, *quarters):
     for o in range(2):
         out_ref[o, TAIL:ROWS, :] = jnp.zeros((ROWS - TAIL, LANES), F32)
         for t in range(TILES):
@@ -101,19 +132,45 @@
             cols = slice(t * LANES, t * LANES + wide)
             out_ref[o, 8 * t : 8 * t + 8, :wide] = orb_ref[o, 0:8, cols]
             out_ref[o, TAIL + t : TAIL + t + 1, :wide] = orb_ref[o, 8:9, cols]
-
-
-def pack(orbitals):
-    return pl.pallas_call(
-        pack_kernel,
-        out_shape=jax.ShapeDtypeStruct((2, ROWS, LANES), F32),
-        compiler_params=PARAMS,
-    )(orbitals)
+    for d in range(4):
+        first = pl.multiple_of(QUARTER * lax.rem(info[MY_X] + d, 4), QUARTER)
+        for o in range(2):
+            quarters[d][o] = out_ref[o, pl.ds(first, QUARTER), :]
+
+
+def pick_x_kernel(info, q0, q1, q2, q3, keep_ref, give_ref):
+    for ref, half in ((keep_ref, info[MY_C]), (give_ref, 1 - info[MY_C])):
+        rows = pl.ds(pl.multiple_of(half * PIECE, PIECE), PIECE)
+        for step in range(2):
+            for m in range(2):
+                choices = [q[m, rows, :] for q in (q0, q1, q2, q3)]
+                ref[2 * step + m] = pick(info[X_STEP + step], choices)
+
+
+def pick_core_kernel(info, keep_ref, got_ref, out_ref):
+    for b in range(4):
+        out_ref[b] = jnp.where(info[C_OWN + b // 2] == 1, keep_ref[b], got_ref[b])
+
+
+def pick_z_kernel(info, z0, z1, z2, z3, out_ref):
+    for b in range(4):
+        value = pick(info[Z_STEP + b // 2], [z[b] for z in (z0, z1, z2, z3)])
+        out_ref[b] = value
+        out_ref[4 + b] = value
 
 
 def field_kernel(
     scale,
-    den_ref,
+    info,
+    orb_ref,
+    p0,
+    p1,
+    p2,
+    p3,
+    c0,
+    c1,
+    c2,
+    c3,
     fx_ref,
     ix_ref,
     ztwo_ref,
@@ -121,20 +178,41 @@
     fy_ref,
     iy_ref,
     sq_ref,
-    out_ref,
+    own_ref,
+    k0,
+    k1,
+    k2,
+    k3,
+    g0,
+    g1,
+    g2,
+    g3,
+    blk_ref,
     wide_ref,
+    orb_tail,
+    blk_tail,
     col_ref,
     re_ref,
     im_ref,
 ):
     lane = lax.broadcasted_iota(jnp.int32, (XR, LANES), 1)
 
-    wide_ref[GRID:XR, :] = jnp.zeros((XR - GRID, TILES * LANES), F32)
+    for d, (mine, other) in enumerate(((p0, c0), (p1, c1), (p2, c2), (p3, c3))):
+        quarter = QUARTER * lax.rem(info[MY_X] + 4 - d, 4)
+        for ref, half in ((mine, info[MY_C]), (other, 1 - info[MY_C])):
+            rows = pl.ds(pl.multiple_of(quarter + PIECE * half, PIECE), PIECE)
+            for s in range(8):
+                blk_ref[s, rows, :] = ref[s]
+
+    wide_ref[GRID:XR, :] = jnp.zeros((XR - GRID, (TILES + 2) * LANES), F32)
     for t in range(TILES):
         cols = slice(t * LANES, (t + 1) * LANES)
+        rows = slice(8 * t, 8 * t + 8)
         for s in range(8):
-            wide_ref[8 * s : 8 * s + 8, cols] = den_ref[s, 8 * t : 8 * t + 8, :]
-            wide_ref[64 + s : 65 + s, cols] = den_ref[s, TAIL + t : TAIL + t + 1, :]
+            wide_ref[8 * s : 8 * s + 8, cols] = orb_ref[s, rows, :] * blk_ref[s, rows, :]
+            orb_tail[s : s + 1, cols] = orb_ref[s, TAIL + t : TAIL + t + 1, :]
+            blk_tail[s : s + 1, cols] = blk_ref[s, TAIL + t : TAIL + t + 1, :]
+        wide_ref[64:72, cols] = orb_tail[:, cols] * blk_tail[:, cols]
     for t in range(0, TILES, 4):
         cols = slice(t * LANES, min(t + 4, TILES) * LANES)
         wide_ref[:, cols] = left_dot(fx_ref[...], wide_ref[:, cols])
@@ -213,141 +291,196 @@
             keep = (lane >= at) & (lane < at + GRID)
             value = jnp.where(keep, piece, value)
         wide_ref[:, t * LANES : (t + 1) * LANES] = value
+
+    for s in range(8):
+        own_ref[s, TAIL + TILES : ROWS, :] = jnp.zeros((ROWS - TAIL - TILES, LANES), F32)
     for t in range(0, TILES, 4):
         last = min(t + 4, TILES)
         cols = slice(t * LANES, last * LANES)
-        pot = left_dot(ix_ref[...], wide_ref[:, cols])
+        pot = -left_dot(ix_ref[...], wide_ref[:, cols])
         for u in range(t, last):
             part = pot[:, (u - t) * LANES : (u - t + 1) * LANES]
+            rows = slice(8 * u, 8 * u + 8)
+            one = slice(u * LANES, (u + 1) * LANES)
+            tail = part[64:72] * blk_tail[:, one]
             for s in range(8):
-                out_ref[s, 8 * u : 8 * u + 8, :] = part[8 * s : 8 * s + 8]
-                out_ref[s, TAIL + u : TAIL + u + 1, :] = part[64 + s : 65 + s]
-    for s in range(8):
-        out_ref[s, TAIL + TILES : ROWS, :] = jnp.zeros((ROWS - TAIL - TILES, LANES), F32)
-
-
-def potentials(densities, scale):
+                piece = part[8 * s : 8 * s + 8]
+                own_ref[s, rows, :] = piece * blk_ref[s, rows, :]
+                own_ref[s, TAIL + u : TAIL + u + 1, :] = tail[s : s + 1]
+                wide_ref[8 * s : 8 * s + 8, one] = piece * orb_ref[s, rows, :]
+            wide_ref[64:72, one] = part[64:72] * orb_tail[:, one]
+    wide_ref[:, TILES * LANES :] = jnp.zeros((XR, 2 * LANES), F32)
+
+    def cut(start):
+        t = start // LANES
+        off = start - t * LANES
+        turn = lax.rem(LANES - off, LANES)
+        cols = [pl.ds(pl.multiple_of((t + k) * LANES, LANES), LANES) for k in range(3)]
+        rolled = [pltpu.roll(wide_ref[:GRID, c], turn, 1) for c in cols]
+        keep = lane[:GRID] < LANES - off
+        return jnp.where(keep, rolled[0], rolled[1]), jnp.where(keep, rolled[1], rolled[2])
+
+    third = lane[:8]
+    for x in range(4):
+        for core, ref in ((0, (k0, k1, k2, k3)[x]), (1, (g0, g1, g2, g3)[x])):
+
+            def share_out(z, carry, x=x, core=core, ref=ref):
+                band = 8 * lax.rem(info[MY_Z] + z, 4) + 2 * lax.rem(info[MY_X] + x, 4)
+                band = band + lax.rem(info[MY_C] + core, 2)
+                head, rest = cut(band * SHARE)
+                ref[z, :GRID, :] = head
+                for j in range(3):
+                    a, b, c = (rest[8 * (3 * j + k) : 8 * (3 * j + k) + 8] for k in range(3))
+                    b, c = pltpu.roll(b, REST, 1), pltpu.roll(c, 2 * REST, 1)
+                    packed = jnp.where(third < REST, a, jnp.where(third < 2 * REST, b, c))
+                    ref[z, GRID + 8 * j : GRID + 8 * j + 8, :] = packed
+                return carry
+
+            lax.fori_loop(0, 4, share_out, 0)
+
+
+def fields(info, orbital, pieces, scale):
     def body(*refs):
         field_kernel(scale, *refs)
 
-    return pl.pallas_call(
+    return call(
         body,
-        out_shape=jax.ShapeDtypeStruct((8, ROWS, LANES), F32),
-        scratch_shapes=[
-            pltpu.VMEM((XR, TILES * LANES), F32),
+        [shape(8, ROWS, LANES)] + [shape(4, PACK, LANES)] * 8,
+        info,
+        orbital,
+        *pieces,
+        *[jnp.asarray(t) for t in tables()],
+        scratch=[
+            pltpu.VMEM((8, ROWS, LANES), F32),
+            pltpu.VMEM((XR, (TILES + 2) * LANES), F32),
+            pltpu.VMEM((8, TILES * LANES), F32),
+            pltpu.VMEM((8, TILES * LANES), F32),
             pltpu.VMEM((GRID * XR, LANES), F32),
             pltpu.VMEM((GRID * KX, LANES), F32),
             pltpu.VMEM((GRID * KX, LANES), F32),
         ],
-        compiler_params=PARAMS,
-    )(densities, *[jnp.asarray(t) for t in tables()])
-
-
-def sums_kernel(pot_ref, orb_ref, blk_ref, field_ref, share_ref, wide_ref):
-    wide_ref[32:40, :] = jnp.zeros((8, TILES * LANES), F32)
+        flops=10**10,
+    )
+
+
+def add_kernel(info, a_ref, b_ref, out_ref):
+    out_ref[...] = a_ref[...] + b_ref[...]
+
+
+def add_x_kernel(info, k_ref, g_ref, r1, r2, r3, *outs):
+    for z in range(4):
+        outs[z][...] = k_ref[z] + g_ref[z] + r1[z] + r2[z] + r3[z]
+
+
+def add_z_kernel(info, s_ref, r1, r2, r3, out_ref, sum_ref):
+    sum_ref[...] = s_ref[...] + r1[...] + r2[...] + r3[...]
+    out_ref[...] = jnp.zeros((8, PART, LANES), F32)
+
+    def rest(tile):
+        value = sum_ref[GRID + 8 * (tile // 3) : GRID + 8 * (tile // 3) + 8, :]
+        turn = tile % 3 * REST
+        return pltpu.roll(value, LANES - turn, 1) if turn else value
+
+    last = rest(8)
+    for s in range(8):
+        out_ref[s, 0:8, :] = sum_ref[8 * s : 8 * s + 8, :]
+        out_ref[s, 8:16, :] = rest(s)
+        out_ref[s, 16:17, :] = sum_ref[64 + s : 65 + s, :]
+        out_ref[s, 17:18, :] = last[s : s + 1]
+
+
+def share_kernel(info, part_ref, out_ref):
+    for b in range(4):
+        total = part_ref[b] + part_ref[4 + b]
+        at = (b // 2, b % 2)
+        out_ref[at[0], at[1], 0:8, :LANES] = total[0:8]
+        out_ref[at[0], at[1], 0:8, LANES:SHARE] = total[8:16, :REST]
+        out_ref[at[0], at[1], 8:9, :LANES] = total[16:17]
+        out_ref[at[0], at[1], 8:9, LANES:SHARE] = total[17:18, :REST]
+
+
+def own_kernel(info, part_ref, out_ref):
     for i in range(2):
         for t in range(TILES + 1):
-            tail = t == TILES
-            rows = slice(TAIL, ROWS) if tail else slice(8 * t, 8 * t + 8)
-            total = blk_ref[0, rows, :] * pot_ref[4 * i, rows, :]
+            rows = slice(TAIL, ROWS) if t == TILES else slice(8 * t, 8 * t + 8)
+            total = part_ref[4 * i, rows, :]
             for b in range(1, 4):
-                total = total + blk_ref[b, rows, :] * pot_ref[4 * i + b, rows, :]
-            total = -total
-            if tail:
+                total = total + part_ref[4 * i + b, rows, :]
+            if t == TILES:
                 for u in range(TILES):
                     wide = min(LANES, PLANE - u * LANES)
-                    field_ref[i, 8:9, u * LANES : u * LANES + wide] = total[u : u + 1, :wide]
+                    out_ref[i, 8:9, u * LANES : u * LANES + wide] = total[u : u + 1, :wide]
             else:
                 wide = min(LANES, PLANE - t * LANES)
-                field_ref[i, 0:8, t * LANES : t * LANES + wide] = total[:, :wide]
-    for b in range(4):
-        for t in range(TILES + 1):
-            tail = t == TILES
-            rows = slice(TAIL, ROWS) if tail else slice(8 * t, 8 * t + 8)
-            total = -(
-                orb_ref[0, rows, :] * pot_ref[b, rows, :]
-                + orb_ref[1, rows, :] * pot_ref[4 + b, rows, :]
-            )
-            if tail:
-                for u in range(TILES):
-                    wide_ref[32 + b : 33 + b, u * LANES : (u + 1) * LANES] = total[u : u + 1]
-            else:
-                wide_ref[8 * b : 8 * b + 8, t * LANES : (t + 1) * LANES] = total
-    lane = lax.broadcasted_iota(jnp.int32, (40, LANES), 1)
-    rest = SHARE - LANES
-
-    def cut(start):
-        t, off = divmod(start, LANES)
-        value = wide_ref[:, t * LANES : (t + 1) * LANES]
-        if off:
-            value = pltpu.roll(value, LANES - off, 1)
-            if t + 1 < TILES:
-                after = pltpu.roll(wide_ref[:, (t + 1) * LANES : (t + 2) * LANES], LANES - off, 1)
-                value = jnp.where(lane < LANES - off, value, after)
-        return value
-
-    for r in range(BAND):
-        share_ref[r, 0:40, :] = cut(r * SHARE)
-        more = cut(r * SHARE + LANES)
-        low, mid, top = more[0:16], more[16:32], more[32:40]
-        mid = pltpu.roll(mid, rest, 1)
-        top = jnp.concatenate([pltpu.roll(top, 2 * rest, 1), jnp.zeros((8, LANES), F32)], axis=0)
-        where = lane[:16]
-        share_ref[r, 40:56, :] = jnp.where(
-            where < rest, low, jnp.where(where < 2 * rest, mid, top)
-        )
-
-
-def sums(pot, packed, blocks):
-    return pl.pallas_call(
-        sums_kernel,
-        out_shape=(
-            jax.ShapeDtypeStruct((2, SLAB, PLANE), F32),
-            jax.ShapeDtypeStruct((BAND, PACK, LANES), F32),
-        ),
-        scratch_shapes=[pltpu.VMEM((40, TILES * LANES), F32)],
-        compiler_params=PARAMS,
-    )(pot, packed, blocks)
-
-
-def share_kernel(part_ref, out_ref):
-    total = part_ref[0]
-    for r in range(1, BAND):
-        total = total + part_ref[r]
-    rest = SHARE - LANES
-    tail = total[40:56]
-    tails = [tail, pltpu.roll(tail, LANES - rest, 1), pltpu.roll(tail, LANES - 2 * rest, 1)]
-    for b in range(4):
-        at = (b // 2, b % 2)
-        out_ref[at[0], at[1], 0:8, :LANES] = total[8 * b : 8 * b + 8]
-        more = tails[b // 2][8 * (b % 2) : 8 * (b % 2) + 8]
-        out_ref[at[0], at[1], 0:8, LANES:SHARE] = more[:, :rest]
-        out_ref[at[0], at[1], 8:9, :LANES] = total[32 + b : 33 + b]
-        out_ref[at[0], at[1], 8:9, LANES:SHARE] = tails[2][b : b + 1, :rest]
-
-
-def share(parts):
-    return pl.pallas_call(
-        share_kernel,
-        out_shape=jax.ShapeDtypeStruct((2, 2, SLAB, SHARE), F32),
-        compiler_params=PARAMS,
-    )(parts)
+                out_ref[i, 0:8, t * LANES : t * LANES + wide] = total[:, :wide]
+
+
+def shift_x(d):
+    return [(i, i // 8 * 8 + (i // 2 + d) % 4 * 2 + i % 2) for i in range(BAND)]
+
+
+def shift_z(d):
+    return [(i, (i + 8 * d) % BAND) for i in range(BAND)]
+
+
+def other_core(x):
+    return lax.ppermute(x, "band", [(i, i ^ 1) for i in range(BAND)])
+
+
+def scalars(block_owner):
+    me = lax.axis_index("band")
+    owner = jnp.clip(block_owner, 0, BAND - 1)
+    x, c, z = me // 2 % 4, me % 2, me // 8
+    parts = [
+        jnp.stack([x, c, z]),
+        (x - owner // 2 % 4) % 4,
+        (c == owner % 2).astype(jnp.int32),
+        (z - owner // 8) % 4,
+    ]
+    return jnp.concatenate([p.astype(jnp.int32) for p in parts])
 
 
 def on_device(orbitals, block_owner):
     scale = math.sqrt(GRID**3 / (2 * BAND))
-    packed = pack(orbitals)
-    pieces = lax.all_to_all(packed.reshape(BAND, CHUNK, LANES), "band", 0, 0)
-    mine = jnp.take(pieces, block_owner, axis=0, mode="clip")
-    spread = jnp.broadcast_to(mine[None], (BAND, 2, CHUNK, LANES))
-    gathered = lax.all_to_all(spread, "band", 0, 0)
-    blocks = gathered.transpose(1, 0, 2, 3).reshape(4, ROWS, LANES)
-    densities = (packed[:, None] * blocks[None]).reshape(8, ROWS, LANES)
-    whole = lax.all_to_all(densities, "grid", 0, 0)
-    pot = potentials(whole, scale)
-    pot = lax.all_to_all(pot, "grid", 0, 0)
-    field, shares = sums(pot, packed, blocks)
-    block_field = share(lax.all_to_all(shares, "band", 0, 0))
+    info = scalars(block_owner)
+    packed, *quarters = call(
+        pack_kernel, [shape(2, ROWS, LANES)] + [shape(2, QUARTER, LANES)] * 4, info, orbitals
+    )
+    spread = jnp.broadcast_to(packed[:, None], (2, 4, ROWS, LANES)).reshape(8, ROWS, LANES)
+    orbital = lax.all_to_all(spread, "grid", 0, 0)
+
+    quarters = quarters[:1] + [lax.ppermute(quarters[d], "band", shift_x(d)) for d in (1, 2, 3)]
+    half = shape(4, PIECE, LANES)
+    keep, give = call(pick_x_kernel, [half, half], info, *quarters)
+    mine = call(pick_core_kernel, half, info, keep, other_core(give))
+    along = [mine] + [lax.ppermute(mine, "band", shift_z(d)) for d in (1, 2, 3)]
+    mine = call(pick_z_kernel, shape(8, PIECE, LANES), info, *along)
+    piece = lax.all_to_all(mine, "grid", 0, 0)
+    pieces = [piece] + [lax.ppermute(piece, "band", shift_x(d)) for d in (1, 2, 3)]
+    pieces = pieces + [other_core(p) for p in pieces]
+
+    own, *shares = fields(info, orbital, pieces, scale)
+    field = call(
+        own_kernel, shape(2, SLAB, PLANE), info, lax.all_to_all(own, "grid", 0, 0)
+    )
+    kept, got = shares[:4], [other_core(g) for g in shares[4:]]
+    part = shape(4, PACK, LANES)
+    moved = []
+    for d in (1, 2, 3):
+        moved.append(lax.ppermute(call(add_kernel, part, info, kept[d], got[d]), "band", shift_x(d)))
+    sums = call(add_x_kernel, [shape(PACK, LANES)] * 4, info, kept[0], got[0], *moved)
+    moved = [lax.ppermute(sums[d], "band", shift_z(d)) for d in (1, 2, 3)]
+    slabs = call(
+        add_z_kernel,
+        shape(8, PART, LANES),
+        info,
+        sums[0],
+        *moved,
+        scratch=[pltpu.VMEM((PACK, LANES), F32)],
+    )
+    block_field = call(
+        share_kernel, shape(2, 2, SLAB, SHARE), info, lax.all_to_all(slabs, "grid", 0, 0)
+    )
     return field, block_field
 
 

time: 164 us -> 160 us (0.976); the launches traced: 161 us -> 160 us
  blocking collectives: 76.5 us -> 20.1 us
  starting transfers between devices: 18.7 us -> 43.2 us
  waiting for transfers between devices: 37.7 us -> 59.3 us
  Pallas kernels: 22.6 us -> 31 us
    all_to_all x3 -> x2, blocking collectives: 76.5 us -> 20.1 us  [the longest x1 11.2 us: on_device(): piece = lax.all_to_all(mine, 'grid', 0, 0)]
    ppermute x0 -> x24, starting transfers between devices: none -> 35.2 us  [the longest x3 9.78 us: on_device(): moved = [lax.ppermute(sums[d], 'band', shift_z(d)) for d in (1, 2, 3)]]
    ppermute x0 -> x24, waiting for transfers between devices: none -> 32.6 us  [the longest x3 8.39 us: on_device(): along = [mine] + [lax.ppermute(mine, 'band', shift_z(d)) for d in (1, 2, 3)]]
    all_to_all x2, waiting for transfers between devices: 37.7 us -> 26.6 us  [the longest x1 19.2 us: on_device(): lax.all_to_all(own, 'grid', 0, 0)]
    all_to_all x2, starting transfers between devices: 18.7 us -> 8.01 us  [the longest x1 4.43 us: on_device(): orbital = lax.all_to_all(spread, 'grid', 0, 0)]
    pallas_call x4 -> x12, Pallas kernels: 22.6 us -> 31 us  [call(): pl.pallas_call(kernel, in_specs=specs, out_shape=out_shape, scratch_shape...]
  transfers between devices with their start and end apart: 2 -> 26, of which waited for: 2 -> 19; matrix products, arithmetic and copies ran while one was open for 1% -> 0% of each run, Pallas kernels for 0% -> 1%
where the time goes in v2:
time: 160 us
  waiting for transfers between devices  59.3 us (37%)
  starting transfers between devices  43.2 us (27%)
  Pallas kernels  31 us (19%)
  blocking collectives  20.1 us (13%)
  local copies, waits for them, and re-layouts  3.99 us (2%)
    pallas_call x12, Pallas kernels, call(): pl.pallas_call(kernel, in_specs=specs, out_shape=out_shape, scratch_shape...  31 us
    all_to_all x1, waiting for transfers between devices, on_device(): lax.all_to_all(own, 'grid', 0, 0)  19.2 us
    all_to_all x1, blocking collectives, on_device(): piece = lax.all_to_all(mine, 'grid', 0, 0)  11.2 us
    ppermute x3, starting transfers between devices, on_device(): moved = [lax.ppermute(sums[d], 'band', shift_z(d)) for d in (1, 2, 3)]  9.78 us
    ppermute x3, starting transfers between devices, on_device(): along = [mine] + [lax.ppermute(mine, 'band', shift_z(d)) for d in (1, 2, 3)]  9.51 us
    all_to_all x1, blocking collectives, on_device(): lax.all_to_all(slabs, 'grid', 0, 0)  8.91 us
    ppermute x3, waiting for transfers between devices, on_device(): along = [mine] + [lax.ppermute(mine, 'band', shift_z(d)) for d in (1, 2, 3)]  8.39 us
    ppermute x3, waiting for transfers between devices, on_device(): lax.ppermute(call(add_kernel, part, info, kept[d], got[d]), 'band', shift...  8.21 us
  transfers between devices with their start and end apart: 26, of which 19 were waited for; matrix products, arithmetic and copies ran while one was open for 0% of the time, Pallas kernels for 1%

profile of v2, /device:TPU:2, one launch (start us, length us, event | category | flops | bytes accessed | tf_op | source)
XLA Modules:
  0.0 159.8 jit_solution(11449195730915442536)
XLA Ops:
  3.8 1.6 collective-permute-start
  5.4 2.8 %collective-permute-start.1 = (f32[2,96,128]{2,1,0:T(8,128)S(1)}, f32[2,96,128]{2,1,0:T(8,128)S(1)}, u32[]{:S(2)}, u32[]{:S(2)}) collective-permute-start(f32[2,96,128]{2,1,0:T(8,128)S(1)} %get-tuple-element.25), channel_id=1, source_target_pairs={{0,32},{8,40},{16,48},{24,56},{32,0},{40,8},{48,16},{56,24},{64,96... | collective-permute-start | bytes 294920 | tf_op jit(solution)/shard_map/ppermute | solution.py:452
  8.7 3.5 %collective-permute-done.1.q2 = f32[2,96,128]{2,1,0:T(8,128)S(1)} collective-permute-done((f32[2,96,128]{2,1,0:T(8,128)S(1)}, f32[2,96,128]{2,1,0:T(8,128)S(1)}, u32[]{:S(2)}, u32[]{:S(2)}) %collective-permute-start.1) | collective-permute-done | bytes 98336 | tf_op jit(solution)/shard_map/ppermute | solution.py:452
  13.9 1.3 collective-permute-done.3.got_ref
  15.8 5.7 %collective-permute-start.6 = (f32[4,48,128]{2,1,0:T(8,128)S(1)}, f32[4,48,128]{2,1,0:T(8,128)S(1)}, u32[]{:S(2)}, u32[]{:S(2)}) collective-permute-start(f32[4,48,128]{2,1,0:T(8,128)S(1)} %shard_map.106.z0), channel_id=1, source_target_pairs={{0,192},{8,200},{16,208},{24,216},{32,224},{40,232},{48,240},{56,2... | collective-permute-start | bytes 294920 | tf_op jit(solution)/shard_map/ppermute | solution.py:456
  22.5 2.8 %collective-permute-start.4 = (f32[4,48,128]{2,1,0:T(8,128)S(1)}, f32[4,48,128]{2,1,0:T(8,128)S(1)}, u32[]{:S(2)}, u32[]{:S(2)}) collective-permute-start(f32[4,48,128]{2,1,0:T(8,128)S(1)} %shard_map.106.z0), channel_id=1, source_target_pairs={{0,64},{8,72},{16,80},{24,88},{32,96},{40,104},{48,112},{56,120},{... | collective-permute-start | bytes 294920 | tf_op jit(solution)/shard_map/ppermute | solution.py:456
  25.3 4.9 %collective-permute-done.6.z3 = f32[4,48,128]{2,1,0:T(8,128)S(1)} collective-permute-done((f32[4,48,128]{2,1,0:T(8,128)S(1)}, f32[4,48,128]{2,1,0:T(8,128)S(1)}, u32[]{:S(2)}, u32[]{:S(2)}) %collective-permute-start.6) | collective-permute-done | bytes 98336 | tf_op jit(solution)/shard_map/ppermute | solution.py:456
  30.2 3.5 %collective-permute-done.5.z2 = f32[4,48,128]{2,1,0:T(8,128)S(1)} collective-permute-done((f32[4,48,128]{2,1,0:T(8,128)S(1)}, f32[4,48,128]{2,1,0:T(8,128)S(1)}, u32[]{:S(2)}, u32[]{:S(2)}) %collective-permute-start.5) | collective-permute-done | bytes 98336 | tf_op jit(solution)/shard_map/ppermute | solution.py:456
  34.3 11.2 %all_to_all.20.refs_2_ = f32[8,48,128]{2,1,0:T(8,128)S(1)} all-to-all(f32[8,48,128]{2,1,0:T(8,128)S(1)} %shard_map.107), channel_id=1, replica_groups=mesh['band'=32,'grid'=8] {'grid'}, dimensions={0} | all-to-all | bytes 393216 | tf_op jit(solution)/shard_map/all_to_all | solution.py:458
  45.5 1.2 broadcast_in_dim.2
  46.8 4.4 %all-to-all-start = ((f32[8,384,128]{2,1,0:T(8,128)}), f32[8,384,128]{2,1,0:T(8,128)}, u32[]{:S(2)}, u32[]{:S(2)}) async-start(f32[8,384,128]{2,1,0:T(8,128)} %bitcast.3), calls=%async_computation | async-start | bytes 3145728 | tf_op jit(solution)/shard_map/all_to_all | solution.py:450
  52.0 2.1 %collective-permute-start.8 = (f32[8,48,128]{2,1,0:T(8,128)S(1)}, f32[8,48,128]{2,1,0:T(8,128)S(1)}, u32[]{:S(2)}, u32[]{:S(2)}) collective-permute-start(f32[8,48,128]{2,1,0:T(8,128)S(1)} %all_to_all.20.refs_2_), channel_id=1, source_target_pairs={{0,32},{8,40},{16,48},{24,56},{32,0},{40,8},{48,16},{56,24},{64,96... | collective-permute-start | bytes 589832 | tf_op jit(solution)/shard_map/ppermute | solution.py:459
  54.0 2.1 %collective-permute-start.7 = (f32[8,48,128]{2,1,0:T(8,128)S(1)}, f32[8,48,128]{2,1,0:T(8,128)S(1)}, u32[]{:S(2)}, u32[]{:S(2)}) collective-permute-start(f32[8,48,128]{2,1,0:T(8,128)S(1)} %all_to_all.20.refs_2_), channel_id=1, source_target_pairs={{0,16},{8,24},{16,32},{24,40},{32,48},{40,56},{48,0},{56,8},{64,80... | collective-permute-start | bytes 589832 | tf_op jit(solution)/shard_map/ppermute | solution.py:459
  56.1 2.6 %collective-permute-done.9.refs_5_ = f32[8,48,128]{2,1,0:T(8,128)S(1)} collective-permute-done((f32[8,48,128]{2,1,0:T(8,128)S(1)}, f32[8,48,128]{2,1,0:T(8,128)S(1)}, u32[]{:S(2)}, u32[]{:S(2)}) %collective-permute-start.9) | collective-permute-done | bytes 196640 | tf_op jit(solution)/shard_map/ppermute | solution.py:459
  58.7 2.1 %collective-permute-done.8.refs_4_ = f32[8,48,128]{2,1,0:T(8,128)S(1)} collective-permute-done((f32[8,48,128]{2,1,0:T(8,128)S(1)}, f32[8,48,128]{2,1,0:T(8,128)S(1)}, u32[]{:S(2)}, u32[]{:S(2)}) %collective-permute-start.8) | collective-permute-done | bytes 196640 | tf_op jit(solution)/shard_map/ppermute | solution.py:459
  60.8 1.1 collective-permute-done.7.refs_3_
  62.2 1.1 collective-permute-done.11.refs_7_
  63.3 7.5 %all-to-all-done.refs_1_ = f32[8,384,128]{2,1,0:T(8,128)} async-done(((f32[8,384,128]{2,1,0:T(8,128)}), f32[8,384,128]{2,1,0:T(8,128)}, u32[]{:S(2)}, u32[]{:S(2)}) %all-to-all-start) | async-done | bytes 1572896 | tf_op jit(solution)/shard_map/all_to_all | solution.py:450
  70.8 24.6 %shard_map.108 = (f32[8,384,128]{2,1,0:T(8,128)}, f32[4,96,128]{2,1,0:T(8,128)S(1)}, f32[4,96,128]{2,1,0:T(8,128)S(1)}, f32[4,96,128]{2,1,0:T(8,128)S(1)}, f32[4...) custom-call(s32[9]{0:T(128)S(1)} %concatenate.3.info.refs_0_, ...), custom_call_target="tpu_custom_call" | custom-call | flops 10000000000 | bytes 8454144 | tf_op jit(solution)/shard_map/pallas_call | solution.py:112
  97.5 1.4 collective-permute-start.16
  99.4 1.6 collective-permute-start.18
  101.5 2.1 %collective-permute-start.20 = (f32[4,96,128]{2,1,0:T(8,128)S(1)}, f32[4,96,128]{2,1,0:T(8,128)S(1)}, u32[]{:S(2)}, u32[]{:S(2)}) collective-permute-start(f32[4,96,128]{2,1,0:T(8,128)S(1)} %shard_map.112), channel_id=1, source_target_pairs={{0,48},{8,56},{16,0},{24,8},{32,16},{40,24},{48,32},{56,40},{64,11... | collective-permute-start | bytes 589832 | tf_op jit(solution)/shard_map/ppermute | solution.py:470
  103.7 1.6 %collective-permute-done.16.r1 = f32[4,96,128]{2,1,0:T(8,128)S(1)} collective-permute-done((f32[4,96,128]{2,1,0:T(8,128)S(1)}, f32[4,96,128]{2,1,0:T(8,128)S(1)}, u32[]{:S(2)}, u32[]{:S(2)}) %collective-permute-start.16) | collective-permute-done | bytes 196640 | tf_op jit(solution)/shard_map/ppermute | solution.py:470
  105.3 3.5 %collective-permute-done.18.r2 = f32[4,96,128]{2,1,0:T(8,128)S(1)} collective-permute-done((f32[4,96,128]{2,1,0:T(8,128)S(1)}, f32[4,96,128]{2,1,0:T(8,128)S(1)}, u32[]{:S(2)}, u32[]{:S(2)}) %collective-permute-start.18) | collective-permute-done | bytes 196640 | tf_op jit(solution)/shard_map/ppermute | solution.py:470
  108.8 3.0 %collective-permute-done.20.r3 = f32[4,96,128]{2,1,0:T(8,128)S(1)} collective-permute-done((f32[4,96,128]{2,1,0:T(8,128)S(1)}, f32[4,96,128]{2,1,0:T(8,128)S(1)}, u32[]{:S(2)}, u32[]{:S(2)}) %collective-permute-start.20) | collective-permute-done | bytes 196640 | tf_op jit(solution)/shard_map/ppermute | solution.py:470
  112.5 2.7 %collective-permute-start.21 = (f32[96,128]{1,0:T(8,128)S(1)}, f32[96,128]{1,0:T(8,128)S(1)}, u32[]{:S(2)}, u32[]{:S(2)}) collective-permute-start(f32[96,128]{1,0:T(8,128)S(1)} %get-tuple-element.39), channel_id=1, source_target_pairs={{0,64},{8,72},{16,80},{24,88},{32,96},{40,104},{48,112},{56,120},{... | collective-permute-start | bytes 147464 | tf_op jit(solution)/shard_map/ppermute | solution.py:472
  115.2 3.8 %collective-permute-start.22 = (f32[96,128]{1,0:T(8,128)S(1)}, f32[96,128]{1,0:T(8,128)S(1)}, u32[]{:S(2)}, u32[]{:S(2)}) collective-permute-start(f32[96,128]{1,0:T(8,128)S(1)} %get-tuple-element.40), channel_id=1, source_target_pairs={{0,128},{8,136},{16,144},{24,152},{32,160},{40,168},{48,176},{56,1... | collective-permute-start | bytes 147464 | tf_op jit(solution)/shard_map/ppermute | solution.py:472
  119.0 3.3 %collective-permute-start.23 = (f32[96,128]{1,0:T(8,128)S(1)}, f32[96,128]{1,0:T(8,128)S(1)}, u32[]{:S(2)}, u32[]{:S(2)}) collective-permute-start(f32[96,128]{1,0:T(8,128)S(1)} %get-tuple-element.41), channel_id=1, source_target_pairs={{0,192},{8,200},{16,208},{24,216},{32,224},{40,232},{48,240},{56,2... | collective-permute-start | bytes 147464 | tf_op jit(solution)/shard_map/ppermute | solution.py:472
  122.3 1.6 collective-permute-done.22.r2
  125.4 8.9 %all_to_all.21.part_ref = f32[8,24,128]{2,1,0:T(8,128)S(1)} all-to-all(f32[8,24,128]{2,1,0:T(8,128)S(1)} %shard_map.114), channel_id=1, replica_groups=mesh['band'=32,'grid'=8] {'grid'}, dimensions={0} | all-to-all | bytes 196608 | tf_op jit(solution)/shard_map/all_to_all | solution.py:482
  134.3 3.6 %all-to-all-start.2 = ((f32[8,384,128]{2,1,0:T(8,128)}), f32[8,384,128]{2,1,0:T(8,128)S(1)}, u32[]{:S(2)}, u32[]{:S(2)}) async-start(f32[8,384,128]{2,1,0:T(8,128)} %get-tuple-element.29), calls=%async_computation.2 | async-start | bytes 3145728 | tf_op jit(solution)/shard_map/all_to_all | solution.py:464
  139.1 19.2 %all-to-all-done.2.part_ref = f32[8,384,128]{2,1,0:T(8,128)S(1)} async-done(((f32[8,384,128]{2,1,0:T(8,128)}), f32[8,384,128]{2,1,0:T(8,128)S(1)}, u32[]{:S(2)}, u32[]{:S(2)}) %all-to-all-start.2) | async-done | bytes 1572896 | tf_op jit(solution)/shard_map/all_to_all | solution.py:464
  (55 shorter events, 16.6 us)
Async XLA Ops:
  3.8 4.9 %collective-permute-start = (f32[2,96,128]{2,1,0:T(8,128)S(1)}, f32[2,96,128]{2,1,0:T(8,128)S(1)}, u32[]{:S(2)}, u32[]{:S(2)}) collective-permute-start(f32[2,96,128]{2,1,0:T(8,128)S(1)} %get-tuple-element.24), channel_id=1, source_target_pairs={{0,16},{8,24},{16,32},{24,40},{32,48},{40,56},{48,0},{56,8},{64,80... | collective-permute-start | bytes 294920 | tf_op jit(solution)/shard_map/ppermute | solution.py:452
  5.4 6.9 %collective-permute-start.1 = (f32[2,96,128]{2,1,0:T(8,128)S(1)}, f32[2,96,128]{2,1,0:T(8,128)S(1)}, u32[]{:S(2)}, u32[]{:S(2)}) collective-permute-start(f32[2,96,128]{2,1,0:T(8,128)S(1)} %get-tuple-element.25), channel_id=1, source_target_pairs={{0,32},{8,40},{16,48},{24,56},{32,0},{40,8},{48,16},{56,24},{64,96... | collective-permute-start | bytes 294920 | tf_op jit(solution)/shard_map/ppermute | solution.py:452
  8.2 5.0 %collective-permute-start.2 = (f32[2,96,128]{2,1,0:T(8,128)S(1)}, f32[2,96,128]{2,1,0:T(8,128)S(1)}, u32[]{:S(2)}, u32[]{:S(2)}) collective-permute-start(f32[2,96,128]{2,1,0:T(8,128)S(1)} %get-tuple-element.26), channel_id=1, source_target_pairs={{0,48},{8,56},{16,0},{24,8},{32,16},{40,24},{48,32},{56,40},{64,11... | collective-permute-start | bytes 294920 | tf_op jit(solution)/shard_map/ppermute | solution.py:452
  13.8 1.4 collective-permute-start.3
  15.8 14.4 %collective-permute-start.6 = (f32[4,48,128]{2,1,0:T(8,128)S(1)}, f32[4,48,128]{2,1,0:T(8,128)S(1)}, u32[]{:S(2)}, u32[]{:S(2)}) collective-permute-start(f32[4,48,128]{2,1,0:T(8,128)S(1)} %shard_map.106.z0), channel_id=1, source_target_pairs={{0,192},{8,200},{16,208},{24,216},{32,224},{40,232},{48,240},{56,2... | collective-permute-start | bytes 294920 | tf_op jit(solution)/shard_map/ppermute | solution.py:456
  21.5 12.2 %collective-permute-start.5 = (f32[4,48,128]{2,1,0:T(8,128)S(1)}, f32[4,48,128]{2,1,0:T(8,128)S(1)}, u32[]{:S(2)}, u32[]{:S(2)}) collective-permute-start(f32[4,48,128]{2,1,0:T(8,128)S(1)} %shard_map.106.z0), channel_id=1, source_target_pairs={{0,128},{8,136},{16,144},{24,152},{32,160},{40,168},{48,176},{56,1... | collective-permute-start | bytes 294920 | tf_op jit(solution)/shard_map/ppermute | solution.py:456
  22.5 11.2 %collective-permute-start.4 = (f32[4,48,128]{2,1,0:T(8,128)S(1)}, f32[4,48,128]{2,1,0:T(8,128)S(1)}, u32[]{:S(2)}, u32[]{:S(2)}) collective-permute-start(f32[4,48,128]{2,1,0:T(8,128)S(1)} %shard_map.106.z0), channel_id=1, source_target_pairs={{0,64},{8,72},{16,80},{24,88},{32,96},{40,104},{48,112},{56,120},{... | collective-permute-start | bytes 294920 | tf_op jit(solution)/shard_map/ppermute | solution.py:456
  46.7 24.0 %copy-start.1 = (bf16[144,432]{1,0:T(8,128)(2,1)S(1)}, bf16[144,432]{1,0:T(8,128)(2,1)}, u32[]{:S(2)}) copy-start(bf16[144,432]{1,0:T(8,128)(2,1)} %constant.110.clone.refs_14_) | copy-start | bytes 373252
  46.7 24.0 %copy-start.2 = (bf16[256,256]{1,0:T(8,128)(2,1)S(1)}, bf16[256,256]{1,0:T(8,128)(2,1)}, u32[]{:S(2)}) copy-start(bf16[256,256]{1,0:T(8,128)(2,1)} %constant.108.clone.refs_12_) | copy-start | bytes 393220
  46.7 24.0 %copy-start.3 = (bf16[128,256]{1,0:T(8,128)(2,1)S(1)}, bf16[128,256]{1,0:T(8,128)(2,1)}, u32[]{:S(2)}) copy-start(bf16[128,256]{1,0:T(8,128)(2,1)} %constant.109.clone.refs_13_) | copy-start | bytes 196612
  46.7 24.0 %copy-start.4 = (bf16[80,240]{1,0:T(8,128)(2,1)S(1)}, bf16[80,240]{1,0:T(8,128)(2,1)}, u32[]{:S(2)}) copy-start(bf16[80,240]{1,0:T(8,128)(2,1)} %constant.107.clone.refs_11_) | copy-start | bytes 115204
  46.8 24.0 %copy-start.5 = (bf16[80,240]{1,0:T(8,128)(2,1)S(1)}, bf16[80,240]{1,0:T(8,128)(2,1)}, u32[]{:S(2)}) copy-start(bf16[80,240]{1,0:T(8,128)(2,1)} %constant.106.clone.refs_10_) | copy-start | bytes 115204
  46.8 24.0 %copy-start.6 = (f32[72,128]{1,0:T(8,128)S(1)}, f32[72,128]{1,0:T(8,128)}, u32[]{:S(2)}) copy-start(f32[72,128]{1,0:T(8,128)} %constant.112.clone.refs_16_) | copy-start | bytes 110596
  46.8 24.0 %all-to-all-start = ((f32[8,384,128]{2,1,0:T(8,128)}), f32[8,384,128]{2,1,0:T(8,128)}, u32[]{:S(2)}, u32[]{:S(2)}) async-start(f32[8,384,128]{2,1,0:T(8,128)} %bitcast.3), calls=%async_computation | async-start | bytes 3145728 | tf_op jit(solution)/shard_map/all_to_all | solution.py:450
  51.2 7.4 %collective-permute-start.9 = (f32[8,48,128]{2,1,0:T(8,128)S(1)}, f32[8,48,128]{2,1,0:T(8,128)S(1)}, u32[]{:S(2)}, u32[]{:S(2)}) collective-permute-start(f32[8,48,128]{2,1,0:T(8,128)S(1)} %all_to_all.20.refs_2_), channel_id=1, source_target_pairs={{0,48},{8,56},{16,0},{24,8},{32,16},{40,24},{48,32},{56,40},{64,11... | collective-permute-start | bytes 589832 | tf_op jit(solution)/shard_map/ppermute | solution.py:459
  52.0 8.8 %collective-permute-start.8 = (f32[8,48,128]{2,1,0:T(8,128)S(1)}, f32[8,48,128]{2,1,0:T(8,128)S(1)}, u32[]{:S(2)}, u32[]{:S(2)}) collective-permute-start(f32[8,48,128]{2,1,0:T(8,128)S(1)} %all_to_all.20.refs_2_), channel_id=1, source_target_pairs={{0,32},{8,40},{16,48},{24,56},{32,0},{40,8},{48,16},{56,24},{64,96... | collective-permute-start | bytes 589832 | tf_op jit(solution)/shard_map/ppermute | solution.py:459
  54.0 7.8 %collective-permute-start.7 = (f32[8,48,128]{2,1,0:T(8,128)S(1)}, f32[8,48,128]{2,1,0:T(8,128)S(1)}, u32[]{:S(2)}, u32[]{:S(2)}) collective-permute-start(f32[8,48,128]{2,1,0:T(8,128)S(1)} %all_to_all.20.refs_2_), channel_id=1, source_target_pairs={{0,16},{8,24},{16,32},{24,40},{32,48},{40,56},{48,0},{56,8},{64,80... | collective-permute-start | bytes 589832 | tf_op jit(solution)/shard_map/ppermute | solution.py:459
  56.1 5.7 %collective-permute-start.10 = (f32[8,48,128]{2,1,0:T(8,128)S(1)}, f32[8,48,128]{2,1,0:T(8,128)S(1)}, u32[]{:S(2)}, u32[]{:S(2)}) collective-permute-start(f32[8,48,128]{2,1,0:T(8,128)S(1)} %all_to_all.20.refs_2_), channel_id=1, source_target_pairs={{0,8},{8,0},{16,24},{24,16},{32,40},{40,32},{48,56},{56,48},{64,72... | collective-permute-start | bytes 589832 | tf_op jit(solution)/shard_map/ppermute | solution.py:427
  58.7 3.2 %collective-permute-start.13 = (f32[8,48,128]{2,1,0:T(8,128)S(1)}, f32[8,48,128]{2,1,0:T(8,128)S(1)}, u32[]{:S(2)}, u32[]{:S(2)}) collective-permute-start(f32[8,48,128]{2,1,0:T(8,128)S(1)} %collective-permute-done.9.refs_5_), channel_id=1, source_target_pairs={{0,8},{8,0},{16,24},{24,16},{32,40},{40,32},{48,56},{56,48},{64,72... | collective-permute-start | bytes 589832 | tf_op jit(solution)/shard_map/ppermute | solution.py:427
  60.8 1.4 collective-permute-start.12
  61.8 1.4 collective-permute-start.11
  95.5 1.4 collective-permute-start.15
  95.5 3.4 %collective-permute-start.17 = (f32[4,96,128]{2,1,0:T(8,128)S(1)}, f32[4,96,128]{2,1,0:T(8,128)S(1)}, u32[]{:S(2)}, u32[]{:S(2)}) collective-permute-start(f32[4,96,128]{2,1,0:T(8,128)S(1)} %get-tuple-element.35), channel_id=1, source_target_pairs={{0,8},{8,0},{16,24},{24,16},{32,40},{40,32},{48,56},{56,48},{64,72... | collective-permute-start | bytes 589832 | tf_op jit(solution)/shard_map/ppermute | solution.py:427
  96.0 5.0 %collective-permute-start.19 = (f32[4,96,128]{2,1,0:T(8,128)S(1)}, f32[4,96,128]{2,1,0:T(8,128)S(1)}, u32[]{:S(2)}, u32[]{:S(2)}) collective-permute-start(f32[4,96,128]{2,1,0:T(8,128)S(1)} %get-tuple-element.37), channel_id=1, source_target_pairs={{0,8},{8,0},{16,24},{24,16},{32,40},{40,32},{48,56},{56,48},{64,72... | collective-permute-start | bytes 589832 | tf_op jit(solution)/shard_map/ppermute | solution.py:427
  96.0 7.7 %collective-permute-start.14 = (f32[4,96,128]{2,1,0:T(8,128)S(1)}, f32[4,96,128]{2,1,0:T(8,128)S(1)}, u32[]{:S(2)}, u32[]{:S(2)}) collective-permute-start(f32[4,96,128]{2,1,0:T(8,128)S(1)} %get-tuple-element.31), channel_id=1, source_target_pairs={{0,8},{8,0},{16,24},{24,16},{32,40},{40,32},{48,56},{56,48},{64,72... | collective-permute-start | bytes 589832 | tf_op jit(solution)/shard_map/ppermute | solution.py:427
  97.5 7.8 %collective-permute-start.16 = (f32[4,96,128]{2,1,0:T(8,128)S(1)}, f32[4,96,128]{2,1,0:T(8,128)S(1)}, u32[]{:S(2)}, u32[]{:S(2)}) collective-permute-start(f32[4,96,128]{2,1,0:T(8,128)S(1)} %shard_map.110), channel_id=1, source_target_pairs={{0,16},{8,24},{16,32},{24,40},{32,48},{40,56},{48,0},{56,8},{64,80... | collective-permute-start | bytes 589832 | tf_op jit(solution)/shard_map/ppermute | solution.py:470
  99.4 9.4 %collective-permute-start.18 = (f32[4,96,128]{2,1,0:T(8,128)S(1)}, f32[4,96,128]{2,1,0:T(8,128)S(1)}, u32[]{:S(2)}, u32[]{:S(2)}) collective-permute-start(f32[4,96,128]{2,1,0:T(8,128)S(1)} %shard_map.111), channel_id=1, source_target_pairs={{0,32},{8,40},{16,48},{24,56},{32,0},{40,8},{48,16},{56,24},{64,96... | collective-permute-start | bytes 589832 | tf_op jit(solution)/shard_map/ppermute | solution.py:470
  101.5 10.3 %collective-permute-start.20 = (f32[4,96,128]{2,1,0:T(8,128)S(1)}, f32[4,96,128]{2,1,0:T(8,128)S(1)}, u32[]{:S(2)}, u32[]{:S(2)}) collective-permute-start(f32[4,96,128]{2,1,0:T(8,128)S(1)} %shard_map.112), channel_id=1, source_target_pairs={{0,48},{8,56},{16,0},{24,8},{32,16},{40,24},{48,32},{56,40},{64,11... | collective-permute-start | bytes 589832 | tf_op jit(solution)/shard_map/ppermute | solution.py:470
  112.5 9.8 %collective-permute-start.21 = (f32[96,128]{1,0:T(8,128)S(1)}, f32[96,128]{1,0:T(8,128)S(1)}, u32[]{:S(2)}, u32[]{:S(2)}) collective-permute-start(f32[96,128]{1,0:T(8,128)S(1)} %get-tuple-element.39), channel_id=1, source_target_pairs={{0,64},{8,72},{16,80},{24,88},{32,96},{40,104},{48,112},{56,120},{... | collective-permute-start | bytes 147464 | tf_op jit(solution)/shard_map/ppermute | solution.py:472
  115.2 8.6 %collective-permute-start.22 = (f32[96,128]{1,0:T(8,128)S(1)}, f32[96,128]{1,0:T(8,128)S(1)}, u32[]{:S(2)}, u32[]{:S(2)}) collective-permute-start(f32[96,128]{1,0:T(8,128)S(1)} %get-tuple-element.40), channel_id=1, source_target_pairs={{0,128},{8,136},{16,144},{24,152},{32,160},{40,168},{48,176},{56,1... | collective-permute-start | bytes 147464 | tf_op jit(solution)/shard_map/ppermute | solution.py:472
  119.0 5.8 %collective-permute-start.23 = (f32[96,128]{1,0:T(8,128)S(1)}, f32[96,128]{1,0:T(8,128)S(1)}, u32[]{:S(2)}, u32[]{:S(2)}) collective-permute-start(f32[96,128]{1,0:T(8,128)S(1)} %get-tuple-element.41), channel_id=1, source_target_pairs={{0,192},{8,200},{16,208},{24,216},{32,224},{40,232},{48,240},{56,2... | collective-permute-start | bytes 147464 | tf_op jit(solution)/shard_map/ppermute | solution.py:472
  134.3 23.9 %all-to-all-start.2 = ((f32[8,384,128]{2,1,0:T(8,128)}), f32[8,384,128]{2,1,0:T(8,128)S(1)}, u32[]{:S(2)}, u32[]{:S(2)}) async-start(f32[8,384,128]{2,1,0:T(8,128)} %get-tuple-element.29), calls=%async_computation.2 | async-start | bytes 3145728 | tf_op jit(solution)/shard_map/all_to_all | solution.py:464
  (1 other events, 24.0 us)

commit v3 on v2

v3 whole, which is shorter than its diff:
```python
import math
import types

import jax
import jax.numpy as jnp
import numpy as np
from jax import lax
from jax.experimental import pallas as pl
from jax.experimental.pallas import tpu as pltpu
from jax.sharding import PartitionSpec as P

GRID = 72
HALF = GRID // 2 + 1
LINES = 72
GROUP = 20
KX = 40
PLANE = GRID * GRID
TILES = 41
LANES = 128
SLAB = 9
TAIL = 8 * TILES
ROWS = 384
XR = 80
BAND = 32
QUARTER = ROWS // 4
PIECE = ROWS // 8
SHARE = PLANE // BAND
REST = SHARE - LANES
PACK = 96
PART = 24
F32 = jnp.float32
BF16 = jnp.bfloat16
PARAMS = pltpu.CompilerParams(vmem_limit_bytes=48 * 1024 * 1024)


def split_np(table):
    high = table.astype(jnp.bfloat16)
    low = (table - high.astype(np.float64)).astype(jnp.bfloat16)
    return high, low


def tables():
    k = np.arange(GRID)
    ang = 2.0 * np.pi / GRID * ((k[:, None] * k[None, :]) % GRID)
    cos, sin = np.cos(ang), np.sin(ang)
    place = np.arange(GRID)
    plane = np.where(place < 64, SLAB * (place // 8) + place % 8, SLAB * (place - 64) + 8)
    forward_x = np.zeros((2 * KX, XR))
    forward_x[:HALF, :GRID] = cos[:HALF][:, plane]
    forward_x[KX : KX + HALF, :GRID] = -sin[:HALF][:, plane]
    weight = np.where((k[:HALF] == 0) | (k[:HALF] == GRID // 2), 1.0, 2.0) / GRID**3
    inverse_x = np.zeros((XR, 2 * KX))
    inverse_x[:GRID, :HALF] = (weight[:, None] * cos[:HALF][:, plane]).T
    inverse_x[:GRID, KX : KX + HALF] = -(weight[:, None] * sin[:HALF][:, plane]).T
    along_z = np.zeros((LANES, 2 * LANES))
    along_z[:GRID, :GRID] = cos
    along_z[:GRID, LANES : LANES + GRID] = sin
    forward_y = np.block([[cos, sin], [-sin, cos]])
    inverse_y = np.block([[cos, -sin], [sin, cos]])

    def left(table):
        high, low = split_np(table)
        return np.concatenate([high, high, low], axis=1)

    z_high, z_low = split_np(along_z)
    z_three = np.concatenate([z_high, z_high, z_low], axis=0)
    fold = np.where(k > GRID // 2, k - GRID, k).astype(np.float64)
    squares = np.ones((GRID, LANES))
    squares[:, :GRID] = fold[:, None] ** 2 + fold[None, :] ** 2
    return (
        left(forward_x),
        left(inverse_x),
        z_three,
        left(forward_y),
        left(inverse_y),
        squares.astype(np.float32),
    )


def split(x):
    high = x.astype(BF16)
    low = (x - high.astype(F32)).astype(BF16)
    return high, low


def left_dot(table, x):
    high, low = split(x)
    return jnp.dot(table, jnp.concatenate([high, low, high], axis=0), preferred_element_type=F32)


def right_dot(x, table):
    high, low = split(x)
    three = jnp.concatenate([high, low, high], axis=1)
    return jnp.dot(three, table, preferred_element_type=F32)


def pick(index, choices):
    value = choices[0]
    for d in range(1, len(choices)):
        value = jnp.where(index == d, choices[d], value)
    return value


def shape(*dims):
    return jax.ShapeDtypeStruct(dims, F32)


def call(kernel, out_shape, info, *arrays, after=(), scratch=(), flops=0):
    specs = [pl.BlockSpec(memory_space=pltpu.SMEM)]
    specs += [pl.BlockSpec(memory_space=pltpu.VMEM) for _ in arrays]
    specs += [pl.BlockSpec(memory_space=pl.ANY) for _ in after]
    size = sum(a.size for a in arrays) * 4
    return pl.pallas_call(
        kernel,
        in_specs=specs,
        out_shape=out_shape,
        scratch_shapes=list(scratch),
        compiler_params=PARAMS,
        cost_estimate=pl.CostEstimate(flops=flops, bytes_accessed=2 * size, transcendentals=0),
    )(info, *arrays, *after)


MY_X, MY_C, MY_Z, X_STEP, C_OWN, Z_STEP = 0, 1, 2, 3, 5, 7


def pack_kernel(info, orb_ref, out_ref, *quarters):
    for o in range(2):
        out_ref[o, TAIL:ROWS, :] = jnp.zeros((ROWS - TAIL, LANES), F32)
        for t in range(TILES):
            wide = min(LANES, PLANE - t * LANES)
            if wide < LANES:
                out_ref[o, 8 * t : 8 * t + 8, :] = jnp.zeros((8, LANES), F32)
            cols = slice(t * LANES, t * LANES + wide)
            out_ref[o, 8 * t : 8 * t + 8, :wide] = orb_ref[o, 0:8, cols]
            out_ref[o, TAIL + t : TAIL + t + 1, :wide] = orb_ref[o, 8:9, cols]
    for d in range(4):
        first = pl.multiple_of(QUARTER * lax.rem(info[MY_X] + d, 4), QUARTER)
        for o in range(2):
            quarters[d][o] = out_ref[o, pl.ds(first, QUARTER), :]


def spread_kernel(info, packed_ref, after_ref, out_ref):
    for g in range(8):
        out_ref[g] = packed_ref[g // 4]


def pick_x_kernel(info, q0, q1, q2, q3, keep_ref, give_ref):
    for ref, half in ((keep_ref, info[MY_C]), (give_ref, 1 - info[MY_C])):
        rows = pl.ds(pl.multiple_of(half * PIECE, PIECE), PIECE)
        for step in range(2):
            for m in range(2):
                choices = [q[m, rows, :] for q in (q0, q1, q2, q3)]
                ref[2 * step + m] = pick(info[X_STEP + step], choices)


def pick_core_kernel(info, keep_ref, got_ref, out_ref):
    for b in range(4):
        out_ref[b] = jnp.where(info[C_OWN + b // 2] == 1, keep_ref[b], got_ref[b])


def pick_z_kernel(info, z0, z1, z2, z3, after_ref, out_ref):
    for b in range(4):
        value = pick(info[Z_STEP + b // 2], [z[b] for z in (z0, z1, z2, z3)])
        out_ref[b] = value
        out_ref[4 + b] = value


def whole_block(r, info, scale):
    for d in range(4):
        quarter = QUARTER * lax.rem(info[MY_X] + 4 - d, 4)
        for ref, half in ((r.mine[d], info[MY_C]), (r.other[d], 1 - info[MY_C])):
            rows = pl.ds(pl.multiple_of(quarter + PIECE * half, PIECE), PIECE)
            for s in range(8):
                r.blk[s, rows, :] = ref[s]


def density(r, info, scale):
    r.wide[GRID:XR, :] = jnp.zeros((XR - GRID, (TILES + 2) * LANES), F32)
    for t in range(TILES):
        cols = slice(t * LANES, (t + 1) * LANES)
        rows = slice(8 * t, 8 * t + 8)
        for s in range(8):
            r.wide[8 * s : 8 * s + 8, cols] = r.orb[s, rows, :] * r.blk[s, rows, :]
            r.orb_tail[s : s + 1, cols] = r.orb[s, TAIL + t : TAIL + t + 1, :]
            r.blk_tail[s : s + 1, cols] = r.blk[s, TAIL + t : TAIL + t + 1, :]
        r.wide[64:72, cols] = r.orb_tail[:, cols] * r.blk_tail[:, cols]


def forward_x(r, info, scale):
    for t in range(0, TILES, 4):
        cols = slice(t * LANES, min(t + 4, TILES) * LANES)
        r.wide[:, cols] = left_dot(r.fx[...], r.wide[:, cols])


def to_columns(r, info, scale):
    lane = lax.broadcasted_iota(jnp.int32, (XR, LANES), 1)
    for y in range(GRID):
        t, off = divmod(y * GRID, LANES)
        value = r.wide[:, t * LANES : (t + 1) * LANES]
        if off:
            value = pltpu.roll(value, LANES - off, 1)
            if off + GRID > LANES:
                after = pltpu.roll(r.wide[:, (t + 1) * LANES : (t + 2) * LANES], LANES - off, 1)
                value = jnp.where(lane < LANES - off, value, after)
        r.col[y * XR : (y + 1) * XR, :] = value


def forward_z(r, info, scale):
    def step(j, carry):
        base = pl.multiple_of(j * LINES * XR, LINES * XR)
        both = right_dot(r.col[pl.ds(base, LINES * XR), :], r.zt[...])
        base = pl.multiple_of(j * LINES * KX, LINES * KX)
        for y in range(LINES):
            real = both[y * XR : y * XR + KX]
            imag = both[y * XR + KX : (y + 1) * XR]
            rows = pl.ds(base + y * KX, KX)
            r.re[rows, :] = real[:, :LANES] + imag[:, LANES:]
            r.im[rows, :] = imag[:, :LANES] - real[:, LANES:]
        return carry

    lax.fori_loop(0, GRID // LINES, step, 0)


def along_y(r, info, scale):
    def step(j, carry):
        strides = [pl.ds(GROUP * j + q, GRID, stride=KX) for q in range(GROUP)]
        lines = [jnp.concatenate([r.re[s, :], r.im[s, :]], axis=0) for s in strides]
        spec = left_dot(r.fy[...], jnp.concatenate(lines, axis=1))
        factors = []
        for q in range(GROUP):
            kx = (GROUP * j + q).astype(F32)
            square = r.sq[...] + kx * kx
            factor = jnp.where(square > 0, scale / jnp.maximum(square, 1.0), 0.0)
            factors.append(jnp.concatenate([factor, factor], axis=0))
        spec = spec * jnp.concatenate(factors, axis=1)
        back = left_dot(r.iy[...], spec)
        for q, s in enumerate(strides):
            cols = slice(q * LANES, (q + 1) * LANES)
            r.re[s, :] = back[:GRID, cols]
            r.im[s, :] = back[GRID:, cols]
        return carry

    lax.fori_loop(0, KX // GROUP, step, 0)


def inverse_z(r, info, scale):
    def step(j, carry):
        base = pl.multiple_of(j * LINES * KX, LINES * KX)
        rows = pl.ds(base, LINES * KX)
        real = right_dot(r.re[rows, :], r.zt[...])
        imag = right_dot(r.im[rows, :], r.zt[...])
        new_re = real[:, :LANES] - imag[:, LANES:]
        new_im = real[:, LANES:] + imag[:, :LANES]
        base = pl.multiple_of(j * LINES * XR, LINES * XR)
        for y in range(LINES):
            r.col[pl.ds(base + y * XR, KX), :] = new_re[y * KX : (y + 1) * KX]
            r.col[pl.ds(base + y * XR + KX, KX), :] = new_im[y * KX : (y + 1) * KX]
        return carry

    lax.fori_loop(0, GRID // LINES, step, 0)


def from_columns(r, info, scale):
    lane = lax.broadcasted_iota(jnp.int32, (XR, LANES), 1)
    for t in range(TILES):
        value = jnp.zeros((XR, LANES), F32)
        for y in range(GRID):
            at = y * GRID - t * LANES
            if at >= LANES or at + GRID <= 0:
                continue
            piece = r.col[y * XR : (y + 1) * XR, :]
            if at % LANES:
                piece = pltpu.roll(piece, at % LANES, 1)
            keep = (lane >= at) & (lane < at + GRID)
            value = jnp.where(keep, piece, value)
        r.wide[:, t * LANES : (t + 1) * LANES] = value


def inverse_x(r, info, scale):
    for s in range(8):
        r.own[s, TAIL + TILES : ROWS, :] = jnp.zeros((ROWS - TAIL - TILES, LANES), F32)
    for t in range(0, TILES, 4):
        last = min(t + 4, TILES)
        cols = slice(t * LANES, last * LANES)
        pot = -left_dot(r.ix[...], r.wide[:, cols])
        for u in range(t, last):
            part = pot[:, (u - t) * LANES : (u - t + 1) * LANES]
            rows = slice(8 * u, 8 * u + 8)
            one = slice(u * LANES, (u + 1) * LANES)
            tail = part[64:72] * r.blk_tail[:, one]
            for s in range(8):
                piece = part[8 * s : 8 * s + 8]
                r.own[s, rows, :] = piece * r.blk[s, rows, :]
                r.own[s, TAIL + u : TAIL + u + 1, :] = tail[s : s + 1]
                r.wide[8 * s : 8 * s + 8, one] = piece * r.orb[s, rows, :]
            r.wide[64:72, one] = part[64:72] * r.orb_tail[:, one]
    r.wide[:, TILES * LANES :] = jnp.zeros((XR, 2 * LANES), F32)


def share_out(r, info, scale):
    lane = lax.broadcasted_iota(jnp.int32, (GRID, LANES), 1)
    third = lane[:8]

    def turned(tile, turn):
        value = r.wide[:GRID, tile * LANES : (tile + 1) * LANES]
        return pltpu.roll(value, turn, 1) if turn else value

    for band in range(BAND):
        z, x, c = band // 8, band // 2 % 4, band % 2
        core = lax.rem(c + info[MY_C], 2)
        place = 4 * core + lax.rem(x + 4 - info[MY_X], 4)
        z = lax.rem(z + 4 - info[MY_Z], 4)
        t, off = divmod(band * SHARE, LANES)
        turn = (LANES - off) % LANES
        first, second = turned(t, turn), turned(t + 1, turn)
        head, rest = jnp.where(lane < LANES - off, first, second), second
        if off + REST > LANES:
            rest = jnp.where(lane < LANES - off, second, turned(t + 2, turn))
        r.cut[place, z, :GRID, :] = head
        for j in range(3):
            one, two, three = (rest[8 * (3 * j + k) : 8 * (3 * j + k) + 8] for k in range(3))
            two, three = pltpu.roll(two, REST, 1), pltpu.roll(three, 2 * REST, 1)
            packed = jnp.where(third < REST, one, jnp.where(third < 2 * REST, two, three))
            r.cut[place, z, GRID + 8 * j : GRID + 8 * j + 8, :] = packed
    for x in range(4):
        r.keep[x][...] = r.cut[x]
        r.give[x][...] = r.cut[4 + x]


STAGES = (
    whole_block,
    density,
    forward_x,
    to_columns,
    forward_z,
    along_y,
    inverse_z,
    from_columns,
    inverse_x,
    share_out,
)


def field_kernel(scale, info, *refs):
    tables = ("fx", "ix", "zt", "fy", "iy", "sq")
    scratch = ("blk", "wide", "orb_tail", "blk_tail", "col", "re", "im", "cut")
    r = types.SimpleNamespace(orb=refs[0], mine=refs[1:5], other=refs[5:9], own=refs[15])
    r.keep, r.give = refs[16:20], refs[20:24]
    vars(r).update(zip(tables, refs[9:15]))
    vars(r).update(zip(scratch, refs[24:]))
    for stage in STAGES:
        stage(r, info, scale)


def fields(info, orbital, pieces, scale):
    def body(*refs):
        field_kernel(scale, *refs)

    return call(
        body,
        [shape(8, ROWS, LANES)] + [shape(4, PACK, LANES)] * 8,
        info,
        orbital,
        *pieces,
        *[jnp.asarray(t) for t in tables()],
        scratch=[
            pltpu.VMEM((8, ROWS, LANES), F32),
            pltpu.VMEM((XR, (TILES + 2) * LANES), F32),
            pltpu.VMEM((8, TILES * LANES), F32),
            pltpu.VMEM((8, TILES * LANES), F32),
            pltpu.VMEM((GRID * XR, LANES), F32),
            pltpu.VMEM((GRID * KX, LANES), F32),
            pltpu.VMEM((GRID * KX, LANES), F32),
            pltpu.VMEM((8, 4, PACK, LANES), F32),
        ],
        flops=10**10,
    )


def add_kernel(info, a_ref, b_ref, out_ref):
    out_ref[...] = a_ref[...] + b_ref[...]


def add_x_kernel(info, k_ref, g_ref, r1, r2, r3, *outs):
    for z in range(4):
        outs[z][...] = k_ref[z] + g_ref[z] + r1[z] + r2[z] + r3[z]


def add_z_kernel(info, s_ref, r1, r2, r3, after_ref, out_ref, sum_ref):
    sum_ref[...] = s_ref[...] + r1[...] + r2[...] + r3[...]
    out_ref[...] = jnp.zeros((8, PART, LANES), F32)

    def rest(tile):
        value = sum_ref[GRID + 8 * (tile // 3) : GRID + 8 * (tile // 3) + 8, :]
        turn = tile % 3 * REST
        return pltpu.roll(value, LANES - turn, 1) if turn else value

    last = rest(8)
    for s in range(8):
        out_ref[s, 0:8, :] = sum_ref[8 * s : 8 * s + 8, :]
        out_ref[s, 8:16, :] = rest(s)
        out_ref[s, 16:17, :] = sum_ref[64 + s : 65 + s, :]
        out_ref[s, 17:18, :] = last[s : s + 1]


def share_kernel(info, part_ref, out_ref):
    for b in range(4):
        total = part_ref[b] + part_ref[4 + b]
        at = (b // 2, b % 2)
        out_ref[at[0], at[1], 0:8, :LANES] = total[0:8]
        out_ref[at[0], at[1], 0:8, LANES:SHARE] = total[8:16, :REST]
        out_ref[at[0], at[1], 8:9, :LANES] = total[16:17]
        out_ref[at[0], at[1], 8:9, LANES:SHARE] = total[17:18, :REST]


def own_kernel(info, part_ref, out_ref):
    for i in range(2):
        for t in range(TILES + 1):
            rows = slice(TAIL, ROWS) if t == TILES else slice(8 * t, 8 * t + 8)
            total = part_ref[4 * i, rows, :]
            for b in range(1, 4):
                total = total + part_ref[4 * i + b, rows, :]
            if t == TILES:
                for u in range(TILES):
                    wide = min(LANES, PLANE - u * LANES)
                    out_ref[i, 8:9, u * LANES : u * LANES + wide] = total[u : u + 1, :wide]
            else:
                wide = min(LANES, PLANE - t * LANES)
                out_ref[i, 0:8, t * LANES : t * LANES + wide] = total[:, :wide]


def shift_x(d):
    return [(i, i // 8 * 8 + (i // 2 + d) % 4 * 2 + i % 2) for i in range(BAND)]


def shift_z(d):
    return [(i, (i + 8 * d) % BAND) for i in range(BAND)]


def other_core(x):
    return lax.ppermute(x, "band", [(i, i ^ 1) for i in range(BAND)])


def scalars(block_owner):
    me = lax.axis_index("band")
    owner = jnp.clip(block_owner, 0, BAND - 1)
    x, c, z = me // 2 % 4, me % 2, me // 8
    parts = [
        jnp.stack([x, c, z]),
        (x - owner // 2 % 4) % 4,
        (c == owner % 2).astype(jnp.int32),
        (z - owner // 8) % 4,
    ]
    return jnp.concatenate([p.astype(jnp.int32) for p in parts])


def on_device(orbitals, block_owner):
    scale = math.sqrt(GRID**3 / (2 * BAND))
    info = scalars(block_owner)
    packed, *quarters = call(
        pack_kernel, [shape(2, ROWS, LANES)] + [shape(2, QUARTER, LANES)] * 4, info, orbitals
    )
    quarters = quarters[:1] + [lax.ppermute(quarters[d], "band", shift_x(d)) for d in (1, 2, 3)]
    spread = call(spread_kernel, shape(8, ROWS, LANES), info, packed, after=quarters[1:2])
    orbital = lax.all_to_all(spread, "grid", 0, 0)
    half = shape(4, PIECE, LANES)
    keep, give = call(pick_x_kernel, [half, half], info, *quarters)
    mine = call(pick_core_kernel, half, info, keep, other_core(give))
    along = [mine] + [lax.ppermute(mine, "band", shift_z(d)) for d in (1, 2, 3)]
    mine = call(pick_z_kernel, shape(8, PIECE, LANES), info, *along, after=[orbital])
    piece = lax.all_to_all(mine, "grid", 0, 0)
    pieces = [piece] + [lax.ppermute(piece, "band", shift_x(d)) for d in (1, 2, 3)]
    pieces = pieces + [other_core(p) for p in pieces]

    own, *shares = fields(info, orbital, pieces, scale)
    own = lax.all_to_all(own, "grid", 0, 0)
    kept, got = shares[:4], [other_core(g) for g in shares[4:]]
    part = shape(4, PACK, LANES)
    moved = []
    for d in (1, 2, 3):
        moved.append(lax.ppermute(call(add_kernel, part, info, kept[d], got[d]), "band", shift_x(d)))
    sums = call(add_x_kernel, [shape(PACK, LANES)] * 4, info, kept[0], got[0], *moved)
    moved = [lax.ppermute(sums[d], "band", shift_z(d)) for d in (1, 2, 3)]
    slabs = call(
        add_z_kernel,
        shape(8, PART, LANES),
        info,
        sums[0],
        *moved,
        after=[own],
        scratch=[pltpu.VMEM((PACK, LANES), F32)],
    )
    block_field = call(
        share_kernel, shape(2, 2, SLAB, SHARE), info, lax.all_to_all(slabs, "grid", 0, 0)
    )
    field = call(own_kernel, shape(2, SLAB, PLANE), info, own)
    return field, block_field


def solution(mesh):
    return jax.shard_map(
        on_device,
        mesh=mesh,
        in_specs=(P("band", "grid", None), P()),
        out_specs=(P("band", "grid", None), P(None, None, "grid", "band")),
        check_vma=False,
    )
```

time: 160 us -> 133 us (0.83)
  waiting for transfers between devices: 59.3 us -> 44.3 us
  Pallas kernels: 31 us -> 19.5 us
  blocking collectives: 20.1 us -> 12 us
  starting transfers between devices: 43.2 us -> 48.1 us
    all_to_all x1 -> x2, waiting for transfers between devices: 19.2 us -> 4.97 us  [the longest x1 4.97 us: on_device(): lax.all_to_all(slabs, 'grid', 0, 0)]
    pallas_call x12 -> x13, Pallas kernels: 31 us -> 19.5 us  [call(): pl.pallas_call(kernel, in_specs=specs, out_shape=out_shape, scratch_shape...]
    all_to_all x1 -> x0, blocking collectives: 8.91 us -> none  [on_device(): lax.all_to_all(slabs, 'grid', 0, 0)]
    all_to_all x1, waiting for transfers between devices: 7.49 us -> 0.01 us  [on_device(): orbital = lax.all_to_all(spread, 'grid', 0, 0)]
    all_to_all x1 -> x2, starting transfers between devices: 3.58 us -> 10.4 us  [the longest x1 6.87 us: on_device(): lax.all_to_all(slabs, 'grid', 0, 0)]
    ppermute x3, starting transfers between devices: 9.78 us -> 6.61 us  [on_device(): moved = [lax.ppermute(sums[d], 'band', shift_z(d)) for d in (1, 2, 3)]]
    ppermute x3, waiting for transfers between devices: 8.39 us -> 11.2 us  [on_device(): along = [mine] + [lax.ppermute(mine, 'band', shift_z(d)) for d in (1, 2, 3)]]
    unnamed x17, local copies, waits for them, and re-layouts: 2.66 us -> 5.09 us
  transfers between devices with their start and end apart: 26 -> 27, of which waited for: 19 -> 19; matrix products, arithmetic and copies ran while one was open for 0% -> 1% of each run, Pallas kernels for 1% -> 3%
where the time goes in v3:
time: 133 us; the launch traced here: 131 us
  starting transfers between devices  48.1 us (36%)
  waiting for transfers between devices  44.3 us (33%)
  Pallas kernels  19.5 us (15%)
  blocking collectives  12 us (9%)
  local copies, waits for them, and re-layouts  5.17 us (4%)
  other arithmetic  1.35 us (1%)
    pallas_call x13, Pallas kernels, call(): pl.pallas_call(kernel, in_specs=specs, out_shape=out_shape, scratch_shape...  19.5 us
    all_to_all x1, blocking collectives, on_device(): piece = lax.all_to_all(mine, 'grid', 0, 0)  12 us
    ppermute x3, waiting for transfers between devices, on_device(): along = [mine] + [lax.ppermute(mine, 'band', shift_z(d)) for d in (1, 2, 3)]  11.2 us
    ppermute x3, starting transfers between devices, on_device(): along = [mine] + [lax.ppermute(mine, 'band', shift_z(d)) for d in (1, 2, 3)]  9.29 us
    ppermute x3, waiting for transfers between devices, on_device(): lax.ppermute(call(add_kernel, part, info, kept[d], got[d]), 'band', shift...  8.46 us
    ppermute x3, waiting for transfers between devices, on_device(): lax.ppermute(quarters[d], 'band', shift_x(d))  6.99 us
    all_to_all x1, starting transfers between devices, on_device(): lax.all_to_all(slabs, 'grid', 0, 0)  6.87 us
    ppermute x3, starting transfers between devices, on_device(): moved = [lax.ppermute(sums[d], 'band', shift_z(d)) for d in (1, 2, 3)]  6.61 us
  transfers between devices with their start and end apart: 27, of which 19 were waited for; matrix products, arithmetic and copies ran while one was open for 1% of the time, Pallas kernels for 3%

profile of v3, /device:TPU:2, one launch (start us, length us, event | category | flops | bytes accessed | tf_op | source)
XLA Modules:
  0.0 131.3 jit_solution(8150581639097365970)
XLA Ops:
  0.7 1.0 copy.10.orb_ref
  3.8 1.6 %collective-permute-start = (f32[2,96,128]{2,1,0:T(8,128)S(1)}, f32[2,96,128]{2,1,0:T(8,128)S(1)}, u32[]{:S(2)}, u32[]{:S(2)}) collective-permute-start(f32[2,96,128]{2,1,0:T(8,128)S(1)} %get-tuple-element.23), channel_id=1, source_target_pairs={{0,16},{8,24},{16,32},{24,40},{32,48},{40,56},{48,0},{56,8},{64,80... | collective-permute-start | bytes 294920 | tf_op jit(solution)/shard_map/ppermute | solution.py:463
  5.4 3.4 %collective-permute-done.after_ref.q1 = f32[2,96,128]{2,1,0:T(8,128)S(1)} collective-permute-done((f32[2,96,128]{2,1,0:T(8,128)S(1)}, f32[2,96,128]{2,1,0:T(8,128)S(1)}, u32[]{:S(2)}, u32[]{:S(2)}) %collective-permute-start) | collective-permute-done | bytes 98336 | tf_op jit(solution)/shard_map/ppermute | solution.py:463
  8.7 1.8 %shard_map.96 = f32[8,384,128]{2,1,0:T(8,128)} custom-call(s32[9]{0:T(128)S(1)} %concatenate.3.info.refs_0_, f32[2,384,128]{2,1,0:T(8,128)S(1)} %get-tuple-element.22.packed_ref, f32[2,96,128]{2,1,0:T(8,128)S(1)} %collective-permute-done.after_ref.q1), custom_call_target="tpu_custom_call" | custom-call | bytes 786432 | tf_op jit(solution)/shard_map/pallas_call | solution.py:113
  10.6 5.6 %all-to-all-start = ((f32[8,384,128]{2,1,0:T(8,128)}), f32[8,384,128]{2,1,0:T(8,128)S(1)}, u32[]{:S(2)}, u32[]{:S(2)}) async-start(f32[8,384,128]{2,1,0:T(8,128)} %shard_map.96), calls=%async_computation | async-start | bytes 3145728 | tf_op jit(solution)/shard_map/all_to_all | solution.py:465
  16.1 2.1 %collective-permute-start.1 = (f32[2,96,128]{2,1,0:T(8,128)S(1)}, f32[2,96,128]{2,1,0:T(8,128)S(1)}, u32[]{:S(2)}, u32[]{:S(2)}) collective-permute-start(f32[2,96,128]{2,1,0:T(8,128)S(1)} %get-tuple-element.25), channel_id=1, source_target_pairs={{0,32},{8,40},{16,48},{24,56},{32,0},{40,8},{48,16},{56,24},{64,96... | collective-permute-start | bytes 294920 | tf_op jit(solution)/shard_map/ppermute | solution.py:463
  18.3 1.4 %collective-permute-start.2 = (f32[2,96,128]{2,1,0:T(8,128)S(1)}, f32[2,96,128]{2,1,0:T(8,128)S(1)}, u32[]{:S(2)}, u32[]{:S(2)}) collective-permute-start(f32[2,96,128]{2,1,0:T(8,128)S(1)} %get-tuple-element.26), channel_id=1, source_target_pairs={{0,48},{8,56},{16,0},{24,8},{32,16},{40,24},{48,32},{56,40},{64,11... | collective-permute-start | bytes 294920 | tf_op jit(solution)/shard_map/ppermute | solution.py:463
  19.7 2.6 %collective-permute-done.1.q2 = f32[2,96,128]{2,1,0:T(8,128)S(1)} collective-permute-done((f32[2,96,128]{2,1,0:T(8,128)S(1)}, f32[2,96,128]{2,1,0:T(8,128)S(1)}, u32[]{:S(2)}, u32[]{:S(2)}) %collective-permute-start.1) | collective-permute-done | bytes 98336 | tf_op jit(solution)/shard_map/ppermute | solution.py:463
  24.0 1.3 collective-permute-done.3.got_ref
  25.9 5.5 %collective-permute-start.6 = (f32[4,48,128]{2,1,0:T(8,128)S(1)}, f32[4,48,128]{2,1,0:T(8,128)S(1)}, u32[]{:S(2)}, u32[]{:S(2)}) collective-permute-start(f32[4,48,128]{2,1,0:T(8,128)S(1)} %shard_map.98.z0), channel_id=1, source_target_pairs={{0,192},{8,200},{16,208},{24,216},{32,224},{40,232},{48,240},{56,2... | collective-permute-start | bytes 294920 | tf_op jit(solution)/shard_map/ppermute | solution.py:469
  31.3 1.4 %collective-permute-start.5 = (f32[4,48,128]{2,1,0:T(8,128)S(1)}, f32[4,48,128]{2,1,0:T(8,128)S(1)}, u32[]{:S(2)}, u32[]{:S(2)}) collective-permute-start(f32[4,48,128]{2,1,0:T(8,128)S(1)} %shard_map.98.z0), channel_id=1, source_target_pairs={{0,128},{8,136},{16,144},{24,152},{32,160},{40,168},{48,176},{56,1... | collective-permute-start | bytes 294920 | tf_op jit(solution)/shard_map/ppermute | solution.py:469
  32.8 2.4 %collective-permute-start.4 = (f32[4,48,128]{2,1,0:T(8,128)S(1)}, f32[4,48,128]{2,1,0:T(8,128)S(1)}, u32[]{:S(2)}, u32[]{:S(2)}) collective-permute-start(f32[4,48,128]{2,1,0:T(8,128)S(1)} %shard_map.98.z0), channel_id=1, source_target_pairs={{0,64},{8,72},{16,80},{24,88},{32,96},{40,104},{48,112},{56,120},{... | collective-permute-start | bytes 294920 | tf_op jit(solution)/shard_map/ppermute | solution.py:469
  35.2 11.0 %collective-permute-done.5.z2 = f32[4,48,128]{2,1,0:T(8,128)S(1)} collective-permute-done((f32[4,48,128]{2,1,0:T(8,128)S(1)}, f32[4,48,128]{2,1,0:T(8,128)S(1)}, u32[]{:S(2)}, u32[]{:S(2)}) %collective-permute-start.5) | collective-permute-done | bytes 98336 | tf_op jit(solution)/shard_map/ppermute | solution.py:469
  46.9 12.0 %all_to_all.20.refs_2_ = f32[8,48,128]{2,1,0:T(8,128)S(1)} all-to-all(f32[8,48,128]{2,1,0:T(8,128)S(1)} %shard_map.99), channel_id=1, replica_groups=mesh['band'=32,'grid'=8] {'grid'}, dimensions={0} | all-to-all | bytes 393216 | tf_op jit(solution)/shard_map/all_to_all | solution.py:471
  58.9 1.7 %collective-permute-start.9 = (f32[8,48,128]{2,1,0:T(8,128)S(1)}, f32[8,48,128]{2,1,0:T(8,128)S(1)}, u32[]{:S(2)}, u32[]{:S(2)}) collective-permute-start(f32[8,48,128]{2,1,0:T(8,128)S(1)} %all_to_all.20.refs_2_), channel_id=1, source_target_pairs={{0,48},{8,56},{16,0},{24,8},{32,16},{40,24},{48,32},{56,40},{64,11... | collective-permute-start | bytes 589832 | tf_op jit(solution)/shard_map/ppermute | solution.py:472
  60.7 1.2 collective-permute-start.8
  61.9 1.8 %collective-permute-start.7 = (f32[8,48,128]{2,1,0:T(8,128)S(1)}, f32[8,48,128]{2,1,0:T(8,128)S(1)}, u32[]{:S(2)}, u32[]{:S(2)}) collective-permute-start(f32[8,48,128]{2,1,0:T(8,128)S(1)} %all_to_all.20.refs_2_), channel_id=1, source_target_pairs={{0,16},{8,24},{16,32},{24,40},{32,48},{40,56},{48,0},{56,8},{64,80... | collective-permute-start | bytes 589832 | tf_op jit(solution)/shard_map/ppermute | solution.py:472
  64.6 3.2 %collective-permute-done.8.refs_4_ = f32[8,48,128]{2,1,0:T(8,128)S(1)} collective-permute-done((f32[8,48,128]{2,1,0:T(8,128)S(1)}, f32[8,48,128]{2,1,0:T(8,128)S(1)}, u32[]{:S(2)}, u32[]{:S(2)}) %collective-permute-start.8) | collective-permute-done | bytes 196640 | tf_op jit(solution)/shard_map/ppermute | solution.py:472
  72.7 10.7 %shard_map.100 = (f32[8,384,128]{2,1,0:T(8,128)}, f32[4,96,128]{2,1,0:T(8,128)S(1)}, f32[4,96,128]{2,1,0:T(8,128)S(1)}, f32[4,96,128]{2,1,0:T(8,128)S(1)}, f32[4...) custom-call(s32[9]{0:T(128)S(1)} %concatenate.3.info.refs_0_, ...), custom_call_target="tpu_custom_call" | custom-call | flops 10000000000 | bytes 8454144 | tf_op jit(solution)/shard_map/pallas_call | solution.py:113
  83.4 3.6 %all-to-all-start.2 = ((f32[8,384,128]{2,1,0:T(8,128)}), f32[8,384,128]{2,1,0:T(8,128)S(1)}, u32[]{:S(2)}, u32[]{:S(2)}) async-start(f32[8,384,128]{2,1,0:T(8,128)} %get-tuple-element.29), calls=%async_computation.2 | async-start | bytes 3145728 | tf_op jit(solution)/shard_map/all_to_all | solution.py:476
  89.1 1.5 %collective-permute-start.16 = (f32[4,96,128]{2,1,0:T(8,128)S(1)}, f32[4,96,128]{2,1,0:T(8,128)S(1)}, u32[]{:S(2)}, u32[]{:S(2)}) collective-permute-start(f32[4,96,128]{2,1,0:T(8,128)S(1)} %shard_map.102), channel_id=1, source_target_pairs={{0,16},{8,24},{16,32},{24,40},{32,48},{40,56},{48,0},{56,8},{64,80... | collective-permute-start | bytes 589832 | tf_op jit(solution)/shard_map/ppermute | solution.py:481
  91.2 3.4 %collective-permute-start.18 = (f32[4,96,128]{2,1,0:T(8,128)S(1)}, f32[4,96,128]{2,1,0:T(8,128)S(1)}, u32[]{:S(2)}, u32[]{:S(2)}) collective-permute-start(f32[4,96,128]{2,1,0:T(8,128)S(1)} %shard_map.103), channel_id=1, source_target_pairs={{0,32},{8,40},{16,48},{24,56},{32,0},{40,8},{48,16},{56,24},{64,96... | collective-permute-start | bytes 589832 | tf_op jit(solution)/shard_map/ppermute | solution.py:481
  95.3 2.3 %collective-permute-done.16.r1 = f32[4,96,128]{2,1,0:T(8,128)S(1)} collective-permute-done((f32[4,96,128]{2,1,0:T(8,128)S(1)}, f32[4,96,128]{2,1,0:T(8,128)S(1)}, u32[]{:S(2)}, u32[]{:S(2)}) %collective-permute-start.16) | collective-permute-done | bytes 196640 | tf_op jit(solution)/shard_map/ppermute | solution.py:481
  97.5 3.0 %collective-permute-done.18.r2 = f32[4,96,128]{2,1,0:T(8,128)S(1)} collective-permute-done((f32[4,96,128]{2,1,0:T(8,128)S(1)}, f32[4,96,128]{2,1,0:T(8,128)S(1)}, u32[]{:S(2)}, u32[]{:S(2)}) %collective-permute-start.18) | collective-permute-done | bytes 196640 | tf_op jit(solution)/shard_map/ppermute | solution.py:481
  100.5 3.2 %collective-permute-done.20.r3 = f32[4,96,128]{2,1,0:T(8,128)S(1)} collective-permute-done((f32[4,96,128]{2,1,0:T(8,128)S(1)}, f32[4,96,128]{2,1,0:T(8,128)S(1)}, u32[]{:S(2)}, u32[]{:S(2)}) %collective-permute-start.20) | collective-permute-done | bytes 196640 | tf_op jit(solution)/shard_map/ppermute | solution.py:481
  104.3 2.6 %collective-permute-start.21 = (f32[96,128]{1,0:T(8,128)S(1)}, f32[96,128]{1,0:T(8,128)S(1)}, u32[]{:S(2)}, u32[]{:S(2)}) collective-permute-start(f32[96,128]{1,0:T(8,128)S(1)} %get-tuple-element.39), channel_id=1, source_target_pairs={{0,64},{8,72},{16,80},{24,88},{32,96},{40,104},{48,112},{56,120},{... | collective-permute-start | bytes 147464 | tf_op jit(solution)/shard_map/ppermute | solution.py:483
  106.9 1.5 %collective-permute-start.22 = (f32[96,128]{1,0:T(8,128)S(1)}, f32[96,128]{1,0:T(8,128)S(1)}, u32[]{:S(2)}, u32[]{:S(2)}) collective-permute-start(f32[96,128]{1,0:T(8,128)S(1)} %get-tuple-element.40), channel_id=1, source_target_pairs={{0,128},{8,136},{16,144},{24,152},{32,160},{40,168},{48,176},{56,1... | collective-permute-start | bytes 147464 | tf_op jit(solution)/shard_map/ppermute | solution.py:483
  108.4 2.5 %collective-permute-start.23 = (f32[96,128]{1,0:T(8,128)S(1)}, f32[96,128]{1,0:T(8,128)S(1)}, u32[]{:S(2)}, u32[]{:S(2)}) collective-permute-start(f32[96,128]{1,0:T(8,128)S(1)} %get-tuple-element.41), channel_id=1, source_target_pairs={{0,192},{8,200},{16,208},{24,216},{32,224},{40,232},{48,240},{56,2... | collective-permute-start | bytes 147464 | tf_op jit(solution)/shard_map/ppermute | solution.py:483
  111.2 3.7 %collective-permute-done.22.r2 = f32[96,128]{1,0:T(8,128)S(1)} collective-permute-done((f32[96,128]{1,0:T(8,128)S(1)}, f32[96,128]{1,0:T(8,128)S(1)}, u32[]{:S(2)}, u32[]{:S(2)}) %collective-permute-start.22) | collective-permute-done | bytes 49184 | tf_op jit(solution)/shard_map/ppermute | solution.py:483
  115.4 1.2 shard_map.106
  116.7 6.9 %all-to-all-start.3 = ((f32[8,24,128]{2,1,0:T(8,128)}), f32[8,24,128]{2,1,0:T(8,128)S(1)}, u32[]{:S(2)}, u32[]{:S(2)}) async-start(f32[8,24,128]{2,1,0:T(8,128)} %shard_map.106), calls=%async_computation.3 | async-start | bytes 196608 | tf_op jit(solution)/shard_map/all_to_all | solution.py:494
  125.1 5.0 %all-to-all-done.3.part_ref = f32[8,24,128]{2,1,0:T(8,128)S(1)} async-done(((f32[8,24,128]{2,1,0:T(8,128)}), f32[8,24,128]{2,1,0:T(8,128)S(1)}, u32[]{:S(2)}, u32[]{:S(2)}) %all-to-all-start.3) | async-done | bytes 98336 | tf_op jit(solution)/shard_map/all_to_all | solution.py:494
  (56 shorter events, 18.2 us)
Async XLA Ops:
  3.8 4.9 %collective-permute-start = (f32[2,96,128]{2,1,0:T(8,128)S(1)}, f32[2,96,128]{2,1,0:T(8,128)S(1)}, u32[]{:S(2)}, u32[]{:S(2)}) collective-permute-start(f32[2,96,128]{2,1,0:T(8,128)S(1)} %get-tuple-element.23), channel_id=1, source_target_pairs={{0,16},{8,24},{16,32},{24,40},{32,48},{40,56},{48,0},{56,8},{64,80... | collective-permute-start | bytes 294920 | tf_op jit(solution)/shard_map/ppermute | solution.py:463
  10.6 35.8 %all-to-all-start = ((f32[8,384,128]{2,1,0:T(8,128)}), f32[8,384,128]{2,1,0:T(8,128)S(1)}, u32[]{:S(2)}, u32[]{:S(2)}) async-start(f32[8,384,128]{2,1,0:T(8,128)} %shard_map.96), calls=%async_computation | async-start | bytes 3145728 | tf_op jit(solution)/shard_map/all_to_all | solution.py:465
  16.1 6.2 %collective-permute-start.1 = (f32[2,96,128]{2,1,0:T(8,128)S(1)}, f32[2,96,128]{2,1,0:T(8,128)S(1)}, u32[]{:S(2)}, u32[]{:S(2)}) collective-permute-start(f32[2,96,128]{2,1,0:T(8,128)S(1)} %get-tuple-element.25), channel_id=1, source_target_pairs={{0,32},{8,40},{16,48},{24,56},{32,0},{40,8},{48,16},{56,24},{64,96... | collective-permute-start | bytes 294920 | tf_op jit(solution)/shard_map/ppermute | solution.py:463
  18.3 5.0 %collective-permute-start.2 = (f32[2,96,128]{2,1,0:T(8,128)S(1)}, f32[2,96,128]{2,1,0:T(8,128)S(1)}, u32[]{:S(2)}, u32[]{:S(2)}) collective-permute-start(f32[2,96,128]{2,1,0:T(8,128)S(1)} %get-tuple-element.26), channel_id=1, source_target_pairs={{0,48},{8,56},{16,0},{24,8},{32,16},{40,24},{48,32},{56,40},{64,11... | collective-permute-start | bytes 294920 | tf_op jit(solution)/shard_map/ppermute | solution.py:463
  23.3 46.9 %copy-start.1 = (bf16[384,256]{1,0:T(8,128)(2,1)S(1)}, bf16[384,256]{1,0:T(8,128)(2,1)}, u32[]{:S(2)}) copy-start(bf16[384,256]{1,0:T(8,128)(2,1)} %constant.106.clone.refs_12_) | copy-start | bytes 589828
  23.3 46.9 %copy-start.2 = (bf16[144,432]{1,0:T(8,128)(2,1)S(1)}, bf16[144,432]{1,0:T(8,128)(2,1)}, u32[]{:S(2)}) copy-start(bf16[144,432]{1,0:T(8,128)(2,1)} %constant.108.clone.refs_14_) | copy-start | bytes 373252
  23.3 46.9 %copy-start.4 = (bf16[80,240]{1,0:T(8,128)(2,1)S(1)}, bf16[80,240]{1,0:T(8,128)(2,1)}, u32[]{:S(2)}) copy-start(bf16[80,240]{1,0:T(8,128)(2,1)} %constant.105.clone.refs_11_) | copy-start | bytes 115204
  23.9 1.4 %collective-permute-start.3 = (f32[4,48,128]{2,1,0:T(8,128)S(1)}, f32[4,48,128]{2,1,0:T(8,128)S(1)}, u32[]{:S(2)}, u32[]{:S(2)}) collective-permute-start(f32[4,48,128]{2,1,0:T(8,128)S(1)} %get-tuple-element.28), channel_id=1, source_target_pairs={{0,8},{8,0},{16,24},{24,16},{32,40},{40,32},{48,56},{56,48},{64,72... | collective-permute-start | bytes 294920 | tf_op jit(solution)/shard_map/ppermute | solution.py:441
  25.9 9.3 %collective-permute-start.6 = (f32[4,48,128]{2,1,0:T(8,128)S(1)}, f32[4,48,128]{2,1,0:T(8,128)S(1)}, u32[]{:S(2)}, u32[]{:S(2)}) collective-permute-start(f32[4,48,128]{2,1,0:T(8,128)S(1)} %shard_map.98.z0), channel_id=1, source_target_pairs={{0,192},{8,200},{16,208},{24,216},{32,224},{40,232},{48,240},{56,2... | collective-permute-start | bytes 294920 | tf_op jit(solution)/shard_map/ppermute | solution.py:469
  31.3 14.8 %collective-permute-start.5 = (f32[4,48,128]{2,1,0:T(8,128)S(1)}, f32[4,48,128]{2,1,0:T(8,128)S(1)}, u32[]{:S(2)}, u32[]{:S(2)}) collective-permute-start(f32[4,48,128]{2,1,0:T(8,128)S(1)} %shard_map.98.z0), channel_id=1, source_target_pairs={{0,128},{8,136},{16,144},{24,152},{32,160},{40,168},{48,176},{56,1... | collective-permute-start | bytes 294920 | tf_op jit(solution)/shard_map/ppermute | solution.py:469
  32.8 13.5 %collective-permute-start.4 = (f32[4,48,128]{2,1,0:T(8,128)S(1)}, f32[4,48,128]{2,1,0:T(8,128)S(1)}, u32[]{:S(2)}, u32[]{:S(2)}) collective-permute-start(f32[4,48,128]{2,1,0:T(8,128)S(1)} %shard_map.98.z0), channel_id=1, source_target_pairs={{0,64},{8,72},{16,80},{24,88},{32,96},{40,104},{48,112},{56,120},{... | collective-permute-start | bytes 294920 | tf_op jit(solution)/shard_map/ppermute | solution.py:469
  46.3 23.9 %copy-start = (f32[8,384,128]{2,1,0:T(8,128)}, f32[8,384,128]{2,1,0:T(8,128)S(1)}, u32[]{:S(2)}) copy-start(f32[8,384,128]{2,1,0:T(8,128)S(1)} %all-to-all-done.after_ref.refs_1_) | copy-start | bytes 4718596
  58.9 5.7 %collective-permute-start.9 = (f32[8,48,128]{2,1,0:T(8,128)S(1)}, f32[8,48,128]{2,1,0:T(8,128)S(1)}, u32[]{:S(2)}, u32[]{:S(2)}) collective-permute-start(f32[8,48,128]{2,1,0:T(8,128)S(1)} %all_to_all.20.refs_2_), channel_id=1, source_target_pairs={{0,48},{8,56},{16,0},{24,8},{32,16},{40,24},{48,32},{56,40},{64,11... | collective-permute-start | bytes 589832 | tf_op jit(solution)/shard_map/ppermute | solution.py:472
  60.7 7.2 %collective-permute-start.8 = (f32[8,48,128]{2,1,0:T(8,128)S(1)}, f32[8,48,128]{2,1,0:T(8,128)S(1)}, u32[]{:S(2)}, u32[]{:S(2)}) collective-permute-start(f32[8,48,128]{2,1,0:T(8,128)S(1)} %all_to_all.20.refs_2_), channel_id=1, source_target_pairs={{0,32},{8,40},{16,48},{24,56},{32,0},{40,8},{48,16},{56,24},{64,96... | collective-permute-start | bytes 589832 | tf_op jit(solution)/shard_map/ppermute | solution.py:472
  61.9 6.9 %collective-permute-start.7 = (f32[8,48,128]{2,1,0:T(8,128)S(1)}, f32[8,48,128]{2,1,0:T(8,128)S(1)}, u32[]{:S(2)}, u32[]{:S(2)}) collective-permute-start(f32[8,48,128]{2,1,0:T(8,128)S(1)} %all_to_all.20.refs_2_), channel_id=1, source_target_pairs={{0,16},{8,24},{16,32},{24,40},{32,48},{40,56},{48,0},{56,8},{64,80... | collective-permute-start | bytes 589832 | tf_op jit(solution)/shard_map/ppermute | solution.py:472
  63.7 5.1 %collective-permute-start.10 = (f32[8,48,128]{2,1,0:T(8,128)S(1)}, f32[8,48,128]{2,1,0:T(8,128)S(1)}, u32[]{:S(2)}, u32[]{:S(2)}) collective-permute-start(f32[8,48,128]{2,1,0:T(8,128)S(1)} %all_to_all.20.refs_2_), channel_id=1, source_target_pairs={{0,8},{8,0},{16,24},{24,16},{32,40},{40,32},{48,56},{56,48},{64,72... | collective-permute-start | bytes 589832 | tf_op jit(solution)/shard_map/ppermute | solution.py:441
  64.6 4.2 %collective-permute-start.13 = (f32[8,48,128]{2,1,0:T(8,128)S(1)}, f32[8,48,128]{2,1,0:T(8,128)S(1)}, u32[]{:S(2)}, u32[]{:S(2)}) collective-permute-start(f32[8,48,128]{2,1,0:T(8,128)S(1)} %collective-permute-done.9.refs_5_), channel_id=1, source_target_pairs={{0,8},{8,0},{16,24},{24,16},{32,40},{40,32},{48,56},{56,48},{64,72... | collective-permute-start | bytes 589832 | tf_op jit(solution)/shard_map/ppermute | solution.py:441
  67.9 1.4 %collective-permute-start.12 = (f32[8,48,128]{2,1,0:T(8,128)S(1)}, f32[8,48,128]{2,1,0:T(8,128)S(1)}, u32[]{:S(2)}, u32[]{:S(2)}) collective-permute-start(f32[8,48,128]{2,1,0:T(8,128)S(1)} %collective-permute-done.8.refs_4_), channel_id=1, source_target_pairs={{0,8},{8,0},{16,24},{24,16},{32,40},{40,32},{48,56},{56,48},{64,72... | collective-permute-start | bytes 589832 | tf_op jit(solution)/shard_map/ppermute | solution.py:441
  68.8 1.4 %collective-permute-start.11 = (f32[8,48,128]{2,1,0:T(8,128)S(1)}, f32[8,48,128]{2,1,0:T(8,128)S(1)}, u32[]{:S(2)}, u32[]{:S(2)}) collective-permute-start(f32[8,48,128]{2,1,0:T(8,128)S(1)} %collective-permute-done.7.refs_3_), channel_id=1, source_target_pairs={{0,8},{8,0},{16,24},{24,16},{32,40},{40,32},{48,56},{56,48},{64,72... | collective-permute-start | bytes 589832 | tf_op jit(solution)/shard_map/ppermute | solution.py:441
  70.2 0.9 copy-start.3
  83.4 32.1 %all-to-all-start.2 = ((f32[8,384,128]{2,1,0:T(8,128)}), f32[8,384,128]{2,1,0:T(8,128)S(1)}, u32[]{:S(2)}, u32[]{:S(2)}) async-start(f32[8,384,128]{2,1,0:T(8,128)} %get-tuple-element.29), calls=%async_computation.2 | async-start | bytes 3145728 | tf_op jit(solution)/shard_map/all_to_all | solution.py:476
  87.0 1.5 %collective-permute-start.15 = (f32[4,96,128]{2,1,0:T(8,128)S(1)}, f32[4,96,128]{2,1,0:T(8,128)S(1)}, u32[]{:S(2)}, u32[]{:S(2)}) collective-permute-start(f32[4,96,128]{2,1,0:T(8,128)S(1)} %get-tuple-element.33), channel_id=1, source_target_pairs={{0,8},{8,0},{16,24},{24,16},{32,40},{40,32},{48,56},{56,48},{64,72... | collective-permute-start | bytes 589832 | tf_op jit(solution)/shard_map/ppermute | solution.py:441
  87.2 3.4 %collective-permute-start.17 = (f32[4,96,128]{2,1,0:T(8,128)S(1)}, f32[4,96,128]{2,1,0:T(8,128)S(1)}, u32[]{:S(2)}, u32[]{:S(2)}) collective-permute-start(f32[4,96,128]{2,1,0:T(8,128)S(1)} %get-tuple-element.35), channel_id=1, source_target_pairs={{0,8},{8,0},{16,24},{24,16},{32,40},{40,32},{48,56},{56,48},{64,72... | collective-permute-start | bytes 589832 | tf_op jit(solution)/shard_map/ppermute | solution.py:441
  87.6 7.0 %collective-permute-start.19 = (f32[4,96,128]{2,1,0:T(8,128)S(1)}, f32[4,96,128]{2,1,0:T(8,128)S(1)}, u32[]{:S(2)}, u32[]{:S(2)}) collective-permute-start(f32[4,96,128]{2,1,0:T(8,128)S(1)} %get-tuple-element.37), channel_id=1, source_target_pairs={{0,8},{8,0},{16,24},{24,16},{32,40},{40,32},{48,56},{56,48},{64,72... | collective-permute-start | bytes 589832 | tf_op jit(solution)/shard_map/ppermute | solution.py:441
  87.7 7.6 %collective-permute-start.14 = (f32[4,96,128]{2,1,0:T(8,128)S(1)}, f32[4,96,128]{2,1,0:T(8,128)S(1)}, u32[]{:S(2)}, u32[]{:S(2)}) collective-permute-start(f32[4,96,128]{2,1,0:T(8,128)S(1)} %get-tuple-element.31), channel_id=1, source_target_pairs={{0,8},{8,0},{16,24},{24,16},{32,40},{40,32},{48,56},{56,48},{64,72... | collective-permute-start | bytes 589832 | tf_op jit(solution)/shard_map/ppermute | solution.py:441
  89.1 8.5 %collective-permute-start.16 = (f32[4,96,128]{2,1,0:T(8,128)S(1)}, f32[4,96,128]{2,1,0:T(8,128)S(1)}, u32[]{:S(2)}, u32[]{:S(2)}) collective-permute-start(f32[4,96,128]{2,1,0:T(8,128)S(1)} %shard_map.102), channel_id=1, source_target_pairs={{0,16},{8,24},{16,32},{24,40},{32,48},{40,56},{48,0},{56,8},{64,80... | collective-permute-start | bytes 589832 | tf_op jit(solution)/shard_map/ppermute | solution.py:481
  91.2 9.4 %collective-permute-start.18 = (f32[4,96,128]{2,1,0:T(8,128)S(1)}, f32[4,96,128]{2,1,0:T(8,128)S(1)}, u32[]{:S(2)}, u32[]{:S(2)}) collective-permute-start(f32[4,96,128]{2,1,0:T(8,128)S(1)} %shard_map.103), channel_id=1, source_target_pairs={{0,32},{8,40},{16,48},{24,56},{32,0},{40,8},{48,16},{56,24},{64,96... | collective-permute-start | bytes 589832 | tf_op jit(solution)/shard_map/ppermute | solution.py:481
  95.2 8.6 %collective-permute-start.20 = (f32[4,96,128]{2,1,0:T(8,128)S(1)}, f32[4,96,128]{2,1,0:T(8,128)S(1)}, u32[]{:S(2)}, u32[]{:S(2)}) collective-permute-start(f32[4,96,128]{2,1,0:T(8,128)S(1)} %shard_map.104), channel_id=1, source_target_pairs={{0,48},{8,56},{16,0},{24,8},{32,16},{40,24},{48,32},{56,40},{64,11... | collective-permute-start | bytes 589832 | tf_op jit(solution)/shard_map/ppermute | solution.py:481
  104.3 6.9 %collective-permute-start.21 = (f32[96,128]{1,0:T(8,128)S(1)}, f32[96,128]{1,0:T(8,128)S(1)}, u32[]{:S(2)}, u32[]{:S(2)}) collective-permute-start(f32[96,128]{1,0:T(8,128)S(1)} %get-tuple-element.39), channel_id=1, source_target_pairs={{0,64},{8,72},{16,80},{24,88},{32,96},{40,104},{48,112},{56,120},{... | collective-permute-start | bytes 147464 | tf_op jit(solution)/shard_map/ppermute | solution.py:483
  106.9 8.0 %collective-permute-start.22 = (f32[96,128]{1,0:T(8,128)S(1)}, f32[96,128]{1,0:T(8,128)S(1)}, u32[]{:S(2)}, u32[]{:S(2)}) collective-permute-start(f32[96,128]{1,0:T(8,128)S(1)} %get-tuple-element.40), channel_id=1, source_target_pairs={{0,128},{8,136},{16,144},{24,152},{32,160},{40,168},{48,176},{56,1... | collective-permute-start | bytes 147464 | tf_op jit(solution)/shard_map/ppermute | solution.py:483
  108.4 7.0 %collective-permute-start.23 = (f32[96,128]{1,0:T(8,128)S(1)}, f32[96,128]{1,0:T(8,128)S(1)}, u32[]{:S(2)}, u32[]{:S(2)}) collective-permute-start(f32[96,128]{1,0:T(8,128)S(1)} %get-tuple-element.41), channel_id=1, source_target_pairs={{0,192},{8,200},{16,208},{24,216},{32,224},{40,232},{48,240},{56,2... | collective-permute-start | bytes 147464 | tf_op jit(solution)/shard_map/ppermute | solution.py:483
  116.7 13.4 %all-to-all-start.3 = ((f32[8,24,128]{2,1,0:T(8,128)}), f32[8,24,128]{2,1,0:T(8,128)S(1)}, u32[]{:S(2)}, u32[]{:S(2)}) async-start(f32[8,24,128]{2,1,0:T(8,128)} %shard_map.106), calls=%async_computation.3 | async-start | bytes 196608 | tf_op jit(solution)/shard_map/all_to_all | solution.py:494
  (2 other events, 1.5 us)

commit v4 on v3

--- a/solution.py
+++ b/solution.py
@@ -30,7 +30,6 @@
 PART = 24
 F32 = jnp.float32
 BF16 = jnp.bfloat16
-PARAMS = pltpu.CompilerParams(vmem_limit_bytes=48 * 1024 * 1024)
 
 
 def split_np(table):
@@ -105,25 +104,46 @@
     return jax.ShapeDtypeStruct(dims, F32)
 
 
-def call(kernel, out_shape, info, *arrays, after=(), scratch=(), flops=0):
+def call(kernel, out_shape, owner, *arrays, after=(), scratch=(), flops=0, vmem=8):
     specs = [pl.BlockSpec(memory_space=pltpu.SMEM)]
     specs += [pl.BlockSpec(memory_space=pltpu.VMEM) for _ in arrays]
     specs += [pl.BlockSpec(memory_space=pl.ANY) for _ in after]
     size = sum(a.size for a in arrays) * 4
+
+    def body(owner_ref, *refs):
+        kernel(scalars(owner_ref), *refs)
+
     return pl.pallas_call(
-        kernel,
+        body,
         in_specs=specs,
         out_shape=out_shape,
         scratch_shapes=list(scratch),
-        compiler_params=PARAMS,
+        compiler_params=pltpu.CompilerParams(vmem_limit_bytes=vmem * 2**20),
         cost_estimate=pl.CostEstimate(flops=flops, bytes_accessed=2 * size, transcendentals=0),
-    )(info, *arrays, *after)
-
-
-MY_X, MY_C, MY_Z, X_STEP, C_OWN, Z_STEP = 0, 1, 2, 3, 5, 7
-
-
-def pack_kernel(info, orb_ref, out_ref, *quarters):
+    )(owner, *arrays, *after)
+
+
+MY_X, MY_C, MY_Z, X_STEP, C_OWN, Z_STEP, MY_Y, MY_PAIR = 0, 1, 2, 3, 5, 7, 9, 10
+
+
+def divide_grid():
+    me = lax.axis_index("grid")
+    return me // 2, lax.rem(me, 2)
+
+
+def scalars(owner):
+    me = lax.axis_index("band")
+    x, c, z = lax.rem(me // 2, 4), lax.rem(me, 2), me // 8
+    values = [x, c, z, 0, 0, 0, 0, 0, 0, *divide_grid()]
+    for step in range(2):
+        band = jnp.clip(owner[step], 0, BAND - 1)
+        values[X_STEP + step] = lax.rem(x + 4 - lax.rem(band // 2, 4), 4)
+        values[C_OWN + step] = (c == lax.rem(band, 2)).astype(jnp.int32)
+        values[Z_STEP + step] = lax.rem(z + 4 - band // 8, 4)
+    return values
+
+
+def pack_kernel(info, orb_ref, stay_ref, cross_ref, q0, q1, q2, q3, out_ref):
     for o in range(2):
         out_ref[o, TAIL:ROWS, :] = jnp.zeros((ROWS - TAIL, LANES), F32)
         for t in range(TILES):
@@ -133,15 +153,17 @@
             cols = slice(t * LANES, t * LANES + wide)
             out_ref[o, 8 * t : 8 * t + 8, :wide] = orb_ref[o, 0:8, cols]
             out_ref[o, TAIL + t : TAIL + t + 1, :wide] = orb_ref[o, 8:9, cols]
-    for d in range(4):
+    stay_ref[...] = out_ref[info[MY_PAIR]]
+    cross_ref[...] = out_ref[1 - info[MY_PAIR]]
+    for d, quarter in enumerate((q0, q1, q2, q3)):
         first = pl.multiple_of(QUARTER * lax.rem(info[MY_X] + d, 4), QUARTER)
         for o in range(2):
-            quarters[d][o] = out_ref[o, pl.ds(first, QUARTER), :]
-
-
-def spread_kernel(info, packed_ref, after_ref, out_ref):
-    for g in range(8):
-        out_ref[g] = packed_ref[g // 4]
+            quarter[o] = out_ref[o, pl.ds(first, QUARTER), :]
+
+
+def join_kernel(info, stay_ref, got_ref, out_ref):
+    out_ref[0] = stay_ref[...]
+    out_ref[1] = got_ref[...]
 
 
 def pick_x_kernel(info, q0, q1, q2, q3, keep_ref, give_ref):
@@ -158,14 +180,18 @@
         out_ref[b] = jnp.where(info[C_OWN + b // 2] == 1, keep_ref[b], got_ref[b])
 
 
-def pick_z_kernel(info, z0, z1, z2, z3, after_ref, out_ref):
+def pick_z_kernel(info, z0, z1, z2, z3, out_ref):
     for b in range(4):
         value = pick(info[Z_STEP + b // 2], [z[b] for z in (z0, z1, z2, z3)])
-        out_ref[b] = value
-        out_ref[4 + b] = value
-
-
-def whole_block(r, info, scale):
+        out_ref[2 * b] = value
+        out_ref[2 * b + 1] = value
+
+
+def whole(r, info, scale):
+    for d in range(4):
+        y = lax.rem(info[MY_Y] + 4 - d, 4)
+        r.orb[2 * y + info[MY_PAIR]] = r.slabs[d][0]
+        r.orb[2 * y + 1 - info[MY_PAIR]] = r.slabs[d][1]
     for d in range(4):
         quarter = QUARTER * lax.rem(info[MY_X] + 4 - d, 4)
         for ref, half in ((r.mine[d], info[MY_C]), (r.other[d], 1 - info[MY_C])):
@@ -295,6 +321,10 @@
                 r.wide[8 * s : 8 * s + 8, one] = piece * r.orb[s, rows, :]
             r.wide[64:72, one] = part[64:72] * r.orb_tail[:, one]
     r.wide[:, TILES * LANES :] = jnp.zeros((XR, 2 * LANES), F32)
+    for d in range(4):
+        y = lax.rem(info[MY_Y] + d, 4)
+        r.sent[d][0] = r.own[2 * y + info[MY_PAIR]]
+        r.sent[d][1] = r.own[2 * y + 1 - info[MY_PAIR]]
 
 
 def share_out(r, info, scale):
@@ -328,7 +358,7 @@
 
 
 STAGES = (
-    whole_block,
+    whole,
     density,
     forward_x,
     to_columns,
@@ -343,28 +373,31 @@
 
 def field_kernel(scale, info, *refs):
     tables = ("fx", "ix", "zt", "fy", "iy", "sq")
-    scratch = ("blk", "wide", "orb_tail", "blk_tail", "col", "re", "im", "cut")
-    r = types.SimpleNamespace(orb=refs[0], mine=refs[1:5], other=refs[5:9], own=refs[15])
-    r.keep, r.give = refs[16:20], refs[20:24]
-    vars(r).update(zip(tables, refs[9:15]))
-    vars(r).update(zip(scratch, refs[24:]))
+    scratch = ("orb", "blk", "own", "wide", "orb_tail", "blk_tail", "col", "re", "im", "cut")
+    r = types.SimpleNamespace(slabs=refs[:4], mine=refs[4:8], other=refs[8:12])
+    vars(r).update(zip(tables, refs[12:18]))
+    r.sent, r.keep, r.give = refs[18:22], refs[22:26], refs[26:30]
+    vars(r).update(zip(scratch, refs[30:]))
     for stage in STAGES:
         stage(r, info, scale)
 
 
-def fields(info, orbital, pieces, scale):
+def fields(block_owner, slabs, pieces, scale):
     def body(*refs):
         field_kernel(scale, *refs)
 
+    whole_slabs = pltpu.VMEM((8, ROWS, LANES), F32)
     return call(
         body,
-        [shape(8, ROWS, LANES)] + [shape(4, PACK, LANES)] * 8,
-        info,
-        orbital,
+        [shape(2, ROWS, LANES)] * 4 + [shape(4, PACK, LANES)] * 8,
+        block_owner,
+        *slabs,
         *pieces,
         *[jnp.asarray(t) for t in tables()],
         scratch=[
-            pltpu.VMEM((8, ROWS, LANES), F32),
+            whole_slabs,
+            whole_slabs,
+            whole_slabs,
             pltpu.VMEM((XR, (TILES + 2) * LANES), F32),
             pltpu.VMEM((8, TILES * LANES), F32),
             pltpu.VMEM((8, TILES * LANES), F32),
@@ -374,6 +407,7 @@
             pltpu.VMEM((8, 4, PACK, LANES), F32),
         ],
         flops=10**10,
+        vmem=36,
     )
 
 
@@ -386,7 +420,7 @@
         outs[z][...] = k_ref[z] + g_ref[z] + r1[z] + r2[z] + r3[z]
 
 
-def add_z_kernel(info, s_ref, r1, r2, r3, after_ref, out_ref, sum_ref):
+def add_z_kernel(info, s_ref, r1, r2, r3, out_ref, sum_ref):
     sum_ref[...] = s_ref[...] + r1[...] + r2[...] + r3[...]
     out_ref[...] = jnp.zeros((8, PART, LANES), F32)
 
@@ -405,7 +439,7 @@
 
 def share_kernel(info, part_ref, out_ref):
     for b in range(4):
-        total = part_ref[b] + part_ref[4 + b]
+        total = part_ref[2 * b] + part_ref[2 * b + 1]
         at = (b // 2, b % 2)
         out_ref[at[0], at[1], 0:8, :LANES] = total[0:8]
         out_ref[at[0], at[1], 0:8, LANES:SHARE] = total[8:16, :REST]
@@ -413,20 +447,18 @@
         out_ref[at[0], at[1], 8:9, LANES:SHARE] = total[17:18, :REST]
 
 
-def own_kernel(info, part_ref, out_ref):
-    for i in range(2):
-        for t in range(TILES + 1):
-            rows = slice(TAIL, ROWS) if t == TILES else slice(8 * t, 8 * t + 8)
-            total = part_ref[4 * i, rows, :]
-            for b in range(1, 4):
-                total = total + part_ref[4 * i + b, rows, :]
-            if t == TILES:
-                for u in range(TILES):
-                    wide = min(LANES, PLANE - u * LANES)
-                    out_ref[i, 8:9, u * LANES : u * LANES + wide] = total[u : u + 1, :wide]
-            else:
-                wide = min(LANES, PLANE - t * LANES)
-                out_ref[i, 0:8, t * LANES : t * LANES + wide] = total[:, :wide]
+def add_y_kernel(info, s_ref, r1, r2, r3, stay_ref, cross_ref):
+    for j, ref in enumerate((stay_ref, cross_ref)):
+        ref[...] = s_ref[j] + r1[j] + r2[j] + r3[j]
+
+
+def own_kernel(info, stay_ref, got_ref, out_ref):
+    for ref, i in ((stay_ref, info[MY_PAIR]), (got_ref, 1 - info[MY_PAIR])):
+        for t in range(TILES):
+            wide = min(LANES, PLANE - t * LANES)
+            cols = slice(t * LANES, t * LANES + wide)
+            out_ref[i, 0:8, cols] = ref[8 * t : 8 * t + 8, :wide]
+            out_ref[i, 8:9, cols] = ref[TAIL + t : TAIL + t + 1, :wide]
 
 
 def shift_x(d):
@@ -437,63 +469,65 @@
     return [(i, (i + 8 * d) % BAND) for i in range(BAND)]
 
 
+def shift_y(d):
+    return [(i, (i + 2 * d) % 8) for i in range(8)]
+
+
+def other_slab(x):
+    return lax.ppermute(x, "grid", [(i, i ^ 1) for i in range(8)])
+
+
 def other_core(x):
     return lax.ppermute(x, "band", [(i, i ^ 1) for i in range(BAND)])
 
 
-def scalars(block_owner):
-    me = lax.axis_index("band")
-    owner = jnp.clip(block_owner, 0, BAND - 1)
-    x, c, z = me // 2 % 4, me % 2, me // 8
-    parts = [
-        jnp.stack([x, c, z]),
-        (x - owner // 2 % 4) % 4,
-        (c == owner % 2).astype(jnp.int32),
-        (z - owner // 8) % 4,
-    ]
-    return jnp.concatenate([p.astype(jnp.int32) for p in parts])
-
-
 def on_device(orbitals, block_owner):
     scale = math.sqrt(GRID**3 / (2 * BAND))
-    info = scalars(block_owner)
-    packed, *quarters = call(
-        pack_kernel, [shape(2, ROWS, LANES)] + [shape(2, QUARTER, LANES)] * 4, info, orbitals
+    slab = shape(ROWS, LANES)
+    stay, cross, *quarters = call(
+        pack_kernel,
+        [slab, slab] + [shape(2, QUARTER, LANES)] * 4,
+        block_owner,
+        orbitals,
+        scratch=[pltpu.VMEM((2, ROWS, LANES), F32)],
     )
+    pair = call(join_kernel, shape(2, ROWS, LANES), block_owner, stay, other_slab(cross))
+    slabs = [pair] + [lax.ppermute(pair, "grid", shift_y(d)) for d in (1, 2, 3)]
+
     quarters = quarters[:1] + [lax.ppermute(quarters[d], "band", shift_x(d)) for d in (1, 2, 3)]
-    spread = call(spread_kernel, shape(8, ROWS, LANES), info, packed, after=quarters[1:2])
-    orbital = lax.all_to_all(spread, "grid", 0, 0)
     half = shape(4, PIECE, LANES)
-    keep, give = call(pick_x_kernel, [half, half], info, *quarters)
-    mine = call(pick_core_kernel, half, info, keep, other_core(give))
+    keep, give = call(pick_x_kernel, [half, half], block_owner, *quarters)
+    mine = call(pick_core_kernel, half, block_owner, keep, other_core(give))
     along = [mine] + [lax.ppermute(mine, "band", shift_z(d)) for d in (1, 2, 3)]
-    mine = call(pick_z_kernel, shape(8, PIECE, LANES), info, *along, after=[orbital])
+    mine = call(pick_z_kernel, shape(8, PIECE, LANES), block_owner, *along)
     piece = lax.all_to_all(mine, "grid", 0, 0)
     pieces = [piece] + [lax.ppermute(piece, "band", shift_x(d)) for d in (1, 2, 3)]
     pieces = pieces + [other_core(p) for p in pieces]
 
-    own, *shares = fields(info, orbital, pieces, scale)
-    own = lax.all_to_all(own, "grid", 0, 0)
+    outs = fields(block_owner, slabs, pieces, scale)
+    sent, shares = list(outs[:4]), outs[4:]
+    sent = sent[:1] + [lax.ppermute(sent[d], "grid", shift_y(d)) for d in (1, 2, 3)]
+    stay, cross = call(add_y_kernel, [slab, slab], block_owner, *sent)
+    own = other_slab(cross)
     kept, got = shares[:4], [other_core(g) for g in shares[4:]]
     part = shape(4, PACK, LANES)
     moved = []
     for d in (1, 2, 3):
-        moved.append(lax.ppermute(call(add_kernel, part, info, kept[d], got[d]), "band", shift_x(d)))
-    sums = call(add_x_kernel, [shape(PACK, LANES)] * 4, info, kept[0], got[0], *moved)
+        moved.append(lax.ppermute(call(add_kernel, part, block_owner, kept[d], got[d]), "band", shift_x(d)))
+    sums = call(add_x_kernel, [shape(PACK, LANES)] * 4, block_owner, kept[0], got[0], *moved)
     moved = [lax.ppermute(sums[d], "band", shift_z(d)) for d in (1, 2, 3)]
     slabs = call(
         add_z_kernel,
         shape(8, PART, LANES),
-        info,
+        block_owner,
         sums[0],
         *moved,
-        after=[own],
         scratch=[pltpu.VMEM((PACK, LANES), F32)],
     )
     block_field = call(
-        share_kernel, shape(2, 2, SLAB, SHARE), info, lax.all_to_all(slabs, "grid", 0, 0)
+        share_kernel, shape(2, 2, SLAB, SHARE), block_owner, lax.all_to_all(slabs, "grid", 0, 0)
     )
-    field = call(own_kernel, shape(2, SLAB, PLANE), info, own)
+    field = call(own_kernel, shape(2, SLAB, PLANE), block_owner, stay, own)
     return field, block_field
 
 

time: 133 us -> 118 us (0.89)
  blocking collectives: 12 us -> 0 us
  starting transfers between devices: 48.1 us -> 58.5 us
  waiting for transfers between devices: 44.3 us -> 37.1 us
  local copies, waits for them, and re-layouts: 5.17 us -> 2.66 us
  Pallas kernels: 19.5 us -> 18 us
  other arithmetic: 1.35 us -> 0 us
    ppermute x3 -> x11, starting transfers between devices: 5.03 us -> 20.6 us  [the longest x3 7.06 us: on_device(): slabs = [pair] + [lax.ppermute(pair, 'grid', shift_y(d)) for d in (1, 2, 3)]]
    all_to_all x1 -> x0, blocking collectives: 12 us -> none  [on_device(): piece = lax.all_to_all(mine, 'grid', 0, 0)]
    ppermute x3 -> x11, waiting for transfers between devices: 8.46 us -> 15.9 us  [the longest x3 8.57 us: on_device(): lax.ppermute(call(add_kernel, part, block_owner, kept[d], got[d]), 'band'...]
    ppermute x3, waiting for transfers between devices: 11.2 us -> 4.72 us  [on_device(): along = [mine] + [lax.ppermute(mine, 'band', shift_z(d)) for d in (1, 2, 3)]]
    all_to_all x2 -> x1, starting transfers between devices: 9.15 us -> 4.6 us  [on_device(): piece = lax.all_to_all(mine, 'grid', 0, 0)]
    ppermute x3, waiting for transfers between devices: 6.99 us -> 2.69 us  [on_device(): lax.ppermute(quarters[d], 'band', shift_x(d))]
    all_to_all x2 -> x1, waiting for transfers between devices: 0.01 us -> 3.66 us  [on_device(): piece = lax.all_to_all(mine, 'grid', 0, 0)]
    ppermute x3, waiting for transfers between devices: 5.08 us -> 1.88 us  [on_device(): lax.ppermute(piece, 'band', shift_x(d))]
  transfers between devices with their start and end apart: 27 -> 34, of which waited for: 19 -> 15; matrix products, arithmetic and copies ran while one was open for 1% -> 1% of each run, Pallas kernels for 3% -> 7%
where the time goes in v4:
time: 118 us; the launch traced here: 117 us
  starting transfers between devices  58.5 us (50%)
  waiting for transfers between devices  37.1 us (31%)
  Pallas kernels  18 us (15%)
  local copies, waits for them, and re-layouts  2.66 us (2%)
    pallas_call x14, Pallas kernels, call(): pl.pallas_call(body, in_specs=specs, out_shape=out_shape, scratch_shapes=...  18 us
    ppermute x3, starting transfers between devices, on_device(): along = [mine] + [lax.ppermute(mine, 'band', shift_z(d)) for d in (1, 2, 3)]  9.51 us
    ppermute x3, waiting for transfers between devices, on_device(): lax.ppermute(call(add_kernel, part, block_owner, kept[d], got[d]), 'band'...  8.57 us
    ppermute x3, starting transfers between devices, on_device(): moved = [lax.ppermute(sums[d], 'band', shift_z(d)) for d in (1, 2, 3)]  7.59 us
    ppermute x3, waiting for transfers between devices, on_device(): slabs = [pair] + [lax.ppermute(pair, 'grid', shift_y(d)) for d in (1, 2, 3)]  7.31 us
    ppermute x3, starting transfers between devices, on_device(): slabs = [pair] + [lax.ppermute(pair, 'grid', shift_y(d)) for d in (1, 2, 3)]  7.06 us
    ppermute x3, starting transfers between devices, on_device(): lax.ppermute(sent[d], 'grid', shift_y(d))  5.52 us
    ppermute x3, starting transfers between devices, on_device(): lax.ppermute(call(add_kernel, part, block_owner, kept[d], got[d]), 'band'...  5.03 us
  transfers between devices with their start and end apart: 34, of which 15 were waited for; matrix products, arithmetic and copies ran while one was open for 1% of the time, Pallas kernels for 7%

profile of v4, /device:TPU:2, one launch (start us, length us, event | category | flops | bytes accessed | tf_op | source)
XLA Modules:
  0.0 117.2 jit_solution(9614657824352731299)
XLA Ops:
  2.4 1.6 %collective-permute-start.4 = (f32[2,96,128]{2,1,0:T(8,128)S(1)}, f32[2,96,128]{2,1,0:T(8,128)S(1)}, u32[]{:S(2)}, u32[]{:S(2)}) collective-permute-start(f32[2,96,128]{2,1,0:T(8,128)S(1)} %get-tuple-element.31), channel_id=1, source_target_pairs={{0,16},{8,24},{16,32},{24,40},{32,48},{40,56},{48,0},{56,8},{64,80... | collective-permute-start | bytes 294920 | tf_op jit(solution)/shard_map/ppermute | solution.py:497
  3.9 2.8 %collective-permute-start.5 = (f32[2,96,128]{2,1,0:T(8,128)S(1)}, f32[2,96,128]{2,1,0:T(8,128)S(1)}, u32[]{:S(2)}, u32[]{:S(2)}) collective-permute-start(f32[2,96,128]{2,1,0:T(8,128)S(1)} %get-tuple-element.32), channel_id=1, source_target_pairs={{0,32},{8,40},{16,48},{24,56},{32,0},{40,8},{48,16},{56,24},{64,96... | collective-permute-start | bytes 294920 | tf_op jit(solution)/shard_map/ppermute | solution.py:497
  7.2 1.9 %collective-permute-start = (f32[384,128]{1,0:T(8,128)S(1)}, f32[384,128]{1,0:T(8,128)S(1)}, u32[]{:S(2)}, u32[]{:S(2)}) collective-permute-start(f32[384,128]{1,0:T(8,128)S(1)} %get-tuple-element.29), channel_id=1, source_target_pairs={{0,1},{1,0},{2,3},{3,2},{4,5},{5,4},{6,7},{7,6},{8,9},{9,8},{10,11... | collective-permute-start | bytes 589832 | tf_op jit(solution)/shard_map/ppermute | solution.py:477
  9.1 1.7 %collective-permute-done.5.refs_2_ = f32[2,96,128]{2,1,0:T(8,128)S(1)} collective-permute-done((f32[2,96,128]{2,1,0:T(8,128)S(1)}, f32[2,96,128]{2,1,0:T(8,128)S(1)}, u32[]{:S(2)}, u32[]{:S(2)}) %collective-permute-start.5) | collective-permute-done | bytes 98336 | tf_op jit(solution)/shard_map/ppermute | solution.py:497
  12.5 1.3 %collective-permute-done.7.refs_1_ = f32[4,48,128]{2,1,0:T(8,128)S(1)} collective-permute-done((f32[4,48,128]{2,1,0:T(8,128)S(1)}, f32[4,48,128]{2,1,0:T(8,128)S(1)}, u32[]{:S(2)}, u32[]{:S(2)}) %collective-permute-start.7) | collective-permute-done | bytes 98336 | tf_op jit(solution)/shard_map/ppermute | solution.py:481
  14.4 5.7 %collective-permute-start.10 = (f32[4,48,128]{2,1,0:T(8,128)S(1)}, f32[4,48,128]{2,1,0:T(8,128)S(1)}, u32[]{:S(2)}, u32[]{:S(2)}) collective-permute-start(f32[4,48,128]{2,1,0:T(8,128)S(1)} %shard_map.98.refs_0_), channel_id=1, source_target_pairs={{0,192},{8,200},{16,208},{24,216},{32,224},{40,232},{48,240},{56,2... | collective-permute-start | bytes 294920 | tf_op jit(solution)/shard_map/ppermute | solution.py:501
  21.1 2.8 %collective-permute-start.8 = (f32[4,48,128]{2,1,0:T(8,128)S(1)}, f32[4,48,128]{2,1,0:T(8,128)S(1)}, u32[]{:S(2)}, u32[]{:S(2)}) collective-permute-start(f32[4,48,128]{2,1,0:T(8,128)S(1)} %shard_map.98.refs_0_), channel_id=1, source_target_pairs={{0,64},{8,72},{16,80},{24,88},{32,96},{40,104},{48,112},{56,120},{... | collective-permute-start | bytes 294920 | tf_op jit(solution)/shard_map/ppermute | solution.py:501
  24.5 3.1 %collective-permute-start.3 = (f32[2,384,128]{2,1,0:T(8,128)S(1)}, f32[2,384,128]{2,1,0:T(8,128)S(1)}, u32[]{:S(2)}, u32[]{:S(2)}) collective-permute-start(f32[2,384,128]{2,1,0:T(8,128)S(1)} %shard_map.96.refs_0_), channel_id=1, source_target_pairs={{0,6},{1,7},{2,0},{3,1},{4,2},{5,3},{6,4},{7,5},{8,14},{9,15},{10,... | collective-permute-start | bytes 1179656 | tf_op jit(solution)/shard_map/ppermute | solution.py:495
  27.6 1.2 %collective-permute-done.10.refs_3_ = f32[4,48,128]{2,1,0:T(8,128)S(1)} collective-permute-done((f32[4,48,128]{2,1,0:T(8,128)S(1)}, f32[4,48,128]{2,1,0:T(8,128)S(1)}, u32[]{:S(2)}, u32[]{:S(2)}) %collective-permute-start.10) | collective-permute-done | bytes 98336 | tf_op jit(solution)/shard_map/ppermute | solution.py:501
  28.8 3.5 %collective-permute-done.9.refs_2_ = f32[4,48,128]{2,1,0:T(8,128)S(1)} collective-permute-done((f32[4,48,128]{2,1,0:T(8,128)S(1)}, f32[4,48,128]{2,1,0:T(8,128)S(1)}, u32[]{:S(2)}, u32[]{:S(2)}) %collective-permute-start.9) | collective-permute-done | bytes 98336 | tf_op jit(solution)/shard_map/ppermute | solution.py:501
  32.3 1.3 %shard_map.99 = f32[8,48,128]{2,1,0:T(8,128)} custom-call(s32[2]{0:T(128)S(1)} %copy-done, f32[4,48,128]{2,1,0:T(8,128)S(1)} %shard_map.98.refs_0_, f32[4,48,128]{2,1,0:T(8,128)S(1)} %collective-permute-done.8.refs_1_, f32[4,48,128]{2,1,0:T(8,128)S(1)} %collective-permute-done.9.refs_2_, f32[4,48,128]{2,1,0:T(8,128)S(1)} %collective-permute-done.10.refs_3_), custom_call_target="tpu_custom_call" | custom-call | bytes 786432 | tf_op jit(solution)/shard_map/pallas_call | solution.py:116
  33.6 4.6 %all-to-all-start = ((f32[8,48,128]{2,1,0:T(8,128)}), f32[8,48,128]{2,1,0:T(8,128)S(1)}, u32[]{:S(2)}, u32[]{:S(2)}) async-start(f32[8,48,128]{2,1,0:T(8,128)} %shard_map.99), calls=%async_computation | async-start | bytes 393216 | tf_op jit(solution)/shard_map/all_to_all | solution.py:503
  38.2 3.5 %collective-permute-start.2 = (f32[2,384,128]{2,1,0:T(8,128)S(1)}, f32[2,384,128]{2,1,0:T(8,128)S(1)}, u32[]{:S(2)}, u32[]{:S(2)}) collective-permute-start(f32[2,384,128]{2,1,0:T(8,128)S(1)} %shard_map.96.refs_0_), channel_id=1, source_target_pairs={{0,4},{1,5},{2,6},{3,7},{4,0},{5,1},{6,2},{7,3},{8,12},{9,13},{10,... | collective-permute-start | bytes 1179656 | tf_op jit(solution)/shard_map/ppermute | solution.py:495
  41.7 3.7 %all-to-all-done.refs_4_ = f32[8,48,128]{2,1,0:T(8,128)S(1)} async-done(((f32[8,48,128]{2,1,0:T(8,128)}), f32[8,48,128]{2,1,0:T(8,128)S(1)}, u32[]{:S(2)}, u32[]{:S(2)}) %all-to-all-start) | async-done | bytes 196640 | tf_op jit(solution)/shard_map/all_to_all | solution.py:503
  46.5 2.1 %collective-permute-start.12 = (f32[8,48,128]{2,1,0:T(8,128)S(1)}, f32[8,48,128]{2,1,0:T(8,128)S(1)}, u32[]{:S(2)}, u32[]{:S(2)}) collective-permute-start(f32[8,48,128]{2,1,0:T(8,128)S(1)} %all-to-all-done.refs_4_), channel_id=1, source_target_pairs={{0,32},{8,40},{16,48},{24,56},{32,0},{40,8},{48,16},{56,24},{64,96... | collective-permute-start | bytes 589832 | tf_op jit(solution)/shard_map/ppermute | solution.py:504
  48.5 2.1 %collective-permute-start.11 = (f32[8,48,128]{2,1,0:T(8,128)S(1)}, f32[8,48,128]{2,1,0:T(8,128)S(1)}, u32[]{:S(2)}, u32[]{:S(2)}) collective-permute-start(f32[8,48,128]{2,1,0:T(8,128)S(1)} %all-to-all-done.refs_4_), channel_id=1, source_target_pairs={{0,16},{8,24},{16,32},{24,40},{32,48},{40,56},{48,0},{56,8},{64,80... | collective-permute-start | bytes 589832 | tf_op jit(solution)/shard_map/ppermute | solution.py:504
  50.6 2.9 %collective-permute-done.2.refs_2_ = f32[2,384,128]{2,1,0:T(8,128)S(1)} collective-permute-done((f32[2,384,128]{2,1,0:T(8,128)S(1)}, f32[2,384,128]{2,1,0:T(8,128)S(1)}, u32[]{:S(2)}, u32[]{:S(2)}) %collective-permute-start.2) | collective-permute-done | bytes 393248 | tf_op jit(solution)/shard_map/ppermute | solution.py:495
  54.8 1.1 collective-permute-done.11.refs_5_
  55.9 4.4 %collective-permute-done.1.refs_1_ = f32[2,384,128]{2,1,0:T(8,128)S(1)} collective-permute-done((f32[2,384,128]{2,1,0:T(8,128)S(1)}, f32[2,384,128]{2,1,0:T(8,128)S(1)}, u32[]{:S(2)}, u32[]{:S(2)}) %collective-permute-start.1) | collective-permute-done | bytes 393248 | tf_op jit(solution)/shard_map/ppermute | solution.py:495
  60.4 9.1 %shard_map.100 = (f32[2,384,128]{2,1,0:T(8,128)S(1)}, f32[2,384,128]{2,1,0:T(8,128)S(1)}, f32[2,384,128]{2,1,0:T(8,128)S(1)}, f32[2,384,128]{2,1,0:T(8,128)S(1)}...) custom-call(s32[2]{0:T(128)S(1)} %copy-done, ...), custom_call_target="tpu_custom_call" | custom-call | flops 10000000000 | bytes 8454144 | tf_op jit(solution)/shard_map/pallas_call | solution.py:116
  71.6 1.3 %collective-permute-start.24 = (f32[4,96,128]{2,1,0:T(8,128)S(1)}, f32[4,96,128]{2,1,0:T(8,128)S(1)}, u32[]{:S(2)}, u32[]{:S(2)}) collective-permute-start(f32[4,96,128]{2,1,0:T(8,128)S(1)} %shard_map.103), channel_id=1, source_target_pairs={{0,16},{8,24},{16,32},{24,40},{32,48},{40,56},{48,0},{56,8},{64,80... | collective-permute-start | bytes 589832 | tf_op jit(solution)/shard_map/ppermute | solution.py:516
  73.0 2.8 %collective-permute-start.18 = (f32[2,384,128]{2,1,0:T(8,128)S(1)}, f32[2,384,128]{2,1,0:T(8,128)S(1)}, u32[]{:S(2)}, u32[]{:S(2)}) collective-permute-start(f32[2,384,128]{2,1,0:T(8,128)S(1)} %get-tuple-element.37), channel_id=1, source_target_pairs={{0,2},{1,3},{2,4},{3,5},{4,6},{5,7},{6,0},{7,1},{8,10},{9,11},{10,... | collective-permute-start | bytes 1179656 | tf_op jit(solution)/shard_map/ppermute | solution.py:509
  75.8 2.6 %collective-permute-start.20 = (f32[2,384,128]{2,1,0:T(8,128)S(1)}, f32[2,384,128]{2,1,0:T(8,128)S(1)}, u32[]{:S(2)}, u32[]{:S(2)}) collective-permute-start(f32[2,384,128]{2,1,0:T(8,128)S(1)} %get-tuple-element.39), channel_id=1, source_target_pairs={{0,6},{1,7},{2,0},{3,1},{4,2},{5,3},{6,4},{7,5},{8,14},{9,15},{10,... | collective-permute-start | bytes 1179656 | tf_op jit(solution)/shard_map/ppermute | solution.py:509
  79.6 3.7 %collective-permute-start.26 = (f32[4,96,128]{2,1,0:T(8,128)S(1)}, f32[4,96,128]{2,1,0:T(8,128)S(1)}, u32[]{:S(2)}, u32[]{:S(2)}) collective-permute-start(f32[4,96,128]{2,1,0:T(8,128)S(1)} %shard_map.104), channel_id=1, source_target_pairs={{0,32},{8,40},{16,48},{24,56},{32,0},{40,8},{48,16},{56,24},{64,96... | collective-permute-start | bytes 589832 | tf_op jit(solution)/shard_map/ppermute | solution.py:516
  83.3 6.0 %collective-permute-done.26.refs_3_ = f32[4,96,128]{2,1,0:T(8,128)S(1)} collective-permute-done((f32[4,96,128]{2,1,0:T(8,128)S(1)}, f32[4,96,128]{2,1,0:T(8,128)S(1)}, u32[]{:S(2)}, u32[]{:S(2)}) %collective-permute-start.26) | collective-permute-done | bytes 196640 | tf_op jit(solution)/shard_map/ppermute | solution.py:516
  89.3 2.6 %collective-permute-done.28.refs_4_ = f32[4,96,128]{2,1,0:T(8,128)S(1)} collective-permute-done((f32[4,96,128]{2,1,0:T(8,128)S(1)}, f32[4,96,128]{2,1,0:T(8,128)S(1)}, u32[]{:S(2)}, u32[]{:S(2)}) %collective-permute-start.28) | collective-permute-done | bytes 196640 | tf_op jit(solution)/shard_map/ppermute | solution.py:516
  93.0 3.9 %collective-permute-start.30 = (f32[96,128]{1,0:T(8,128)S(1)}, f32[96,128]{1,0:T(8,128)S(1)}, u32[]{:S(2)}, u32[]{:S(2)}) collective-permute-start(f32[96,128]{1,0:T(8,128)S(1)} %get-tuple-element.52), channel_id=1, source_target_pairs={{0,128},{8,136},{16,144},{24,152},{32,160},{40,168},{48,176},{56,1... | collective-permute-start | bytes 147464 | tf_op jit(solution)/shard_map/ppermute | solution.py:518
  96.9 3.2 %collective-permute-start.31 = (f32[96,128]{1,0:T(8,128)S(1)}, f32[96,128]{1,0:T(8,128)S(1)}, u32[]{:S(2)}, u32[]{:S(2)}) collective-permute-start(f32[96,128]{1,0:T(8,128)S(1)} %get-tuple-element.53), channel_id=1, source_target_pairs={{0,192},{8,200},{16,208},{24,216},{32,224},{40,232},{48,240},{56,2... | collective-permute-start | bytes 147464 | tf_op jit(solution)/shard_map/ppermute | solution.py:518
  101.8 1.6 %collective-permute-done.31.refs_3_ = f32[96,128]{1,0:T(8,128)S(1)} collective-permute-done((f32[96,128]{1,0:T(8,128)S(1)}, f32[96,128]{1,0:T(8,128)S(1)}, u32[]{:S(2)}, u32[]{:S(2)}) %collective-permute-start.31) | collective-permute-done | bytes 49184 | tf_op jit(solution)/shard_map/ppermute | solution.py:518
  103.3 1.2 %shard_map.107 = f32[8,24,128]{2,1,0:T(8,128)} custom-call(s32[2]{0:T(128)S(1)} %copy-done, f32[96,128]{1,0:T(8,128)S(1)} %get-tuple-element.50.refs_0_, f32[96,128]{1,0:T(8,128)S(1)} %collective-permute-done.29.refs_1_, f32[96,128]{1,0:T(8,128)S(1)} %collective-permute-done.30.refs_2_, f32[96,128]{1,0:T(8,128)S(1)} %collective-permute-done.31.refs_3_), custom_call_target="tpu_custom_call" | custom-call | bytes 393216 | tf_op jit(solution)/shard_map/pallas_call | solution.py:116
  104.6 4.9 %all-to-all-start.1 = ((f32[8,24,128]{2,1,0:T(8,128)}), f32[8,24,128]{2,1,0:T(8,128)S(1)}, u32[]{:S(2)}, u32[]{:S(2)}) async-start(f32[8,24,128]{2,1,0:T(8,128)} %shard_map.107), calls=%async_computation.1 | async-start | bytes 196608 | tf_op jit(solution)/shard_map/all_to_all | solution.py:528
  111.0 5.0 %all-to-all-done.1.refs_0_ = f32[8,24,128]{2,1,0:T(8,128)S(1)} async-done(((f32[8,24,128]{2,1,0:T(8,128)}), f32[8,24,128]{2,1,0:T(8,128)S(1)}, u32[]{:S(2)}, u32[]{:S(2)}) %all-to-all-start.1) | async-done | bytes 98336 | tf_op jit(solution)/shard_map/all_to_all | solution.py:528
  (67 shorter events, 17.2 us)
Async XLA Ops:
  2.4 6.8 %collective-permute-start.4 = (f32[2,96,128]{2,1,0:T(8,128)S(1)}, f32[2,96,128]{2,1,0:T(8,128)S(1)}, u32[]{:S(2)}, u32[]{:S(2)}) collective-permute-start(f32[2,96,128]{2,1,0:T(8,128)S(1)} %get-tuple-element.31), channel_id=1, source_target_pairs={{0,16},{8,24},{16,32},{24,40},{32,48},{40,56},{48,0},{56,8},{64,80... | collective-permute-start | bytes 294920 | tf_op jit(solution)/shard_map/ppermute | solution.py:497
  3.9 6.9 %collective-permute-start.5 = (f32[2,96,128]{2,1,0:T(8,128)S(1)}, f32[2,96,128]{2,1,0:T(8,128)S(1)}, u32[]{:S(2)}, u32[]{:S(2)}) collective-permute-start(f32[2,96,128]{2,1,0:T(8,128)S(1)} %get-tuple-element.32), channel_id=1, source_target_pairs={{0,32},{8,40},{16,48},{24,56},{32,0},{40,8},{48,16},{56,24},{64,96... | collective-permute-start | bytes 294920 | tf_op jit(solution)/shard_map/ppermute | solution.py:497
  6.8 5.0 %collective-permute-start.6 = (f32[2,96,128]{2,1,0:T(8,128)S(1)}, f32[2,96,128]{2,1,0:T(8,128)S(1)}, u32[]{:S(2)}, u32[]{:S(2)}) collective-permute-start(f32[2,96,128]{2,1,0:T(8,128)S(1)} %get-tuple-element.33), channel_id=1, source_target_pairs={{0,48},{8,56},{16,0},{24,8},{32,16},{40,24},{48,32},{56,40},{64,11... | collective-permute-start | bytes 294920 | tf_op jit(solution)/shard_map/ppermute | solution.py:497
  7.2 16.7 %collective-permute-start = (f32[384,128]{1,0:T(8,128)S(1)}, f32[384,128]{1,0:T(8,128)S(1)}, u32[]{:S(2)}, u32[]{:S(2)}) collective-permute-start(f32[384,128]{1,0:T(8,128)S(1)} %get-tuple-element.29), channel_id=1, source_target_pairs={{0,1},{1,0},{2,3},{3,2},{4,5},{5,4},{6,7},{7,6},{8,9},{9,8},{10,11... | collective-permute-start | bytes 589832 | tf_op jit(solution)/shard_map/ppermute | solution.py:477
  14.4 14.4 %collective-permute-start.10 = (f32[4,48,128]{2,1,0:T(8,128)S(1)}, f32[4,48,128]{2,1,0:T(8,128)S(1)}, u32[]{:S(2)}, u32[]{:S(2)}) collective-permute-start(f32[4,48,128]{2,1,0:T(8,128)S(1)} %shard_map.98.refs_0_), channel_id=1, source_target_pairs={{0,192},{8,200},{16,208},{24,216},{32,224},{40,232},{48,240},{56,2... | collective-permute-start | bytes 294920 | tf_op jit(solution)/shard_map/ppermute | solution.py:501
  20.1 12.2 %collective-permute-start.9 = (f32[4,48,128]{2,1,0:T(8,128)S(1)}, f32[4,48,128]{2,1,0:T(8,128)S(1)}, u32[]{:S(2)}, u32[]{:S(2)}) collective-permute-start(f32[4,48,128]{2,1,0:T(8,128)S(1)} %shard_map.98.refs_0_), channel_id=1, source_target_pairs={{0,128},{8,136},{16,144},{24,152},{32,160},{40,168},{48,176},{56,1... | collective-permute-start | bytes 294920 | tf_op jit(solution)/shard_map/ppermute | solution.py:501
  21.1 11.2 %collective-permute-start.8 = (f32[4,48,128]{2,1,0:T(8,128)S(1)}, f32[4,48,128]{2,1,0:T(8,128)S(1)}, u32[]{:S(2)}, u32[]{:S(2)}) collective-permute-start(f32[4,48,128]{2,1,0:T(8,128)S(1)} %shard_map.98.refs_0_), channel_id=1, source_target_pairs={{0,64},{8,72},{16,80},{24,88},{32,96},{40,104},{48,112},{56,120},{... | collective-permute-start | bytes 294920 | tf_op jit(solution)/shard_map/ppermute | solution.py:501
  24.5 24.1 %collective-permute-start.3 = (f32[2,384,128]{2,1,0:T(8,128)S(1)}, f32[2,384,128]{2,1,0:T(8,128)S(1)}, u32[]{:S(2)}, u32[]{:S(2)}) collective-permute-start(f32[2,384,128]{2,1,0:T(8,128)S(1)} %shard_map.96.refs_0_), channel_id=1, source_target_pairs={{0,6},{1,7},{2,0},{3,1},{4,2},{5,3},{6,4},{7,5},{8,14},{9,15},{10,... | collective-permute-start | bytes 1179656 | tf_op jit(solution)/shard_map/ppermute | solution.py:495
  33.6 11.8 %all-to-all-start = ((f32[8,48,128]{2,1,0:T(8,128)}), f32[8,48,128]{2,1,0:T(8,128)S(1)}, u32[]{:S(2)}, u32[]{:S(2)}) async-start(f32[8,48,128]{2,1,0:T(8,128)} %shard_map.99), calls=%async_computation | async-start | bytes 393216 | tf_op jit(solution)/shard_map/all_to_all | solution.py:503
  38.2 15.3 %collective-permute-start.2 = (f32[2,384,128]{2,1,0:T(8,128)S(1)}, f32[2,384,128]{2,1,0:T(8,128)S(1)}, u32[]{:S(2)}, u32[]{:S(2)}) collective-permute-start(f32[2,384,128]{2,1,0:T(8,128)S(1)} %shard_map.96.refs_0_), channel_id=1, source_target_pairs={{0,4},{1,5},{2,6},{3,7},{4,0},{5,1},{6,2},{7,3},{8,12},{9,13},{10,... | collective-permute-start | bytes 1179656 | tf_op jit(solution)/shard_map/ppermute | solution.py:495
  45.4 8.2 %collective-permute-start.13 = (f32[8,48,128]{2,1,0:T(8,128)S(1)}, f32[8,48,128]{2,1,0:T(8,128)S(1)}, u32[]{:S(2)}, u32[]{:S(2)}) collective-permute-start(f32[8,48,128]{2,1,0:T(8,128)S(1)} %all-to-all-done.refs_4_), channel_id=1, source_target_pairs={{0,48},{8,56},{16,0},{24,8},{32,16},{40,24},{48,32},{56,40},{64,11... | collective-permute-start | bytes 589832 | tf_op jit(solution)/shard_map/ppermute | solution.py:504
  46.0 14.3 %collective-permute-start.1 = (f32[2,384,128]{2,1,0:T(8,128)S(1)}, f32[2,384,128]{2,1,0:T(8,128)S(1)}, u32[]{:S(2)}, u32[]{:S(2)}) collective-permute-start(f32[2,384,128]{2,1,0:T(8,128)S(1)} %shard_map.96.refs_0_), channel_id=1, source_target_pairs={{0,2},{1,3},{2,4},{3,5},{4,6},{5,7},{6,0},{7,1},{8,10},{9,11},{10,... | collective-permute-start | bytes 1179656 | tf_op jit(solution)/shard_map/ppermute | solution.py:495
  46.5 8.3 %collective-permute-start.12 = (f32[8,48,128]{2,1,0:T(8,128)S(1)}, f32[8,48,128]{2,1,0:T(8,128)S(1)}, u32[]{:S(2)}, u32[]{:S(2)}) collective-permute-start(f32[8,48,128]{2,1,0:T(8,128)S(1)} %all-to-all-done.refs_4_), channel_id=1, source_target_pairs={{0,32},{8,40},{16,48},{24,56},{32,0},{40,8},{48,16},{56,24},{64,96... | collective-permute-start | bytes 589832 | tf_op jit(solution)/shard_map/ppermute | solution.py:504
  48.5 7.4 %collective-permute-start.11 = (f32[8,48,128]{2,1,0:T(8,128)S(1)}, f32[8,48,128]{2,1,0:T(8,128)S(1)}, u32[]{:S(2)}, u32[]{:S(2)}) collective-permute-start(f32[8,48,128]{2,1,0:T(8,128)S(1)} %all-to-all-done.refs_4_), channel_id=1, source_target_pairs={{0,16},{8,24},{16,32},{24,40},{32,48},{40,56},{48,0},{56,8},{64,80... | collective-permute-start | bytes 589832 | tf_op jit(solution)/shard_map/ppermute | solution.py:504
  53.5 6.8 %collective-permute-start.14 = (f32[8,48,128]{2,1,0:T(8,128)S(1)}, f32[8,48,128]{2,1,0:T(8,128)S(1)}, u32[]{:S(2)}, u32[]{:S(2)}) collective-permute-start(f32[8,48,128]{2,1,0:T(8,128)S(1)} %all-to-all-done.refs_4_), channel_id=1, source_target_pairs={{0,8},{8,0},{16,24},{24,16},{32,40},{40,32},{48,56},{56,48},{64,72... | collective-permute-start | bytes 589832 | tf_op jit(solution)/shard_map/ppermute | solution.py:481
  53.5 6.8 %collective-permute-start.17 = (f32[8,48,128]{2,1,0:T(8,128)S(1)}, f32[8,48,128]{2,1,0:T(8,128)S(1)}, u32[]{:S(2)}, u32[]{:S(2)}) collective-permute-start(f32[8,48,128]{2,1,0:T(8,128)S(1)} %collective-permute-done.13.refs_7_), channel_id=1, source_target_pairs={{0,8},{8,0},{16,24},{24,16},{32,40},{40,32},{48,56},{56,48},{64,72... | collective-permute-start | bytes 589832 | tf_op jit(solution)/shard_map/ppermute | solution.py:481
  54.8 5.5 %collective-permute-start.16 = (f32[8,48,128]{2,1,0:T(8,128)S(1)}, f32[8,48,128]{2,1,0:T(8,128)S(1)}, u32[]{:S(2)}, u32[]{:S(2)}) collective-permute-start(f32[8,48,128]{2,1,0:T(8,128)S(1)} %collective-permute-done.12.refs_6_), channel_id=1, source_target_pairs={{0,8},{8,0},{16,24},{24,16},{32,40},{40,32},{48,56},{56,48},{64,72... | collective-permute-start | bytes 589832 | tf_op jit(solution)/shard_map/ppermute | solution.py:481
  55.9 4.4 %collective-permute-start.15 = (f32[8,48,128]{2,1,0:T(8,128)S(1)}, f32[8,48,128]{2,1,0:T(8,128)S(1)}, u32[]{:S(2)}, u32[]{:S(2)}) collective-permute-start(f32[8,48,128]{2,1,0:T(8,128)S(1)} %collective-permute-done.11.refs_5_), channel_id=1, source_target_pairs={{0,8},{8,0},{16,24},{24,16},{32,40},{40,32},{48,56},{56,48},{64,72... | collective-permute-start | bytes 589832 | tf_op jit(solution)/shard_map/ppermute | solution.py:481
  69.6 6.2 %collective-permute-start.25 = (f32[4,96,128]{2,1,0:T(8,128)S(1)}, f32[4,96,128]{2,1,0:T(8,128)S(1)}, u32[]{:S(2)}, u32[]{:S(2)}) collective-permute-start(f32[4,96,128]{2,1,0:T(8,128)S(1)} %get-tuple-element.47), channel_id=1, source_target_pairs={{0,8},{8,0},{16,24},{24,16},{32,40},{40,32},{48,56},{56,48},{64,72... | collective-permute-start | bytes 589832 | tf_op jit(solution)/shard_map/ppermute | solution.py:481
  70.1 5.7 %collective-permute-start.27 = (f32[4,96,128]{2,1,0:T(8,128)S(1)}, f32[4,96,128]{2,1,0:T(8,128)S(1)}, u32[]{:S(2)}, u32[]{:S(2)}) collective-permute-start(f32[4,96,128]{2,1,0:T(8,128)S(1)} %get-tuple-element.49), channel_id=1, source_target_pairs={{0,8},{8,0},{16,24},{24,16},{32,40},{40,32},{48,56},{56,48},{64,72... | collective-permute-start | bytes 589832 | tf_op jit(solution)/shard_map/ppermute | solution.py:481
  70.2 9.4 %collective-permute-start.22 = (f32[4,96,128]{2,1,0:T(8,128)S(1)}, f32[4,96,128]{2,1,0:T(8,128)S(1)}, u32[]{:S(2)}, u32[]{:S(2)}) collective-permute-start(f32[4,96,128]{2,1,0:T(8,128)S(1)} %get-tuple-element.43), channel_id=1, source_target_pairs={{0,8},{8,0},{16,24},{24,16},{32,40},{40,32},{48,56},{56,48},{64,72... | collective-permute-start | bytes 589832 | tf_op jit(solution)/shard_map/ppermute | solution.py:481
  71.6 11.7 %collective-permute-start.24 = (f32[4,96,128]{2,1,0:T(8,128)S(1)}, f32[4,96,128]{2,1,0:T(8,128)S(1)}, u32[]{:S(2)}, u32[]{:S(2)}) collective-permute-start(f32[4,96,128]{2,1,0:T(8,128)S(1)} %shard_map.103), channel_id=1, source_target_pairs={{0,16},{8,24},{16,32},{24,40},{32,48},{40,56},{48,0},{56,8},{64,80... | collective-permute-start | bytes 589832 | tf_op jit(solution)/shard_map/ppermute | solution.py:516
  73.0 23.9 %collective-permute-start.18 = (f32[2,384,128]{2,1,0:T(8,128)S(1)}, f32[2,384,128]{2,1,0:T(8,128)S(1)}, u32[]{:S(2)}, u32[]{:S(2)}) collective-permute-start(f32[2,384,128]{2,1,0:T(8,128)S(1)} %get-tuple-element.37), channel_id=1, source_target_pairs={{0,2},{1,3},{2,4},{3,5},{4,6},{5,7},{6,0},{7,1},{8,10},{9,11},{10,... | collective-permute-start | bytes 1179656 | tf_op jit(solution)/shard_map/ppermute | solution.py:509
  75.8 24.3 %collective-permute-start.19 = (f32[2,384,128]{2,1,0:T(8,128)S(1)}, f32[2,384,128]{2,1,0:T(8,128)S(1)}, u32[]{:S(2)}, u32[]{:S(2)}) collective-permute-start(f32[2,384,128]{2,1,0:T(8,128)S(1)} %get-tuple-element.38), channel_id=1, source_target_pairs={{0,4},{1,5},{2,6},{3,7},{4,0},{5,1},{6,2},{7,3},{8,12},{9,13},{10,... | collective-permute-start | bytes 1179656 | tf_op jit(solution)/shard_map/ppermute | solution.py:509
  75.8 24.2 %collective-permute-start.20 = (f32[2,384,128]{2,1,0:T(8,128)S(1)}, f32[2,384,128]{2,1,0:T(8,128)S(1)}, u32[]{:S(2)}, u32[]{:S(2)}) collective-permute-start(f32[2,384,128]{2,1,0:T(8,128)S(1)} %get-tuple-element.39), channel_id=1, source_target_pairs={{0,6},{1,7},{2,0},{3,1},{4,2},{5,3},{6,4},{7,5},{8,14},{9,15},{10,... | collective-permute-start | bytes 1179656 | tf_op jit(solution)/shard_map/ppermute | solution.py:509
  79.6 9.7 %collective-permute-start.26 = (f32[4,96,128]{2,1,0:T(8,128)S(1)}, f32[4,96,128]{2,1,0:T(8,128)S(1)}, u32[]{:S(2)}, u32[]{:S(2)}) collective-permute-start(f32[4,96,128]{2,1,0:T(8,128)S(1)} %shard_map.104), channel_id=1, source_target_pairs={{0,32},{8,40},{16,48},{24,56},{32,0},{40,8},{48,16},{56,24},{64,96... | collective-permute-start | bytes 589832 | tf_op jit(solution)/shard_map/ppermute | solution.py:516
  83.3 8.6 %collective-permute-start.28 = (f32[4,96,128]{2,1,0:T(8,128)S(1)}, f32[4,96,128]{2,1,0:T(8,128)S(1)}, u32[]{:S(2)}, u32[]{:S(2)}) collective-permute-start(f32[4,96,128]{2,1,0:T(8,128)S(1)} %shard_map.105), channel_id=1, source_target_pairs={{0,48},{8,56},{16,0},{24,8},{32,16},{40,24},{48,32},{56,40},{64,11... | collective-permute-start | bytes 589832 | tf_op jit(solution)/shard_map/ppermute | solution.py:516
  92.5 9.3 %collective-permute-start.29 = (f32[96,128]{1,0:T(8,128)S(1)}, f32[96,128]{1,0:T(8,128)S(1)}, u32[]{:S(2)}, u32[]{:S(2)}) collective-permute-start(f32[96,128]{1,0:T(8,128)S(1)} %get-tuple-element.51), channel_id=1, source_target_pairs={{0,64},{8,72},{16,80},{24,88},{32,96},{40,104},{48,112},{56,120},{... | collective-permute-start | bytes 147464 | tf_op jit(solution)/shard_map/ppermute | solution.py:518
  93.0 8.8 %collective-permute-start.30 = (f32[96,128]{1,0:T(8,128)S(1)}, f32[96,128]{1,0:T(8,128)S(1)}, u32[]{:S(2)}, u32[]{:S(2)}) collective-permute-start(f32[96,128]{1,0:T(8,128)S(1)} %get-tuple-element.52), channel_id=1, source_target_pairs={{0,128},{8,136},{16,144},{24,152},{32,160},{40,168},{48,176},{56,1... | collective-permute-start | bytes 147464 | tf_op jit(solution)/shard_map/ppermute | solution.py:518
  96.9 6.5 %collective-permute-start.31 = (f32[96,128]{1,0:T(8,128)S(1)}, f32[96,128]{1,0:T(8,128)S(1)}, u32[]{:S(2)}, u32[]{:S(2)}) collective-permute-start(f32[96,128]{1,0:T(8,128)S(1)} %get-tuple-element.53), channel_id=1, source_target_pairs={{0,192},{8,200},{16,208},{24,216},{32,224},{40,232},{48,240},{56,2... | collective-permute-start | bytes 147464 | tf_op jit(solution)/shard_map/ppermute | solution.py:518
  100.7 8.8 %collective-permute-start.21 = (f32[384,128]{1,0:T(8,128)S(1)}, f32[384,128]{1,0:T(8,128)S(1)}, u32[]{:S(2)}, u32[]{:S(2)}) collective-permute-start(f32[384,128]{1,0:T(8,128)S(1)} %get-tuple-element.41), channel_id=1, source_target_pairs={{0,1},{1,0},{2,3},{3,2},{4,5},{5,4},{6,7},{7,6},{8,9},{9,8},{10,11... | collective-permute-start | bytes 589832 | tf_op jit(solution)/shard_map/ppermute | solution.py:477
  104.6 11.4 %all-to-all-start.1 = ((f32[8,24,128]{2,1,0:T(8,128)}), f32[8,24,128]{2,1,0:T(8,128)S(1)}, u32[]{:S(2)}, u32[]{:S(2)}) async-start(f32[8,24,128]{2,1,0:T(8,128)} %shard_map.107), calls=%async_computation.1 | async-start | bytes 196608 | tf_op jit(solution)/shard_map/all_to_all | solution.py:528
  (9 other events, 168.6 us)

commit v5 on v4

--- a/solution.py
+++ b/solution.py
@@ -180,7 +180,8 @@
         out_ref[b] = jnp.where(info[C_OWN + b // 2] == 1, keep_ref[b], got_ref[b])
 
 
-def pick_z_kernel(info, z0, z1, z2, z3, out_ref):
+def pick_z_kernel(info, z0, z1, z2, z3, *refs):
+    out_ref = refs[-1]
     for b in range(4):
         value = pick(info[Z_STEP + b // 2], [z[b] for z in (z0, z1, z2, z3)])
         out_ref[2 * b] = value
@@ -321,10 +322,6 @@
                 r.wide[8 * s : 8 * s + 8, one] = piece * r.orb[s, rows, :]
             r.wide[64:72, one] = part[64:72] * r.orb_tail[:, one]
     r.wide[:, TILES * LANES :] = jnp.zeros((XR, 2 * LANES), F32)
-    for d in range(4):
-        y = lax.rem(info[MY_Y] + d, 4)
-        r.sent[d][0] = r.own[2 * y + info[MY_PAIR]]
-        r.sent[d][1] = r.own[2 * y + 1 - info[MY_PAIR]]
 
 
 def share_out(r, info, scale):
@@ -373,11 +370,11 @@
 
 def field_kernel(scale, info, *refs):
     tables = ("fx", "ix", "zt", "fy", "iy", "sq")
-    scratch = ("orb", "blk", "own", "wide", "orb_tail", "blk_tail", "col", "re", "im", "cut")
+    scratch = ("orb", "blk", "wide", "orb_tail", "blk_tail", "col", "re", "im", "cut")
     r = types.SimpleNamespace(slabs=refs[:4], mine=refs[4:8], other=refs[8:12])
     vars(r).update(zip(tables, refs[12:18]))
-    r.sent, r.keep, r.give = refs[18:22], refs[22:26], refs[26:30]
-    vars(r).update(zip(scratch, refs[30:]))
+    r.own, r.keep, r.give = refs[18], refs[19:23], refs[23:27]
+    vars(r).update(zip(scratch, refs[27:]))
     for stage in STAGES:
         stage(r, info, scale)
 
@@ -389,13 +386,12 @@
     whole_slabs = pltpu.VMEM((8, ROWS, LANES), F32)
     return call(
         body,
-        [shape(2, ROWS, LANES)] * 4 + [shape(4, PACK, LANES)] * 8,
+        [shape(8, ROWS, LANES)] + [shape(4, PACK, LANES)] * 8,
         block_owner,
         *slabs,
         *pieces,
         *[jnp.asarray(t) for t in tables()],
         scratch=[
-            whole_slabs,
             whole_slabs,
             whole_slabs,
             pltpu.VMEM((XR, (TILES + 2) * LANES), F32),
@@ -411,8 +407,16 @@
     )
 
 
-def add_kernel(info, a_ref, b_ref, out_ref):
-    out_ref[...] = a_ref[...] + b_ref[...]
+def send_kernel(info, own_ref, after_ref, *outs):
+    for d in range(4):
+        y = lax.rem(info[MY_Y] + d, 4)
+        outs[d][0] = own_ref[2 * y + info[MY_PAIR]]
+        outs[d][1] = own_ref[2 * y + 1 - info[MY_PAIR]]
+
+
+def add_core_kernel(info, *refs):
+    for d in range(3):
+        refs[6 + d][...] = refs[d][...] + refs[3 + d][...]
 
 
 def add_x_kernel(info, k_ref, g_ref, r1, r2, r3, *outs):
@@ -437,7 +441,7 @@
         out_ref[s, 17:18, :] = last[s : s + 1]
 
 
-def share_kernel(info, part_ref, out_ref):
+def share_kernel(info, part_ref, after_ref, out_ref):
     for b in range(4):
         total = part_ref[2 * b] + part_ref[2 * b + 1]
         at = (b // 2, b % 2)
@@ -447,7 +451,7 @@
         out_ref[at[0], at[1], 8:9, LANES:SHARE] = total[17:18, :REST]
 
 
-def add_y_kernel(info, s_ref, r1, r2, r3, stay_ref, cross_ref):
+def add_y_kernel(info, s_ref, r1, r2, r3, after_ref, stay_ref, cross_ref):
     for j, ref in enumerate((stay_ref, cross_ref)):
         ref[...] = s_ref[j] + r1[j] + r2[j] + r3[j]
 
@@ -492,7 +496,8 @@
         scratch=[pltpu.VMEM((2, ROWS, LANES), F32)],
     )
     pair = call(join_kernel, shape(2, ROWS, LANES), block_owner, stay, other_slab(cross))
-    slabs = [pair] + [lax.ppermute(pair, "grid", shift_y(d)) for d in (1, 2, 3)]
+    slabs = [pair] + [lax.ppermute(pair, "grid", shift_y(d)) for d in (1, 3)]
+    slabs.insert(2, lax.ppermute(slabs[1], "grid", shift_y(1)))
 
     quarters = quarters[:1] + [lax.ppermute(quarters[d], "band", shift_x(d)) for d in (1, 2, 3)]
     half = shape(4, PIECE, LANES)
@@ -504,16 +509,13 @@
     pieces = [piece] + [lax.ppermute(piece, "band", shift_x(d)) for d in (1, 2, 3)]
     pieces = pieces + [other_core(p) for p in pieces]
 
-    outs = fields(block_owner, slabs, pieces, scale)
-    sent, shares = list(outs[:4]), outs[4:]
-    sent = sent[:1] + [lax.ppermute(sent[d], "grid", shift_y(d)) for d in (1, 2, 3)]
-    stay, cross = call(add_y_kernel, [slab, slab], block_owner, *sent)
-    own = other_slab(cross)
+    own, *shares = fields(block_owner, slabs, pieces, scale)
     kept, got = shares[:4], [other_core(g) for g in shares[4:]]
     part = shape(4, PACK, LANES)
-    moved = []
-    for d in (1, 2, 3):
-        moved.append(lax.ppermute(call(add_kernel, part, block_owner, kept[d], got[d]), "band", shift_x(d)))
+    added = call(add_core_kernel, [part] * 3, block_owner, *kept[1:], *got[1:])
+    moved = [lax.ppermute(added[d - 1], "band", shift_x(d)) for d in (1, 2, 3)]
+    sent = call(send_kernel, [shape(2, ROWS, LANES)] * 4, block_owner, own, after=added[:1])
+    sent = [sent[0]] + [lax.ppermute(sent[d], "grid", shift_y(d)) for d in (1, 2, 3)]
     sums = call(add_x_kernel, [shape(PACK, LANES)] * 4, block_owner, kept[0], got[0], *moved)
     moved = [lax.ppermute(sums[d], "band", shift_z(d)) for d in (1, 2, 3)]
     slabs = call(
@@ -524,10 +526,12 @@
         *moved,
         scratch=[pltpu.VMEM((PACK, LANES), F32)],
     )
+    stay, cross = call(add_y_kernel, [slab, slab], block_owner, *sent, after=[slabs])
+    field = call(own_kernel, shape(2, SLAB, PLANE), block_owner, stay, other_slab(cross))
+    slabs = lax.all_to_all(slabs, "grid", 0, 0)
     block_field = call(
-        share_kernel, shape(2, 2, SLAB, SHARE), block_owner, lax.all_to_all(slabs, "grid", 0, 0)
+        share_kernel, shape(2, 2, SLAB, SHARE), block_owner, slabs, after=[field]
     )
-    field = call(own_kernel, shape(2, SLAB, PLANE), block_owner, stay, own)
     return field, block_field
 
 

time: 118 us -> 114 us (0.966)
  the two profiles are of different devices: /device:TPU:2 before, /device:TPU:64 now
where the time goes in v5:
time: 114 us
  starting transfers between devices  50.3 us (44%)
  waiting for transfers between devices  42.1 us (37%)
  Pallas kernels  17.3 us (15%)
  local copies, waits for them, and re-layouts  3.31 us (3%)
    pallas_call x13, Pallas kernels, call(): pl.pallas_call(body, in_specs=specs, out_shape=out_shape, scratch_shapes=...  17.3 us
    ppermute x3, starting transfers between devices, on_device(): along = [mine] + [lax.ppermute(mine, 'band', shift_z(d)) for d in (1, 2, 3)]  9.6 us
    ppermute x3, waiting for transfers between devices, on_device(): moved = [lax.ppermute(added[d - 1], 'band', shift_x(d)) for d in (1, 2, 3)]  9.27 us
    ppermute x3, waiting for transfers between devices, on_device(): moved = [lax.ppermute(sums[d], 'band', shift_z(d)) for d in (1, 2, 3)]  7.73 us
    ppermute x3, waiting for transfers between devices, on_device(): lax.ppermute(piece, 'band', shift_x(d))  7.46 us
    all_to_all x1, starting transfers between devices, on_device(): piece = lax.all_to_all(mine, 'grid', 0, 0)  6.77 us
    ppermute x3, starting transfers between devices, on_device(): lax.ppermute(quarters[d], 'band', shift_x(d))  5.73 us
    ppermute x3, starting transfers between devices, on_device(): moved = [lax.ppermute(sums[d], 'band', shift_z(d)) for d in (1, 2, 3)]  5.07 us
  transfers between devices with their start and end apart: 34, of which 21 were waited for; matrix products, arithmetic and copies ran while one was open for 1% of the time, Pallas kernels for 6%

profile of v5, /device:TPU:64, one launch (start us, length us, event | category | flops | bytes accessed | tf_op | source)
XLA Modules:
  0.0 114.0 jit_solution(16623140593860897833)
XLA Ops:
  3.0 1.6 %collective-permute-start.4 = (f32[2,96,128]{2,1,0:T(8,128)S(1)}, f32[2,96,128]{2,1,0:T(8,128)S(1)}, u32[]{:S(2)}, u32[]{:S(2)}) collective-permute-start(f32[2,96,128]{2,1,0:T(8,128)S(1)} %get-tuple-element.35), channel_id=1, source_target_pairs={{0,16},{8,24},{16,32},{24,40},{32,48},{40,56},{48,0},{56,8},{64,80... | collective-permute-start | bytes 294920 | tf_op jit(solution)/shard_map/ppermute | solution.py:502
  4.6 2.7 %collective-permute-start.5 = (f32[2,96,128]{2,1,0:T(8,128)S(1)}, f32[2,96,128]{2,1,0:T(8,128)S(1)}, u32[]{:S(2)}, u32[]{:S(2)}) collective-permute-start(f32[2,96,128]{2,1,0:T(8,128)S(1)} %get-tuple-element.36), channel_id=1, source_target_pairs={{0,32},{8,40},{16,48},{24,56},{32,0},{40,8},{48,16},{56,24},{64,96... | collective-permute-start | bytes 294920 | tf_op jit(solution)/shard_map/ppermute | solution.py:502
  7.3 1.4 %collective-permute-start.6 = (f32[2,96,128]{2,1,0:T(8,128)S(1)}, f32[2,96,128]{2,1,0:T(8,128)S(1)}, u32[]{:S(2)}, u32[]{:S(2)}) collective-permute-start(f32[2,96,128]{2,1,0:T(8,128)S(1)} %get-tuple-element.37), channel_id=1, source_target_pairs={{0,48},{8,56},{16,0},{24,8},{32,16},{40,24},{48,32},{56,40},{64,11... | collective-permute-start | bytes 294920 | tf_op jit(solution)/shard_map/ppermute | solution.py:502
  8.8 1.9 %collective-permute-start = (f32[384,128]{1,0:T(8,128)S(1)}, f32[384,128]{1,0:T(8,128)S(1)}, u32[]{:S(2)}, u32[]{:S(2)}) collective-permute-start(f32[384,128]{1,0:T(8,128)S(1)} %get-tuple-element.33), channel_id=1, source_target_pairs={{0,1},{1,0},{2,3},{3,2},{4,5},{5,4},{6,7},{7,6},{8,9},{9,8},{10,11... | collective-permute-start | bytes 589832 | tf_op jit(solution)/shard_map/ppermute | solution.py:481
  10.7 1.3 %collective-permute-done.5.refs_2_ = f32[2,96,128]{2,1,0:T(8,128)S(1)} collective-permute-done((f32[2,96,128]{2,1,0:T(8,128)S(1)}, f32[2,96,128]{2,1,0:T(8,128)S(1)}, u32[]{:S(2)}, u32[]{:S(2)}) %collective-permute-start.5) | collective-permute-done | bytes 98336 | tf_op jit(solution)/shard_map/ppermute | solution.py:502
  12.7 1.3 %collective-permute-done.7.refs_1_ = f32[4,48,128]{2,1,0:T(8,128)S(1)} collective-permute-done((f32[4,48,128]{2,1,0:T(8,128)S(1)}, f32[4,48,128]{2,1,0:T(8,128)S(1)}, u32[]{:S(2)}, u32[]{:S(2)}) %collective-permute-start.7) | collective-permute-done | bytes 98336 | tf_op jit(solution)/shard_map/ppermute | solution.py:485
  14.9 6.6 %collective-permute-start.9 = (f32[4,48,128]{2,1,0:T(8,128)S(1)}, f32[4,48,128]{2,1,0:T(8,128)S(1)}, u32[]{:S(2)}, u32[]{:S(2)}) collective-permute-start(f32[4,48,128]{2,1,0:T(8,128)S(1)} %shard_map.98.refs_0_), channel_id=1, source_target_pairs={{0,128},{8,136},{16,144},{24,152},{32,160},{40,168},{48,176},{56,1... | collective-permute-start | bytes 294920 | tf_op jit(solution)/shard_map/ppermute | solution.py:506
  21.5 2.7 %collective-permute-start.8 = (f32[4,48,128]{2,1,0:T(8,128)S(1)}, f32[4,48,128]{2,1,0:T(8,128)S(1)}, u32[]{:S(2)}, u32[]{:S(2)}) collective-permute-start(f32[4,48,128]{2,1,0:T(8,128)S(1)} %shard_map.98.refs_0_), channel_id=1, source_target_pairs={{0,64},{8,72},{16,80},{24,88},{32,96},{40,104},{48,112},{56,120},{... | collective-permute-start | bytes 294920 | tf_op jit(solution)/shard_map/ppermute | solution.py:506
  24.7 1.7 %collective-permute-start.1 = (f32[2,384,128]{2,1,0:T(8,128)S(1)}, f32[2,384,128]{2,1,0:T(8,128)S(1)}, u32[]{:S(2)}, u32[]{:S(2)}) collective-permute-start(f32[2,384,128]{2,1,0:T(8,128)S(1)} %shard_map.96.refs_0_), channel_id=1, source_target_pairs={{0,2},{1,3},{2,4},{3,5},{4,6},{5,7},{6,0},{7,1},{8,10},{9,11},{10,... | collective-permute-start | bytes 1179656 | tf_op jit(solution)/shard_map/ppermute | solution.py:499
  26.4 3.0 %collective-permute-done.8.refs_1_ = f32[4,48,128]{2,1,0:T(8,128)S(1)} collective-permute-done((f32[4,48,128]{2,1,0:T(8,128)S(1)}, f32[4,48,128]{2,1,0:T(8,128)S(1)}, u32[]{:S(2)}, u32[]{:S(2)}) %collective-permute-start.8) | collective-permute-done | bytes 98336 | tf_op jit(solution)/shard_map/ppermute | solution.py:506
  29.3 1.3 %shard_map.99 = f32[8,48,128]{2,1,0:T(8,128)} custom-call(s32[2]{0:T(128)S(1)} %copy-done, f32[4,48,128]{2,1,0:T(8,128)S(1)} %shard_map.98.refs_0_, f32[4,48,128]{2,1,0:T(8,128)S(1)} %collective-permute-done.8.refs_1_, f32[4,48,128]{2,1,0:T(8,128)S(1)} %collective-permute-done.9.refs_2_, f32[4,48,128]{2,1,0:T(8,128)S(1)} %collective-permute-done.10.refs_3_), custom_call_target="tpu_custom_call" | custom-call | bytes 786432 | tf_op jit(solution)/shard_map/pallas_call | solution.py:116
  30.6 6.8 %all-to-all-start = ((f32[8,48,128]{2,1,0:T(8,128)}), f32[8,48,128]{2,1,0:T(8,128)S(1)}, u32[]{:S(2)}, u32[]{:S(2)}) async-start(f32[8,48,128]{2,1,0:T(8,128)} %shard_map.99), calls=%async_computation | async-start | bytes 393216 | tf_op jit(solution)/shard_map/all_to_all | solution.py:508
  37.4 3.2 %collective-permute-start.3 = (f32[2,384,128]{2,1,0:T(8,128)S(1)}, f32[2,384,128]{2,1,0:T(8,128)S(1)}, u32[]{:S(2)}, u32[]{:S(2)}) collective-permute-start(f32[2,384,128]{2,1,0:T(8,128)S(1)} %shard_map.96.refs_0_), channel_id=1, source_target_pairs={{0,6},{1,7},{2,0},{3,1},{4,2},{5,3},{6,4},{7,5},{8,14},{9,15},{10,... | collective-permute-start | bytes 1179656 | tf_op jit(solution)/shard_map/ppermute | solution.py:499
  40.6 3.7 %all-to-all-done.refs_4_ = f32[8,48,128]{2,1,0:T(8,128)S(1)} async-done(((f32[8,48,128]{2,1,0:T(8,128)}), f32[8,48,128]{2,1,0:T(8,128)S(1)}, u32[]{:S(2)}, u32[]{:S(2)}) %all-to-all-start) | async-done | bytes 196640 | tf_op jit(solution)/shard_map/all_to_all | solution.py:508
  44.3 2.6 %collective-permute-start.13 = (f32[8,48,128]{2,1,0:T(8,128)S(1)}, f32[8,48,128]{2,1,0:T(8,128)S(1)}, u32[]{:S(2)}, u32[]{:S(2)}) collective-permute-start(f32[8,48,128]{2,1,0:T(8,128)S(1)} %all-to-all-done.refs_4_), channel_id=1, source_target_pairs={{0,48},{8,56},{16,0},{24,8},{32,16},{40,24},{48,32},{56,40},{64,11... | collective-permute-start | bytes 589832 | tf_op jit(solution)/shard_map/ppermute | solution.py:509
  50.4 3.8 %collective-permute-done.13.refs_7_ = f32[8,48,128]{2,1,0:T(8,128)S(1)} collective-permute-done((f32[8,48,128]{2,1,0:T(8,128)S(1)}, f32[8,48,128]{2,1,0:T(8,128)S(1)}, u32[]{:S(2)}, u32[]{:S(2)}) %collective-permute-start.13) | collective-permute-done | bytes 196640 | tf_op jit(solution)/shard_map/ppermute | solution.py:509
  54.2 1.7 %collective-permute-done.12.refs_6_ = f32[8,48,128]{2,1,0:T(8,128)S(1)} collective-permute-done((f32[8,48,128]{2,1,0:T(8,128)S(1)}, f32[8,48,128]{2,1,0:T(8,128)S(1)}, u32[]{:S(2)}, u32[]{:S(2)}) %collective-permute-start.12) | collective-permute-done | bytes 196640 | tf_op jit(solution)/shard_map/ppermute | solution.py:509
  55.8 2.0 %collective-permute-done.11.refs_5_ = f32[8,48,128]{2,1,0:T(8,128)S(1)} collective-permute-done((f32[8,48,128]{2,1,0:T(8,128)S(1)}, f32[8,48,128]{2,1,0:T(8,128)S(1)}, u32[]{:S(2)}, u32[]{:S(2)}) %collective-permute-start.11) | collective-permute-done | bytes 196640 | tf_op jit(solution)/shard_map/ppermute | solution.py:509
  58.0 1.2 %collective-permute-done.15.refs_9_ = f32[8,48,128]{2,1,0:T(8,128)S(1)} collective-permute-done((f32[8,48,128]{2,1,0:T(8,128)S(1)}, f32[8,48,128]{2,1,0:T(8,128)S(1)}, u32[]{:S(2)}, u32[]{:S(2)}) %collective-permute-start.15) | collective-permute-done | bytes 196640 | tf_op jit(solution)/shard_map/ppermute | solution.py:485
  59.3 8.8 %shard_map.100 = (f32[8,384,128]{2,1,0:T(8,128)S(1)}, f32[4,96,128]{2,1,0:T(8,128)S(1)}, f32[4,96,128]{2,1,0:T(8,128)S(1)}, f32[4,96,128]{2,1,0:T(8,128)S(1)}, f...) custom-call(s32[2]{0:T(128)S(1)} %copy-done.1, ...), custom_call_target="tpu_custom_call" | custom-call | flops 10000000000 | bytes 8454144 | tf_op jit(solution)/shard_map/pallas_call | solution.py:116
  70.9 1.6 %collective-permute-start.26 = (f32[4,96,128]{2,1,0:T(8,128)S(1)}, f32[4,96,128]{2,1,0:T(8,128)S(1)}, u32[]{:S(2)}, u32[]{:S(2)}) collective-permute-start(f32[4,96,128]{2,1,0:T(8,128)S(1)} %get-tuple-element.54), channel_id=1, source_target_pairs={{0,32},{8,40},{16,48},{24,56},{32,0},{40,8},{48,16},{56,24},{64,96... | collective-permute-start | bytes 589832 | tf_op jit(solution)/shard_map/ppermute | solution.py:516
  73.3 2.5 %collective-permute-start.22 = (f32[2,384,128]{2,1,0:T(8,128)S(1)}, f32[2,384,128]{2,1,0:T(8,128)S(1)}, u32[]{:S(2)}, u32[]{:S(2)}) collective-permute-start(f32[2,384,128]{2,1,0:T(8,128)S(1)} %get-tuple-element.50), channel_id=1, source_target_pairs={{0,4},{1,5},{2,6},{3,7},{4,0},{5,1},{6,2},{7,3},{8,12},{9,13},{10,... | collective-permute-start | bytes 1179656 | tf_op jit(solution)/shard_map/ppermute | solution.py:518
  77.7 1.8 %collective-permute-done.26.refs_3_ = f32[4,96,128]{2,1,0:T(8,128)S(1)} collective-permute-done((f32[4,96,128]{2,1,0:T(8,128)S(1)}, f32[4,96,128]{2,1,0:T(8,128)S(1)}, u32[]{:S(2)}, u32[]{:S(2)}) %collective-permute-start.26) | collective-permute-done | bytes 196640 | tf_op jit(solution)/shard_map/ppermute | solution.py:516
  79.5 3.2 %collective-permute-done.27.refs_4_ = f32[4,96,128]{2,1,0:T(8,128)S(1)} collective-permute-done((f32[4,96,128]{2,1,0:T(8,128)S(1)}, f32[4,96,128]{2,1,0:T(8,128)S(1)}, u32[]{:S(2)}, u32[]{:S(2)}) %collective-permute-start.27) | collective-permute-done | bytes 196640 | tf_op jit(solution)/shard_map/ppermute | solution.py:516
  82.7 4.2 %collective-permute-done.25.refs_2_ = f32[4,96,128]{2,1,0:T(8,128)S(1)} collective-permute-done((f32[4,96,128]{2,1,0:T(8,128)S(1)}, f32[4,96,128]{2,1,0:T(8,128)S(1)}, u32[]{:S(2)}, u32[]{:S(2)}) %collective-permute-start.25) | collective-permute-done | bytes 196640 | tf_op jit(solution)/shard_map/ppermute | solution.py:516
  87.5 3.6 %collective-permute-start.28 = (f32[96,128]{1,0:T(8,128)S(1)}, f32[96,128]{1,0:T(8,128)S(1)}, u32[]{:S(2)}, u32[]{:S(2)}) collective-permute-start(f32[96,128]{1,0:T(8,128)S(1)} %get-tuple-element.57), channel_id=1, source_target_pairs={{0,64},{8,72},{16,80},{24,88},{32,96},{40,104},{48,112},{56,120},{... | collective-permute-start | bytes 147464 | tf_op jit(solution)/shard_map/ppermute | solution.py:520
  91.5 1.7 %collective-permute-done.28.refs_1_ = f32[96,128]{1,0:T(8,128)S(1)} collective-permute-done((f32[96,128]{1,0:T(8,128)S(1)}, f32[96,128]{1,0:T(8,128)S(1)}, u32[]{:S(2)}, u32[]{:S(2)}) %collective-permute-start.28) | collective-permute-done | bytes 49184 | tf_op jit(solution)/shard_map/ppermute | solution.py:520
  94.3 4.8 %collective-permute-done.29.refs_2_ = f32[96,128]{1,0:T(8,128)S(1)} collective-permute-done((f32[96,128]{1,0:T(8,128)S(1)}, f32[96,128]{1,0:T(8,128)S(1)}, u32[]{:S(2)}, u32[]{:S(2)}) %collective-permute-start.29) | collective-permute-done | bytes 49184 | tf_op jit(solution)/shard_map/ppermute | solution.py:520
  100.3 1.3 %shard_map.104.refs_4_ = f32[8,24,128]{2,1,0:T(8,128)} custom-call(s32[2]{0:T(128)S(1)} %copy-done.1, f32[96,128]{1,0:T(8,128)S(1)} %get-tuple-element.56.refs_0_, f32[96,128]{1,0:T(8,128)S(1)} %collective-permute-done.28.refs_1_, f32[96,128]{1,0:T(8,128)S(1)} %collective-permute-done.29.refs_2_, f32[96,128]{1,0:T(8,128)S(1)} %collective-permute-done.30.refs_3_), custom_call_target="tpu_custom_call" | custom-call | bytes 393216 | tf_op jit(solution)/shard_map/pallas_call | solution.py:116
  102.5 3.7 %all-to-all-start.1 = ((f32[8,24,128]{2,1,0:T(8,128)}), f32[8,24,128]{2,1,0:T(8,128)S(1)}, u32[]{:S(2)}, u32[]{:S(2)}) async-start(f32[8,24,128]{2,1,0:T(8,128)} %shard_map.104.refs_4_), calls=%async_computation.1 | async-start | bytes 196608 | tf_op jit(solution)/shard_map/all_to_all | solution.py:531
  106.2 2.2 %collective-permute-done.31.refs_1_ = f32[384,128]{1,0:T(8,128)S(1)} collective-permute-done((f32[384,128]{1,0:T(8,128)S(1)}, f32[384,128]{1,0:T(8,128)S(1)}, u32[]{:S(2)}, u32[]{:S(2)}) %collective-permute-start.31) | collective-permute-done | bytes 196640 | tf_op jit(solution)/shard_map/ppermute | solution.py:481
  110.0 2.8 %all-to-all-done.1.refs_0_ = f32[8,24,128]{2,1,0:T(8,128)S(1)} async-done(((f32[8,24,128]{2,1,0:T(8,128)}), f32[8,24,128]{2,1,0:T(8,128)S(1)}, u32[]{:S(2)}, u32[]{:S(2)}) %all-to-all-start.1) | async-done | bytes 98336 | tf_op jit(solution)/shard_map/all_to_all | solution.py:531
  (68 shorter events, 20.5 us)
Async XLA Ops:
  3.0 7.7 %collective-permute-start.4 = (f32[2,96,128]{2,1,0:T(8,128)S(1)}, f32[2,96,128]{2,1,0:T(8,128)S(1)}, u32[]{:S(2)}, u32[]{:S(2)}) collective-permute-start(f32[2,96,128]{2,1,0:T(8,128)S(1)} %get-tuple-element.35), channel_id=1, source_target_pairs={{0,16},{8,24},{16,32},{24,40},{32,48},{40,56},{48,0},{56,8},{64,80... | collective-permute-start | bytes 294920 | tf_op jit(solution)/shard_map/ppermute | solution.py:502
  4.6 7.3 %collective-permute-start.5 = (f32[2,96,128]{2,1,0:T(8,128)S(1)}, f32[2,96,128]{2,1,0:T(8,128)S(1)}, u32[]{:S(2)}, u32[]{:S(2)}) collective-permute-start(f32[2,96,128]{2,1,0:T(8,128)S(1)} %get-tuple-element.36), channel_id=1, source_target_pairs={{0,32},{8,40},{16,48},{24,56},{32,0},{40,8},{48,16},{56,24},{64,96... | collective-permute-start | bytes 294920 | tf_op jit(solution)/shard_map/ppermute | solution.py:502
  7.3 4.6 %collective-permute-start.6 = (f32[2,96,128]{2,1,0:T(8,128)S(1)}, f32[2,96,128]{2,1,0:T(8,128)S(1)}, u32[]{:S(2)}, u32[]{:S(2)}) collective-permute-start(f32[2,96,128]{2,1,0:T(8,128)S(1)} %get-tuple-element.37), channel_id=1, source_target_pairs={{0,48},{8,56},{16,0},{24,8},{32,16},{40,24},{48,32},{56,40},{64,11... | collective-permute-start | bytes 294920 | tf_op jit(solution)/shard_map/ppermute | solution.py:502
  8.8 15.4 %collective-permute-start = (f32[384,128]{1,0:T(8,128)S(1)}, f32[384,128]{1,0:T(8,128)S(1)}, u32[]{:S(2)}, u32[]{:S(2)}) collective-permute-start(f32[384,128]{1,0:T(8,128)S(1)} %get-tuple-element.33), channel_id=1, source_target_pairs={{0,1},{1,0},{2,3},{3,2},{4,5},{5,4},{6,7},{7,6},{8,9},{9,8},{10,11... | collective-permute-start | bytes 589832 | tf_op jit(solution)/shard_map/ppermute | solution.py:481
  14.5 11.8 %collective-permute-start.10 = (f32[4,48,128]{2,1,0:T(8,128)S(1)}, f32[4,48,128]{2,1,0:T(8,128)S(1)}, u32[]{:S(2)}, u32[]{:S(2)}) collective-permute-start(f32[4,48,128]{2,1,0:T(8,128)S(1)} %shard_map.98.refs_0_), channel_id=1, source_target_pairs={{0,192},{8,200},{16,208},{24,216},{32,224},{40,232},{48,240},{56,2... | collective-permute-start | bytes 294920 | tf_op jit(solution)/shard_map/ppermute | solution.py:506
  14.9 11.5 %collective-permute-start.9 = (f32[4,48,128]{2,1,0:T(8,128)S(1)}, f32[4,48,128]{2,1,0:T(8,128)S(1)}, u32[]{:S(2)}, u32[]{:S(2)}) collective-permute-start(f32[4,48,128]{2,1,0:T(8,128)S(1)} %shard_map.98.refs_0_), channel_id=1, source_target_pairs={{0,128},{8,136},{16,144},{24,152},{32,160},{40,168},{48,176},{56,1... | collective-permute-start | bytes 294920 | tf_op jit(solution)/shard_map/ppermute | solution.py:506
  21.5 7.9 %collective-permute-start.8 = (f32[4,48,128]{2,1,0:T(8,128)S(1)}, f32[4,48,128]{2,1,0:T(8,128)S(1)}, u32[]{:S(2)}, u32[]{:S(2)}) collective-permute-start(f32[4,48,128]{2,1,0:T(8,128)S(1)} %shard_map.98.refs_0_), channel_id=1, source_target_pairs={{0,64},{8,72},{16,80},{24,88},{32,96},{40,104},{48,112},{56,120},{... | collective-permute-start | bytes 294920 | tf_op jit(solution)/shard_map/ppermute | solution.py:506
  24.7 23.0 %collective-permute-start.1 = (f32[2,384,128]{2,1,0:T(8,128)S(1)}, f32[2,384,128]{2,1,0:T(8,128)S(1)}, u32[]{:S(2)}, u32[]{:S(2)}) collective-permute-start(f32[2,384,128]{2,1,0:T(8,128)S(1)} %shard_map.96.refs_0_), channel_id=1, source_target_pairs={{0,2},{1,3},{2,4},{3,5},{4,6},{5,7},{6,0},{7,1},{8,10},{9,11},{10,... | collective-permute-start | bytes 1179656 | tf_op jit(solution)/shard_map/ppermute | solution.py:499
  30.6 13.7 %all-to-all-start = ((f32[8,48,128]{2,1,0:T(8,128)}), f32[8,48,128]{2,1,0:T(8,128)S(1)}, u32[]{:S(2)}, u32[]{:S(2)}) async-start(f32[8,48,128]{2,1,0:T(8,128)} %shard_map.99), calls=%async_computation | async-start | bytes 393216 | tf_op jit(solution)/shard_map/all_to_all | solution.py:508
  37.4 13.0 %collective-permute-start.3 = (f32[2,384,128]{2,1,0:T(8,128)S(1)}, f32[2,384,128]{2,1,0:T(8,128)S(1)}, u32[]{:S(2)}, u32[]{:S(2)}) collective-permute-start(f32[2,384,128]{2,1,0:T(8,128)S(1)} %shard_map.96.refs_0_), channel_id=1, source_target_pairs={{0,6},{1,7},{2,0},{3,1},{4,2},{5,3},{6,4},{7,5},{8,14},{9,15},{10,... | collective-permute-start | bytes 1179656 | tf_op jit(solution)/shard_map/ppermute | solution.py:499
  44.3 9.8 %collective-permute-start.13 = (f32[8,48,128]{2,1,0:T(8,128)S(1)}, f32[8,48,128]{2,1,0:T(8,128)S(1)}, u32[]{:S(2)}, u32[]{:S(2)}) collective-permute-start(f32[8,48,128]{2,1,0:T(8,128)S(1)} %all-to-all-done.refs_4_), channel_id=1, source_target_pairs={{0,48},{8,56},{16,0},{24,8},{32,16},{40,24},{48,32},{56,40},{64,11... | collective-permute-start | bytes 589832 | tf_op jit(solution)/shard_map/ppermute | solution.py:509
  47.0 8.9 %collective-permute-start.12 = (f32[8,48,128]{2,1,0:T(8,128)S(1)}, f32[8,48,128]{2,1,0:T(8,128)S(1)}, u32[]{:S(2)}, u32[]{:S(2)}) collective-permute-start(f32[8,48,128]{2,1,0:T(8,128)S(1)} %all-to-all-done.refs_4_), channel_id=1, source_target_pairs={{0,32},{8,40},{16,48},{24,56},{32,0},{40,8},{48,16},{56,24},{64,96... | collective-permute-start | bytes 589832 | tf_op jit(solution)/shard_map/ppermute | solution.py:509
  47.7 10.3 %collective-permute-start.2 = (f32[2,384,128]{2,1,0:T(8,128)S(1)}, f32[2,384,128]{2,1,0:T(8,128)S(1)}, u32[]{:S(2)}, u32[]{:S(2)}) collective-permute-start(f32[2,384,128]{2,1,0:T(8,128)S(1)} %collective-permute-done.1.refs_1_), channel_id=1, source_target_pairs={{0,2},{1,3},{2,4},{3,5},{4,6},{5,7},{6,0},{7,1},{8,10},{9,11},{10,... | collective-permute-start | bytes 1179656 | tf_op jit(solution)/shard_map/ppermute | solution.py:500
  48.7 9.1 %collective-permute-start.11 = (f32[8,48,128]{2,1,0:T(8,128)S(1)}, f32[8,48,128]{2,1,0:T(8,128)S(1)}, u32[]{:S(2)}, u32[]{:S(2)}) collective-permute-start(f32[8,48,128]{2,1,0:T(8,128)S(1)} %all-to-all-done.refs_4_), channel_id=1, source_target_pairs={{0,16},{8,24},{16,32},{24,40},{32,48},{40,56},{48,0},{56,8},{64,80... | collective-permute-start | bytes 589832 | tf_op jit(solution)/shard_map/ppermute | solution.py:509
  50.4 7.5 %collective-permute-start.14 = (f32[8,48,128]{2,1,0:T(8,128)S(1)}, f32[8,48,128]{2,1,0:T(8,128)S(1)}, u32[]{:S(2)}, u32[]{:S(2)}) collective-permute-start(f32[8,48,128]{2,1,0:T(8,128)S(1)} %all-to-all-done.refs_4_), channel_id=1, source_target_pairs={{0,8},{8,0},{16,24},{24,16},{32,40},{40,32},{48,56},{56,48},{64,72... | collective-permute-start | bytes 589832 | tf_op jit(solution)/shard_map/ppermute | solution.py:485
  54.2 3.9 %collective-permute-start.17 = (f32[8,48,128]{2,1,0:T(8,128)S(1)}, f32[8,48,128]{2,1,0:T(8,128)S(1)}, u32[]{:S(2)}, u32[]{:S(2)}) collective-permute-start(f32[8,48,128]{2,1,0:T(8,128)S(1)} %collective-permute-done.13.refs_7_), channel_id=1, source_target_pairs={{0,8},{8,0},{16,24},{24,16},{32,40},{40,32},{48,56},{56,48},{64,72... | collective-permute-start | bytes 589832 | tf_op jit(solution)/shard_map/ppermute | solution.py:485
  55.8 2.2 %collective-permute-start.16 = (f32[8,48,128]{2,1,0:T(8,128)S(1)}, f32[8,48,128]{2,1,0:T(8,128)S(1)}, u32[]{:S(2)}, u32[]{:S(2)}) collective-permute-start(f32[8,48,128]{2,1,0:T(8,128)S(1)} %collective-permute-done.12.refs_6_), channel_id=1, source_target_pairs={{0,8},{8,0},{16,24},{24,16},{32,40},{40,32},{48,56},{56,48},{64,72... | collective-permute-start | bytes 589832 | tf_op jit(solution)/shard_map/ppermute | solution.py:485
  68.2 1.5 %collective-permute-start.18 = (f32[4,96,128]{2,1,0:T(8,128)S(1)}, f32[4,96,128]{2,1,0:T(8,128)S(1)}, u32[]{:S(2)}, u32[]{:S(2)}) collective-permute-start(f32[4,96,128]{2,1,0:T(8,128)S(1)} %get-tuple-element.44), channel_id=1, source_target_pairs={{0,8},{8,0},{16,24},{24,16},{32,40},{40,32},{48,56},{56,48},{64,72... | collective-permute-start | bytes 589832 | tf_op jit(solution)/shard_map/ppermute | solution.py:485
  68.4 1.6 %collective-permute-start.19 = (f32[4,96,128]{2,1,0:T(8,128)S(1)}, f32[4,96,128]{2,1,0:T(8,128)S(1)}, u32[]{:S(2)}, u32[]{:S(2)}) collective-permute-start(f32[4,96,128]{2,1,0:T(8,128)S(1)} %get-tuple-element.45), channel_id=1, source_target_pairs={{0,8},{8,0},{16,24},{24,16},{32,40},{40,32},{48,56},{56,48},{64,72... | collective-permute-start | bytes 589832 | tf_op jit(solution)/shard_map/ppermute | solution.py:485
  68.8 1.5 %collective-permute-start.20 = (f32[4,96,128]{2,1,0:T(8,128)S(1)}, f32[4,96,128]{2,1,0:T(8,128)S(1)}, u32[]{:S(2)}, u32[]{:S(2)}) collective-permute-start(f32[4,96,128]{2,1,0:T(8,128)S(1)} %get-tuple-element.46), channel_id=1, source_target_pairs={{0,8},{8,0},{16,24},{24,16},{32,40},{40,32},{48,56},{56,48},{64,72... | collective-permute-start | bytes 589832 | tf_op jit(solution)/shard_map/ppermute | solution.py:485
  68.9 7.6 %collective-permute-start.24 = (f32[4,96,128]{2,1,0:T(8,128)S(1)}, f32[4,96,128]{2,1,0:T(8,128)S(1)}, u32[]{:S(2)}, u32[]{:S(2)}) collective-permute-start(f32[4,96,128]{2,1,0:T(8,128)S(1)} %get-tuple-element.53), channel_id=1, source_target_pairs={{0,8},{8,0},{16,24},{24,16},{32,40},{40,32},{48,56},{56,48},{64,72... | collective-permute-start | bytes 589832 | tf_op jit(solution)/shard_map/ppermute | solution.py:485
  70.9 8.6 %collective-permute-start.26 = (f32[4,96,128]{2,1,0:T(8,128)S(1)}, f32[4,96,128]{2,1,0:T(8,128)S(1)}, u32[]{:S(2)}, u32[]{:S(2)}) collective-permute-start(f32[4,96,128]{2,1,0:T(8,128)S(1)} %get-tuple-element.54), channel_id=1, source_target_pairs={{0,32},{8,40},{16,48},{24,56},{32,0},{40,8},{48,16},{56,24},{64,96... | collective-permute-start | bytes 589832 | tf_op jit(solution)/shard_map/ppermute | solution.py:516
  73.2 28.4 %collective-permute-start.21 = (f32[2,384,128]{2,1,0:T(8,128)S(1)}, f32[2,384,128]{2,1,0:T(8,128)S(1)}, u32[]{:S(2)}, u32[]{:S(2)}) collective-permute-start(f32[2,384,128]{2,1,0:T(8,128)S(1)} %get-tuple-element.49), channel_id=1, source_target_pairs={{0,2},{1,3},{2,4},{3,5},{4,6},{5,7},{6,0},{7,1},{8,10},{9,11},{10,... | collective-permute-start | bytes 1179656 | tf_op jit(solution)/shard_map/ppermute | solution.py:518
  73.3 28.3 %collective-permute-start.22 = (f32[2,384,128]{2,1,0:T(8,128)S(1)}, f32[2,384,128]{2,1,0:T(8,128)S(1)}, u32[]{:S(2)}, u32[]{:S(2)}) collective-permute-start(f32[2,384,128]{2,1,0:T(8,128)S(1)} %get-tuple-element.50), channel_id=1, source_target_pairs={{0,4},{1,5},{2,6},{3,7},{4,0},{5,1},{6,2},{7,3},{8,12},{9,13},{10,... | collective-permute-start | bytes 1179656 | tf_op jit(solution)/shard_map/ppermute | solution.py:518
  75.8 25.8 %collective-permute-start.23 = (f32[2,384,128]{2,1,0:T(8,128)S(1)}, f32[2,384,128]{2,1,0:T(8,128)S(1)}, u32[]{:S(2)}, u32[]{:S(2)}) collective-permute-start(f32[2,384,128]{2,1,0:T(8,128)S(1)} %get-tuple-element.51), channel_id=1, source_target_pairs={{0,6},{1,7},{2,0},{3,1},{4,2},{5,3},{6,4},{7,5},{8,14},{9,15},{10,... | collective-permute-start | bytes 1179656 | tf_op jit(solution)/shard_map/ppermute | solution.py:518
  76.5 6.2 %collective-permute-start.27 = (f32[4,96,128]{2,1,0:T(8,128)S(1)}, f32[4,96,128]{2,1,0:T(8,128)S(1)}, u32[]{:S(2)}, u32[]{:S(2)}) collective-permute-start(f32[4,96,128]{2,1,0:T(8,128)S(1)} %get-tuple-element.55), channel_id=1, source_target_pairs={{0,48},{8,56},{16,0},{24,8},{32,16},{40,24},{48,32},{56,40},{64,11... | collective-permute-start | bytes 589832 | tf_op jit(solution)/shard_map/ppermute | solution.py:516
  79.5 7.4 %collective-permute-start.25 = (f32[4,96,128]{2,1,0:T(8,128)S(1)}, f32[4,96,128]{2,1,0:T(8,128)S(1)}, u32[]{:S(2)}, u32[]{:S(2)}) collective-permute-start(f32[4,96,128]{2,1,0:T(8,128)S(1)} %get-tuple-element.47.refs_1_), channel_id=1, source_target_pairs={{0,16},{8,24},{16,32},{24,40},{32,48},{40,56},{48,0},{56,8},{64,80... | collective-permute-start | bytes 589832 | tf_op jit(solution)/shard_map/ppermute | solution.py:516
  87.5 5.7 %collective-permute-start.28 = (f32[96,128]{1,0:T(8,128)S(1)}, f32[96,128]{1,0:T(8,128)S(1)}, u32[]{:S(2)}, u32[]{:S(2)}) collective-permute-start(f32[96,128]{1,0:T(8,128)S(1)} %get-tuple-element.57), channel_id=1, source_target_pairs={{0,64},{8,72},{16,80},{24,88},{32,96},{40,104},{48,112},{56,120},{... | collective-permute-start | bytes 147464 | tf_op jit(solution)/shard_map/ppermute | solution.py:520
  91.1 8.0 %collective-permute-start.29 = (f32[96,128]{1,0:T(8,128)S(1)}, f32[96,128]{1,0:T(8,128)S(1)}, u32[]{:S(2)}, u32[]{:S(2)}) collective-permute-start(f32[96,128]{1,0:T(8,128)S(1)} %get-tuple-element.58), channel_id=1, source_target_pairs={{0,128},{8,136},{16,144},{24,152},{32,160},{40,168},{48,176},{56,1... | collective-permute-start | bytes 147464 | tf_op jit(solution)/shard_map/ppermute | solution.py:520
  93.2 7.1 %collective-permute-start.30 = (f32[96,128]{1,0:T(8,128)S(1)}, f32[96,128]{1,0:T(8,128)S(1)}, u32[]{:S(2)}, u32[]{:S(2)}) collective-permute-start(f32[96,128]{1,0:T(8,128)S(1)} %get-tuple-element.59), channel_id=1, source_target_pairs={{0,192},{8,200},{16,208},{24,216},{32,224},{40,232},{48,240},{56,2... | collective-permute-start | bytes 147464 | tf_op jit(solution)/shard_map/ppermute | solution.py:520
  102.2 6.2 %collective-permute-start.31 = (f32[384,128]{1,0:T(8,128)S(1)}, f32[384,128]{1,0:T(8,128)S(1)}, u32[]{:S(2)}, u32[]{:S(2)}) collective-permute-start(f32[384,128]{1,0:T(8,128)S(1)} %get-tuple-element.61), channel_id=1, source_target_pairs={{0,1},{1,0},{2,3},{3,2},{4,5},{5,4},{6,7},{7,6},{8,9},{9,8},{10,11... | collective-permute-start | bytes 589832 | tf_op jit(solution)/shard_map/ppermute | solution.py:481
  102.5 10.2 %all-to-all-start.1 = ((f32[8,24,128]{2,1,0:T(8,128)}), f32[8,24,128]{2,1,0:T(8,128)S(1)}, u32[]{:S(2)}, u32[]{:S(2)}) async-start(f32[8,24,128]{2,1,0:T(8,128)} %shard_map.104.refs_4_), calls=%async_computation.1 | async-start | bytes 196608 | tf_op jit(solution)/shard_map/all_to_all | solution.py:531
  (10 other events, 402.2 us)

commit v6 on v5

--- a/solution.py
+++ b/solution.py
@@ -105,13 +105,19 @@
 
 
 def call(kernel, out_shape, owner, *arrays, after=(), scratch=(), flops=0, vmem=8):
-    specs = [pl.BlockSpec(memory_space=pltpu.SMEM)]
-    specs += [pl.BlockSpec(memory_space=pltpu.VMEM) for _ in arrays]
+    specs = [pl.BlockSpec(memory_space=pltpu.VMEM) for _ in arrays]
     specs += [pl.BlockSpec(memory_space=pl.ANY) for _ in after]
     size = sum(a.size for a in arrays) * 4
-
-    def body(owner_ref, *refs):
-        kernel(scalars(owner_ref), *refs)
+    operands = [*arrays, *after]
+    if owner is not None:
+        specs = [pl.BlockSpec(memory_space=pltpu.SMEM)] + specs
+        operands = [owner] + operands
+
+    def body(*refs):
+        if owner is None:
+            kernel(scalars(), *refs)
+        else:
+            kernel(scalars(refs[0]), *refs[1:])
 
     return pl.pallas_call(
         body,
@@ -120,7 +126,7 @@
         scratch_shapes=list(scratch),
         compiler_params=pltpu.CompilerParams(vmem_limit_bytes=vmem * 2**20),
         cost_estimate=pl.CostEstimate(flops=flops, bytes_accessed=2 * size, transcendentals=0),
-    )(owner, *arrays, *after)
+    )(*operands)
 
 
 MY_X, MY_C, MY_Z, X_STEP, C_OWN, Z_STEP, MY_Y, MY_PAIR = 0, 1, 2, 3, 5, 7, 9, 10
@@ -131,11 +137,11 @@
     return me // 2, lax.rem(me, 2)
 
 
-def scalars(owner):
+def scalars(owner=None):
     me = lax.axis_index("band")
     x, c, z = lax.rem(me // 2, 4), lax.rem(me, 2), me // 8
     values = [x, c, z, 0, 0, 0, 0, 0, 0, *divide_grid()]
-    for step in range(2):
+    for step in range(2 if owner is not None else 0):
         band = jnp.clip(owner[step], 0, BAND - 1)
         values[X_STEP + step] = lax.rem(x + 4 - lax.rem(band // 2, 4), 4)
         values[C_OWN + step] = (c == lax.rem(band, 2)).astype(jnp.int32)
@@ -379,7 +385,7 @@
         stage(r, info, scale)
 
 
-def fields(block_owner, slabs, pieces, scale):
+def fields(slabs, pieces, scale):
     def body(*refs):
         field_kernel(scale, *refs)
 
@@ -387,7 +393,7 @@
     return call(
         body,
         [shape(8, ROWS, LANES)] + [shape(4, PACK, LANES)] * 8,
-        block_owner,
+        None,
         *slabs,
         *pieces,
         *[jnp.asarray(t) for t in tables()],
@@ -451,7 +457,7 @@
         out_ref[at[0], at[1], 8:9, LANES:SHARE] = total[17:18, :REST]
 
 
-def add_y_kernel(info, s_ref, r1, r2, r3, after_ref, stay_ref, cross_ref):
+def add_y_kernel(info, s_ref, r1, r2, r3, stay_ref, cross_ref):
     for j, ref in enumerate((stay_ref, cross_ref)):
         ref[...] = s_ref[j] + r1[j] + r2[j] + r3[j]
 
@@ -491,11 +497,11 @@
     stay, cross, *quarters = call(
         pack_kernel,
         [slab, slab] + [shape(2, QUARTER, LANES)] * 4,
-        block_owner,
+        None,
         orbitals,
         scratch=[pltpu.VMEM((2, ROWS, LANES), F32)],
     )
-    pair = call(join_kernel, shape(2, ROWS, LANES), block_owner, stay, other_slab(cross))
+    pair = call(join_kernel, shape(2, ROWS, LANES), None, stay, other_slab(cross))
     slabs = [pair] + [lax.ppermute(pair, "grid", shift_y(d)) for d in (1, 3)]
     slabs.insert(2, lax.ppermute(slabs[1], "grid", shift_y(1)))
 
@@ -509,28 +515,28 @@
     pieces = [piece] + [lax.ppermute(piece, "band", shift_x(d)) for d in (1, 2, 3)]
     pieces = pieces + [other_core(p) for p in pieces]
 
-    own, *shares = fields(block_owner, slabs, pieces, scale)
+    own, *shares = fields(slabs, pieces, scale)
     kept, got = shares[:4], [other_core(g) for g in shares[4:]]
     part = shape(4, PACK, LANES)
-    added = call(add_core_kernel, [part] * 3, block_owner, *kept[1:], *got[1:])
+    added = call(add_core_kernel, [part] * 3, None, *kept[1:], *got[1:])
     moved = [lax.ppermute(added[d - 1], "band", shift_x(d)) for d in (1, 2, 3)]
-    sent = call(send_kernel, [shape(2, ROWS, LANES)] * 4, block_owner, own, after=added[:1])
+    sent = call(send_kernel, [shape(2, ROWS, LANES)] * 4, None, own, after=added[:1])
     sent = [sent[0]] + [lax.ppermute(sent[d], "grid", shift_y(d)) for d in (1, 2, 3)]
-    sums = call(add_x_kernel, [shape(PACK, LANES)] * 4, block_owner, kept[0], got[0], *moved)
+    sums = call(add_x_kernel, [shape(PACK, LANES)] * 4, None, kept[0], got[0], *moved)
     moved = [lax.ppermute(sums[d], "band", shift_z(d)) for d in (1, 2, 3)]
     slabs = call(
         add_z_kernel,
         shape(8, PART, LANES),
-        block_owner,
+        None,
         sums[0],
         *moved,
         scratch=[pltpu.VMEM((PACK, LANES), F32)],
     )
-    stay, cross = call(add_y_kernel, [slab, slab], block_owner, *sent, after=[slabs])
-    field = call(own_kernel, shape(2, SLAB, PLANE), block_owner, stay, other_slab(cross))
+    stay, cross = call(add_y_kernel, [slab, slab], None, *sent)
+    field = call(own_kernel, shape(2, SLAB, PLANE), None, stay, other_slab(cross))
     slabs = lax.all_to_all(slabs, "grid", 0, 0)
     block_field = call(
-        share_kernel, shape(2, 2, SLAB, SHARE), block_owner, slabs, after=[field]
+        share_kernel, shape(2, 2, SLAB, SHARE), None, slabs, after=[field]
     )
     return field, block_field
 

time: 114 us -> 109 us (0.956)
  the two profiles are of different devices: /device:TPU:64 before, /device:TPU:2 now
where the time goes in v6:
time: 109 us; the launch traced here: 107 us
  starting transfers between devices  56.5 us (52%)
  waiting for transfers between devices  35.6 us (33%)
  Pallas kernels  11.9 us (11%)
  local copies, waits for them, and re-layouts  2.68 us (2%)
    pallas_call x13, Pallas kernels, call(): pl.pallas_call(body, in_specs=specs, out_shape=out_shape, scratch_shapes=...  11.9 us
    ppermute x3, starting transfers between devices, on_device(): moved = [lax.ppermute(sums[d], 'band', shift_z(d)) for d in (1, 2, 3)]  10.6 us
    ppermute x3, starting transfers between devices, on_device(): along = [mine] + [lax.ppermute(mine, 'band', shift_z(d)) for d in (1, 2, 3)]  9.51 us
    ppermute x3, waiting for transfers between devices, on_device(): along = [mine] + [lax.ppermute(mine, 'band', shift_z(d)) for d in (1, 2, 3)]  6.7 us
    ppermute x3, waiting for transfers between devices, on_device(): moved = [lax.ppermute(added[d - 1], 'band', shift_x(d)) for d in (1, 2, 3)]  5.95 us
    ppermute x3, starting transfers between devices, on_device(): moved = [lax.ppermute(added[d - 1], 'band', shift_x(d)) for d in (1, 2, 3)]  5.5 us
    all_to_all x1, waiting for transfers between devices, on_device(): slabs = lax.all_to_all(slabs, 'grid', 0, 0)  5.46 us
    ppermute x3, waiting for transfers between devices, on_device(): lax.ppermute(piece, 'band', shift_x(d))  5.24 us
  transfers between devices with their start and end apart: 34, of which 19 were waited for; matrix products, arithmetic and copies ran while one was open for 1% of the time, Pallas kernels for 3%

profile of v6, /device:TPU:2, one launch (start us, length us, event | category | flops | bytes accessed | tf_op | source)
XLA Modules:
  0.0 107.5 jit_solution(166858436732539393)
XLA Ops:
  1.9 1.6 %collective-permute-start.4 = (f32[2,96,128]{2,1,0:T(8,128)S(1)}, f32[2,96,128]{2,1,0:T(8,128)S(1)}, u32[]{:S(2)}, u32[]{:S(2)}) collective-permute-start(f32[2,96,128]{2,1,0:T(8,128)S(1)} %get-tuple-element.35), channel_id=1, source_target_pairs={{0,16},{8,24},{16,32},{24,40},{32,48},{40,56},{48,0},{56,8},{64,80... | collective-permute-start | bytes 294920 | tf_op jit(solution)/shard_map/ppermute | solution.py:508
  3.5 2.8 %collective-permute-start.5 = (f32[2,96,128]{2,1,0:T(8,128)S(1)}, f32[2,96,128]{2,1,0:T(8,128)S(1)}, u32[]{:S(2)}, u32[]{:S(2)}) collective-permute-start(f32[2,96,128]{2,1,0:T(8,128)S(1)} %get-tuple-element.36), channel_id=1, source_target_pairs={{0,32},{8,40},{16,48},{24,56},{32,0},{40,8},{48,16},{56,24},{64,96... | collective-permute-start | bytes 294920 | tf_op jit(solution)/shard_map/ppermute | solution.py:508
  6.7 1.9 %collective-permute-start = (f32[384,128]{1,0:T(8,128)S(1)}, f32[384,128]{1,0:T(8,128)S(1)}, u32[]{:S(2)}, u32[]{:S(2)}) collective-permute-start(f32[384,128]{1,0:T(8,128)S(1)} %get-tuple-element.33), channel_id=1, source_target_pairs={{0,1},{1,0},{2,3},{3,2},{4,5},{5,4},{6,7},{7,6},{8,9},{9,8},{10,11... | collective-permute-start | bytes 589832 | tf_op jit(solution)/shard_map/ppermute | solution.py:487
  8.6 1.7 %collective-permute-done.5.refs_3_ = f32[2,96,128]{2,1,0:T(8,128)S(1)} collective-permute-done((f32[2,96,128]{2,1,0:T(8,128)S(1)}, f32[2,96,128]{2,1,0:T(8,128)S(1)}, u32[]{:S(2)}, u32[]{:S(2)}) %collective-permute-start.5) | collective-permute-done | bytes 98336 | tf_op jit(solution)/shard_map/ppermute | solution.py:508
  12.0 1.3 %collective-permute-done.7.refs_2_ = f32[4,48,128]{2,1,0:T(8,128)S(1)} collective-permute-done((f32[4,48,128]{2,1,0:T(8,128)S(1)}, f32[4,48,128]{2,1,0:T(8,128)S(1)}, u32[]{:S(2)}, u32[]{:S(2)}) %collective-permute-start.7) | collective-permute-done | bytes 98336 | tf_op jit(solution)/shard_map/ppermute | solution.py:491
  13.9 5.7 %collective-permute-start.10 = (f32[4,48,128]{2,1,0:T(8,128)S(1)}, f32[4,48,128]{2,1,0:T(8,128)S(1)}, u32[]{:S(2)}, u32[]{:S(2)}) collective-permute-start(f32[4,48,128]{2,1,0:T(8,128)S(1)} %shard_map.98.refs_1_), channel_id=1, source_target_pairs={{0,192},{8,200},{16,208},{24,216},{32,224},{40,232},{48,240},{56,2... | collective-permute-start | bytes 294920 | tf_op jit(solution)/shard_map/ppermute | solution.py:512
  20.6 2.8 %collective-permute-start.8 = (f32[4,48,128]{2,1,0:T(8,128)S(1)}, f32[4,48,128]{2,1,0:T(8,128)S(1)}, u32[]{:S(2)}, u32[]{:S(2)}) collective-permute-start(f32[4,48,128]{2,1,0:T(8,128)S(1)} %shard_map.98.refs_1_), channel_id=1, source_target_pairs={{0,64},{8,72},{16,80},{24,88},{32,96},{40,104},{48,112},{56,120},{... | collective-permute-start | bytes 294920 | tf_op jit(solution)/shard_map/ppermute | solution.py:512
  23.4 1.7 %collective-permute-start.1 = (f32[2,384,128]{2,1,0:T(8,128)S(1)}, f32[2,384,128]{2,1,0:T(8,128)S(1)}, u32[]{:S(2)}, u32[]{:S(2)}) collective-permute-start(f32[2,384,128]{2,1,0:T(8,128)S(1)} %shard_map.96.refs_0_), channel_id=1, source_target_pairs={{0,2},{1,3},{2,4},{3,5},{4,6},{5,7},{6,0},{7,1},{8,10},{9,11},{10,... | collective-permute-start | bytes 1179656 | tf_op jit(solution)/shard_map/ppermute | solution.py:505
  25.1 3.2 %collective-permute-done.10.refs_4_ = f32[4,48,128]{2,1,0:T(8,128)S(1)} collective-permute-done((f32[4,48,128]{2,1,0:T(8,128)S(1)}, f32[4,48,128]{2,1,0:T(8,128)S(1)}, u32[]{:S(2)}, u32[]{:S(2)}) %collective-permute-start.10) | collective-permute-done | bytes 98336 | tf_op jit(solution)/shard_map/ppermute | solution.py:512
  28.3 3.5 %collective-permute-done.9.refs_3_ = f32[4,48,128]{2,1,0:T(8,128)S(1)} collective-permute-done((f32[4,48,128]{2,1,0:T(8,128)S(1)}, f32[4,48,128]{2,1,0:T(8,128)S(1)}, u32[]{:S(2)}, u32[]{:S(2)}) %collective-permute-start.9) | collective-permute-done | bytes 98336 | tf_op jit(solution)/shard_map/ppermute | solution.py:512
  31.8 1.3 %shard_map.99 = f32[8,48,128]{2,1,0:T(8,128)} custom-call(s32[2]{0:T(128)S(1)} %copy-done, f32[4,48,128]{2,1,0:T(8,128)S(1)} %shard_map.98.refs_1_, f32[4,48,128]{2,1,0:T(8,128)S(1)} %collective-permute-done.8.refs_2_, f32[4,48,128]{2,1,0:T(8,128)S(1)} %collective-permute-done.9.refs_3_, f32[4,48,128]{2,1,0:T(8,128)S(1)} %collective-permute-done.10.refs_4_), custom_call_target="tpu_custom_call" | custom-call | bytes 786432 | tf_op jit(solution)/shard_map/pallas_call | solution.py:122
  33.1 4.5 %all-to-all-start = ((f32[8,48,128]{2,1,0:T(8,128)}), f32[8,48,128]{2,1,0:T(8,128)S(1)}, u32[]{:S(2)}, u32[]{:S(2)}) async-start(f32[8,48,128]{2,1,0:T(8,128)} %shard_map.99), calls=%async_computation | async-start | bytes 393216 | tf_op jit(solution)/shard_map/all_to_all | solution.py:514
  37.5 3.2 %collective-permute-start.3 = (f32[2,384,128]{2,1,0:T(8,128)S(1)}, f32[2,384,128]{2,1,0:T(8,128)S(1)}, u32[]{:S(2)}, u32[]{:S(2)}) collective-permute-start(f32[2,384,128]{2,1,0:T(8,128)S(1)} %shard_map.96.refs_0_), channel_id=1, source_target_pairs={{0,6},{1,7},{2,0},{3,1},{4,2},{5,3},{6,4},{7,5},{8,14},{9,15},{10,... | collective-permute-start | bytes 1179656 | tf_op jit(solution)/shard_map/ppermute | solution.py:505
  40.8 3.7 %all-to-all-done.refs_4_ = f32[8,48,128]{2,1,0:T(8,128)S(1)} async-done(((f32[8,48,128]{2,1,0:T(8,128)}), f32[8,48,128]{2,1,0:T(8,128)S(1)}, u32[]{:S(2)}, u32[]{:S(2)}) %all-to-all-start) | async-done | bytes 196640 | tf_op jit(solution)/shard_map/all_to_all | solution.py:514
  45.2 2.1 %collective-permute-start.12 = (f32[8,48,128]{2,1,0:T(8,128)S(1)}, f32[8,48,128]{2,1,0:T(8,128)S(1)}, u32[]{:S(2)}, u32[]{:S(2)}) collective-permute-start(f32[8,48,128]{2,1,0:T(8,128)S(1)} %all-to-all-done.refs_4_), channel_id=1, source_target_pairs={{0,32},{8,40},{16,48},{24,56},{32,0},{40,8},{48,16},{56,24},{64,96... | collective-permute-start | bytes 589832 | tf_op jit(solution)/shard_map/ppermute | solution.py:515
  47.7 2.1 %collective-permute-start.11 = (f32[8,48,128]{2,1,0:T(8,128)S(1)}, f32[8,48,128]{2,1,0:T(8,128)S(1)}, u32[]{:S(2)}, u32[]{:S(2)}) collective-permute-start(f32[8,48,128]{2,1,0:T(8,128)S(1)} %all-to-all-done.refs_4_), channel_id=1, source_target_pairs={{0,16},{8,24},{16,32},{24,40},{32,48},{40,56},{48,0},{56,8},{64,80... | collective-permute-start | bytes 589832 | tf_op jit(solution)/shard_map/ppermute | solution.py:515
  49.8 2.1 %collective-permute-done.13.refs_7_ = f32[8,48,128]{2,1,0:T(8,128)S(1)} collective-permute-done((f32[8,48,128]{2,1,0:T(8,128)S(1)}, f32[8,48,128]{2,1,0:T(8,128)S(1)}, u32[]{:S(2)}, u32[]{:S(2)}) %collective-permute-start.13) | collective-permute-done | bytes 196640 | tf_op jit(solution)/shard_map/ppermute | solution.py:515
  51.9 2.1 %collective-permute-done.12.refs_6_ = f32[8,48,128]{2,1,0:T(8,128)S(1)} collective-permute-done((f32[8,48,128]{2,1,0:T(8,128)S(1)}, f32[8,48,128]{2,1,0:T(8,128)S(1)}, u32[]{:S(2)}, u32[]{:S(2)}) %collective-permute-start.12) | collective-permute-done | bytes 196640 | tf_op jit(solution)/shard_map/ppermute | solution.py:515
  55.0 1.6 %collective-permute-done.2.refs_2_ = f32[2,384,128]{2,1,0:T(8,128)S(1)} collective-permute-done((f32[2,384,128]{2,1,0:T(8,128)S(1)}, f32[2,384,128]{2,1,0:T(8,128)S(1)}, u32[]{:S(2)}, u32[]{:S(2)}) %collective-permute-start.2) | collective-permute-done | bytes 393248 | tf_op jit(solution)/shard_map/ppermute | solution.py:506
  56.7 8.3 %shard_map.100 = (f32[8,384,128]{2,1,0:T(8,128)S(1)}, f32[4,96,128]{2,1,0:T(8,128)S(1)}, f32[4,96,128]{2,1,0:T(8,128)S(1)}, f32[4,96,128]{2,1,0:T(8,128)S(1)}, f...) custom-call(f32[2,384,128]{2,1,0:T(8,128)S(1)} %shard_map.96.refs_0_, ...), custom_call_target="tpu_custom_call" | custom-call | flops 10000000000 | bytes 8454144 | tf_op jit(solution)/shard_map/pallas_call | solution.py:122
  67.1 2.1 %collective-permute-start.27 = (f32[4,96,128]{2,1,0:T(8,128)S(1)}, f32[4,96,128]{2,1,0:T(8,128)S(1)}, u32[]{:S(2)}, u32[]{:S(2)}) collective-permute-start(f32[4,96,128]{2,1,0:T(8,128)S(1)} %get-tuple-element.56), channel_id=1, source_target_pairs={{0,32},{8,40},{16,48},{24,56},{32,0},{40,8},{48,16},{56,24},{64,96... | collective-permute-start | bytes 589832 | tf_op jit(solution)/shard_map/ppermute | solution.py:522
  69.8 2.0 %collective-permute-start.22 = (f32[2,384,128]{2,1,0:T(8,128)S(1)}, f32[2,384,128]{2,1,0:T(8,128)S(1)}, u32[]{:S(2)}, u32[]{:S(2)}) collective-permute-start(f32[2,384,128]{2,1,0:T(8,128)S(1)} %get-tuple-element.50), channel_id=1, source_target_pairs={{0,4},{1,5},{2,6},{3,7},{4,0},{5,1},{6,2},{7,3},{8,12},{9,13},{10,... | collective-permute-start | bytes 1179656 | tf_op jit(solution)/shard_map/ppermute | solution.py:524
  71.8 1.6 %collective-permute-start.23 = (f32[2,384,128]{2,1,0:T(8,128)S(1)}, f32[2,384,128]{2,1,0:T(8,128)S(1)}, u32[]{:S(2)}, u32[]{:S(2)}) collective-permute-start(f32[2,384,128]{2,1,0:T(8,128)S(1)} %get-tuple-element.51), channel_id=1, source_target_pairs={{0,6},{1,7},{2,0},{3,1},{4,2},{5,3},{6,4},{7,5},{8,14},{9,15},{10,... | collective-permute-start | bytes 1179656 | tf_op jit(solution)/shard_map/ppermute | solution.py:524
  73.5 1.4 %collective-permute-start.28 = (f32[4,96,128]{2,1,0:T(8,128)S(1)}, f32[4,96,128]{2,1,0:T(8,128)S(1)}, u32[]{:S(2)}, u32[]{:S(2)}) collective-permute-start(f32[4,96,128]{2,1,0:T(8,128)S(1)} %get-tuple-element.57), channel_id=1, source_target_pairs={{0,48},{8,56},{16,0},{24,8},{32,16},{40,24},{48,32},{56,40},{64,11... | collective-permute-start | bytes 589832 | tf_op jit(solution)/shard_map/ppermute | solution.py:522
  75.8 2.0 %collective-permute-start.26 = (f32[4,96,128]{2,1,0:T(8,128)S(1)}, f32[4,96,128]{2,1,0:T(8,128)S(1)}, u32[]{:S(2)}, u32[]{:S(2)}) collective-permute-start(f32[4,96,128]{2,1,0:T(8,128)S(1)} %get-tuple-element.47.refs_1_), channel_id=1, source_target_pairs={{0,16},{8,24},{16,32},{24,40},{32,48},{40,56},{48,0},{56,8},{64,80... | collective-permute-start | bytes 589832 | tf_op jit(solution)/shard_map/ppermute | solution.py:522
  77.8 2.2 %collective-permute-done.28.refs_4_ = f32[4,96,128]{2,1,0:T(8,128)S(1)} collective-permute-done((f32[4,96,128]{2,1,0:T(8,128)S(1)}, f32[4,96,128]{2,1,0:T(8,128)S(1)}, u32[]{:S(2)}, u32[]{:S(2)}) %collective-permute-start.28) | collective-permute-done | bytes 196640 | tf_op jit(solution)/shard_map/ppermute | solution.py:522
  80.0 2.8 %collective-permute-done.26.refs_2_ = f32[4,96,128]{2,1,0:T(8,128)S(1)} collective-permute-done((f32[4,96,128]{2,1,0:T(8,128)S(1)}, f32[4,96,128]{2,1,0:T(8,128)S(1)}, u32[]{:S(2)}, u32[]{:S(2)}) %collective-permute-start.26) | collective-permute-done | bytes 196640 | tf_op jit(solution)/shard_map/ppermute | solution.py:522
  82.8 2.8 %collective-permute-start.29 = (f32[96,128]{1,0:T(8,128)S(1)}, f32[96,128]{1,0:T(8,128)S(1)}, u32[]{:S(2)}, u32[]{:S(2)}) collective-permute-start(f32[96,128]{1,0:T(8,128)S(1)} %get-tuple-element.59), channel_id=1, source_target_pairs={{0,64},{8,72},{16,80},{24,88},{32,96},{40,104},{48,112},{56,120},{... | collective-permute-start | bytes 147464 | tf_op jit(solution)/shard_map/ppermute | solution.py:526
  85.6 3.7 %collective-permute-start.30 = (f32[96,128]{1,0:T(8,128)S(1)}, f32[96,128]{1,0:T(8,128)S(1)}, u32[]{:S(2)}, u32[]{:S(2)}) collective-permute-start(f32[96,128]{1,0:T(8,128)S(1)} %get-tuple-element.60), channel_id=1, source_target_pairs={{0,128},{8,136},{16,144},{24,152},{32,160},{40,168},{48,176},{56,1... | collective-permute-start | bytes 147464 | tf_op jit(solution)/shard_map/ppermute | solution.py:526
  90.1 4.0 %collective-permute-start.31 = (f32[96,128]{1,0:T(8,128)S(1)}, f32[96,128]{1,0:T(8,128)S(1)}, u32[]{:S(2)}, u32[]{:S(2)}) collective-permute-start(f32[96,128]{1,0:T(8,128)S(1)} %get-tuple-element.61), channel_id=1, source_target_pairs={{0,192},{8,200},{16,208},{24,216},{32,224},{40,232},{48,240},{56,2... | collective-permute-start | bytes 147464 | tf_op jit(solution)/shard_map/ppermute | solution.py:526
  97.0 3.4 %all-to-all-start.1 = ((f32[8,24,128]{2,1,0:T(8,128)}), f32[8,24,128]{2,1,0:T(8,128)S(1)}, u32[]{:S(2)}, u32[]{:S(2)}) async-start(f32[8,24,128]{2,1,0:T(8,128)} %shard_map.106), calls=%async_computation.1 | async-start | bytes 196608 | tf_op jit(solution)/shard_map/all_to_all | solution.py:537
  101.3 5.5 %all-to-all-done.1.refs_0_ = f32[8,24,128]{2,1,0:T(8,128)S(1)} async-done(((f32[8,24,128]{2,1,0:T(8,128)}), f32[8,24,128]{2,1,0:T(8,128)S(1)}, u32[]{:S(2)}, u32[]{:S(2)}) %all-to-all-start.1) | async-done | bytes 98336 | tf_op jit(solution)/shard_map/all_to_all | solution.py:537
  (66 shorter events, 16.0 us)
Async XLA Ops:
  1.9 6.8 %collective-permute-start.4 = (f32[2,96,128]{2,1,0:T(8,128)S(1)}, f32[2,96,128]{2,1,0:T(8,128)S(1)}, u32[]{:S(2)}, u32[]{:S(2)}) collective-permute-start(f32[2,96,128]{2,1,0:T(8,128)S(1)} %get-tuple-element.35), channel_id=1, source_target_pairs={{0,16},{8,24},{16,32},{24,40},{32,48},{40,56},{48,0},{56,8},{64,80... | collective-permute-start | bytes 294920 | tf_op jit(solution)/shard_map/ppermute | solution.py:508
  3.5 6.9 %collective-permute-start.5 = (f32[2,96,128]{2,1,0:T(8,128)S(1)}, f32[2,96,128]{2,1,0:T(8,128)S(1)}, u32[]{:S(2)}, u32[]{:S(2)}) collective-permute-start(f32[2,96,128]{2,1,0:T(8,128)S(1)} %get-tuple-element.36), channel_id=1, source_target_pairs={{0,32},{8,40},{16,48},{24,56},{32,0},{40,8},{48,16},{56,24},{64,96... | collective-permute-start | bytes 294920 | tf_op jit(solution)/shard_map/ppermute | solution.py:508
  6.3 5.0 %collective-permute-start.6 = (f32[2,96,128]{2,1,0:T(8,128)S(1)}, f32[2,96,128]{2,1,0:T(8,128)S(1)}, u32[]{:S(2)}, u32[]{:S(2)}) collective-permute-start(f32[2,96,128]{2,1,0:T(8,128)S(1)} %get-tuple-element.37), channel_id=1, source_target_pairs={{0,48},{8,56},{16,0},{24,8},{32,16},{40,24},{48,32},{56,40},{64,11... | collective-permute-start | bytes 294920 | tf_op jit(solution)/shard_map/ppermute | solution.py:508
  6.7 16.7 %collective-permute-start = (f32[384,128]{1,0:T(8,128)S(1)}, f32[384,128]{1,0:T(8,128)S(1)}, u32[]{:S(2)}, u32[]{:S(2)}) collective-permute-start(f32[384,128]{1,0:T(8,128)S(1)} %get-tuple-element.33), channel_id=1, source_target_pairs={{0,1},{1,0},{2,3},{3,2},{4,5},{5,4},{6,7},{7,6},{8,9},{9,8},{10,11... | collective-permute-start | bytes 589832 | tf_op jit(solution)/shard_map/ppermute | solution.py:487
  13.9 14.4 %collective-permute-start.10 = (f32[4,48,128]{2,1,0:T(8,128)S(1)}, f32[4,48,128]{2,1,0:T(8,128)S(1)}, u32[]{:S(2)}, u32[]{:S(2)}) collective-permute-start(f32[4,48,128]{2,1,0:T(8,128)S(1)} %shard_map.98.refs_1_), channel_id=1, source_target_pairs={{0,192},{8,200},{16,208},{24,216},{32,224},{40,232},{48,240},{56,2... | collective-permute-start | bytes 294920 | tf_op jit(solution)/shard_map/ppermute | solution.py:512
  19.6 12.2 %collective-permute-start.9 = (f32[4,48,128]{2,1,0:T(8,128)S(1)}, f32[4,48,128]{2,1,0:T(8,128)S(1)}, u32[]{:S(2)}, u32[]{:S(2)}) collective-permute-start(f32[4,48,128]{2,1,0:T(8,128)S(1)} %shard_map.98.refs_1_), channel_id=1, source_target_pairs={{0,128},{8,136},{16,144},{24,152},{32,160},{40,168},{48,176},{56,1... | collective-permute-start | bytes 294920 | tf_op jit(solution)/shard_map/ppermute | solution.py:512
  20.6 11.2 %collective-permute-start.8 = (f32[4,48,128]{2,1,0:T(8,128)S(1)}, f32[4,48,128]{2,1,0:T(8,128)S(1)}, u32[]{:S(2)}, u32[]{:S(2)}) collective-permute-start(f32[4,48,128]{2,1,0:T(8,128)S(1)} %shard_map.98.refs_1_), channel_id=1, source_target_pairs={{0,64},{8,72},{16,80},{24,88},{32,96},{40,104},{48,112},{56,120},{... | collective-permute-start | bytes 294920 | tf_op jit(solution)/shard_map/ppermute | solution.py:512
  23.4 23.8 %collective-permute-start.1 = (f32[2,384,128]{2,1,0:T(8,128)S(1)}, f32[2,384,128]{2,1,0:T(8,128)S(1)}, u32[]{:S(2)}, u32[]{:S(2)}) collective-permute-start(f32[2,384,128]{2,1,0:T(8,128)S(1)} %shard_map.96.refs_0_), channel_id=1, source_target_pairs={{0,2},{1,3},{2,4},{3,5},{4,6},{5,7},{6,0},{7,1},{8,10},{9,11},{10,... | collective-permute-start | bytes 1179656 | tf_op jit(solution)/shard_map/ppermute | solution.py:505
  33.1 11.4 %all-to-all-start = ((f32[8,48,128]{2,1,0:T(8,128)}), f32[8,48,128]{2,1,0:T(8,128)S(1)}, u32[]{:S(2)}, u32[]{:S(2)}) async-start(f32[8,48,128]{2,1,0:T(8,128)} %shard_map.99), calls=%async_computation | async-start | bytes 393216 | tf_op jit(solution)/shard_map/all_to_all | solution.py:514
  37.5 12.2 %collective-permute-start.3 = (f32[2,384,128]{2,1,0:T(8,128)S(1)}, f32[2,384,128]{2,1,0:T(8,128)S(1)}, u32[]{:S(2)}, u32[]{:S(2)}) collective-permute-start(f32[2,384,128]{2,1,0:T(8,128)S(1)} %shard_map.96.refs_0_), channel_id=1, source_target_pairs={{0,6},{1,7},{2,0},{3,1},{4,2},{5,3},{6,4},{7,5},{8,14},{9,15},{10,... | collective-permute-start | bytes 1179656 | tf_op jit(solution)/shard_map/ppermute | solution.py:505
  44.5 7.4 %collective-permute-start.13 = (f32[8,48,128]{2,1,0:T(8,128)S(1)}, f32[8,48,128]{2,1,0:T(8,128)S(1)}, u32[]{:S(2)}, u32[]{:S(2)}) collective-permute-start(f32[8,48,128]{2,1,0:T(8,128)S(1)} %all-to-all-done.refs_4_), channel_id=1, source_target_pairs={{0,48},{8,56},{16,0},{24,8},{32,16},{40,24},{48,32},{56,40},{64,11... | collective-permute-start | bytes 589832 | tf_op jit(solution)/shard_map/ppermute | solution.py:515
  45.2 8.8 %collective-permute-start.12 = (f32[8,48,128]{2,1,0:T(8,128)S(1)}, f32[8,48,128]{2,1,0:T(8,128)S(1)}, u32[]{:S(2)}, u32[]{:S(2)}) collective-permute-start(f32[8,48,128]{2,1,0:T(8,128)S(1)} %all-to-all-done.refs_4_), channel_id=1, source_target_pairs={{0,32},{8,40},{16,48},{24,56},{32,0},{40,8},{48,16},{56,24},{64,96... | collective-permute-start | bytes 589832 | tf_op jit(solution)/shard_map/ppermute | solution.py:515
  47.2 9.4 %collective-permute-start.2 = (f32[2,384,128]{2,1,0:T(8,128)S(1)}, f32[2,384,128]{2,1,0:T(8,128)S(1)}, u32[]{:S(2)}, u32[]{:S(2)}) collective-permute-start(f32[2,384,128]{2,1,0:T(8,128)S(1)} %collective-permute-done.1.refs_1_), channel_id=1, source_target_pairs={{0,2},{1,3},{2,4},{3,5},{4,6},{5,7},{6,0},{7,1},{8,10},{9,11},{10,... | collective-permute-start | bytes 1179656 | tf_op jit(solution)/shard_map/ppermute | solution.py:506
  47.7 7.3 %collective-permute-start.11 = (f32[8,48,128]{2,1,0:T(8,128)S(1)}, f32[8,48,128]{2,1,0:T(8,128)S(1)}, u32[]{:S(2)}, u32[]{:S(2)}) collective-permute-start(f32[8,48,128]{2,1,0:T(8,128)S(1)} %all-to-all-done.refs_4_), channel_id=1, source_target_pairs={{0,16},{8,24},{16,32},{24,40},{32,48},{40,56},{48,0},{56,8},{64,80... | collective-permute-start | bytes 589832 | tf_op jit(solution)/shard_map/ppermute | solution.py:515
  49.8 5.3 %collective-permute-start.14 = (f32[8,48,128]{2,1,0:T(8,128)S(1)}, f32[8,48,128]{2,1,0:T(8,128)S(1)}, u32[]{:S(2)}, u32[]{:S(2)}) collective-permute-start(f32[8,48,128]{2,1,0:T(8,128)S(1)} %all-to-all-done.refs_4_), channel_id=1, source_target_pairs={{0,8},{8,0},{16,24},{24,16},{32,40},{40,32},{48,56},{56,48},{64,72... | collective-permute-start | bytes 589832 | tf_op jit(solution)/shard_map/ppermute | solution.py:491
  51.9 4.8 %collective-permute-start.17 = (f32[8,48,128]{2,1,0:T(8,128)S(1)}, f32[8,48,128]{2,1,0:T(8,128)S(1)}, u32[]{:S(2)}, u32[]{:S(2)}) collective-permute-start(f32[8,48,128]{2,1,0:T(8,128)S(1)} %collective-permute-done.13.refs_7_), channel_id=1, source_target_pairs={{0,8},{8,0},{16,24},{24,16},{32,40},{40,32},{48,56},{56,48},{64,72... | collective-permute-start | bytes 589832 | tf_op jit(solution)/shard_map/ppermute | solution.py:491
  54.0 2.7 %collective-permute-start.16 = (f32[8,48,128]{2,1,0:T(8,128)S(1)}, f32[8,48,128]{2,1,0:T(8,128)S(1)}, u32[]{:S(2)}, u32[]{:S(2)}) collective-permute-start(f32[8,48,128]{2,1,0:T(8,128)S(1)} %collective-permute-done.12.refs_6_), channel_id=1, source_target_pairs={{0,8},{8,0},{16,24},{24,16},{32,40},{40,32},{48,56},{56,48},{64,72... | collective-permute-start | bytes 589832 | tf_op jit(solution)/shard_map/ppermute | solution.py:491
  55.0 1.6 %collective-permute-start.15 = (f32[8,48,128]{2,1,0:T(8,128)S(1)}, f32[8,48,128]{2,1,0:T(8,128)S(1)}, u32[]{:S(2)}, u32[]{:S(2)}) collective-permute-start(f32[8,48,128]{2,1,0:T(8,128)S(1)} %collective-permute-done.11.refs_5_), channel_id=1, source_target_pairs={{0,8},{8,0},{16,24},{24,16},{32,40},{40,32},{48,56},{56,48},{64,72... | collective-permute-start | bytes 589832 | tf_op jit(solution)/shard_map/ppermute | solution.py:491
  65.0 1.5 %collective-permute-start.18 = (f32[4,96,128]{2,1,0:T(8,128)S(1)}, f32[4,96,128]{2,1,0:T(8,128)S(1)}, u32[]{:S(2)}, u32[]{:S(2)}) collective-permute-start(f32[4,96,128]{2,1,0:T(8,128)S(1)} %get-tuple-element.44), channel_id=1, source_target_pairs={{0,8},{8,0},{16,24},{24,16},{32,40},{40,32},{48,56},{56,48},{64,72... | collective-permute-start | bytes 589832 | tf_op jit(solution)/shard_map/ppermute | solution.py:491
  65.1 1.7 %collective-permute-start.19 = (f32[4,96,128]{2,1,0:T(8,128)S(1)}, f32[4,96,128]{2,1,0:T(8,128)S(1)}, u32[]{:S(2)}, u32[]{:S(2)}) collective-permute-start(f32[4,96,128]{2,1,0:T(8,128)S(1)} %get-tuple-element.45), channel_id=1, source_target_pairs={{0,8},{8,0},{16,24},{24,16},{32,40},{40,32},{48,56},{56,48},{64,72... | collective-permute-start | bytes 589832 | tf_op jit(solution)/shard_map/ppermute | solution.py:491
  65.7 7.8 %collective-permute-start.25 = (f32[4,96,128]{2,1,0:T(8,128)S(1)}, f32[4,96,128]{2,1,0:T(8,128)S(1)}, u32[]{:S(2)}, u32[]{:S(2)}) collective-permute-start(f32[4,96,128]{2,1,0:T(8,128)S(1)} %get-tuple-element.55), channel_id=1, source_target_pairs={{0,8},{8,0},{16,24},{24,16},{32,40},{40,32},{48,56},{56,48},{64,72... | collective-permute-start | bytes 589832 | tf_op jit(solution)/shard_map/ppermute | solution.py:491
  67.1 8.7 %collective-permute-start.27 = (f32[4,96,128]{2,1,0:T(8,128)S(1)}, f32[4,96,128]{2,1,0:T(8,128)S(1)}, u32[]{:S(2)}, u32[]{:S(2)}) collective-permute-start(f32[4,96,128]{2,1,0:T(8,128)S(1)} %get-tuple-element.56), channel_id=1, source_target_pairs={{0,32},{8,40},{16,48},{24,56},{32,0},{40,8},{48,16},{56,24},{64,96... | collective-permute-start | bytes 589832 | tf_op jit(solution)/shard_map/ppermute | solution.py:522
  69.4 20.7 %collective-permute-start.21 = (f32[2,384,128]{2,1,0:T(8,128)S(1)}, f32[2,384,128]{2,1,0:T(8,128)S(1)}, u32[]{:S(2)}, u32[]{:S(2)}) collective-permute-start(f32[2,384,128]{2,1,0:T(8,128)S(1)} %get-tuple-element.49), channel_id=1, source_target_pairs={{0,2},{1,3},{2,4},{3,5},{4,6},{5,7},{6,0},{7,1},{8,10},{9,11},{10,... | collective-permute-start | bytes 1179656 | tf_op jit(solution)/shard_map/ppermute | solution.py:524
  69.8 24.3 %collective-permute-start.22 = (f32[2,384,128]{2,1,0:T(8,128)S(1)}, f32[2,384,128]{2,1,0:T(8,128)S(1)}, u32[]{:S(2)}, u32[]{:S(2)}) collective-permute-start(f32[2,384,128]{2,1,0:T(8,128)S(1)} %get-tuple-element.50), channel_id=1, source_target_pairs={{0,4},{1,5},{2,6},{3,7},{4,0},{5,1},{6,2},{7,3},{8,12},{9,13},{10,... | collective-permute-start | bytes 1179656 | tf_op jit(solution)/shard_map/ppermute | solution.py:524
  71.8 22.2 %collective-permute-start.23 = (f32[2,384,128]{2,1,0:T(8,128)S(1)}, f32[2,384,128]{2,1,0:T(8,128)S(1)}, u32[]{:S(2)}, u32[]{:S(2)}) collective-permute-start(f32[2,384,128]{2,1,0:T(8,128)S(1)} %get-tuple-element.51), channel_id=1, source_target_pairs={{0,6},{1,7},{2,0},{3,1},{4,2},{5,3},{6,4},{7,5},{8,14},{9,15},{10,... | collective-permute-start | bytes 1179656 | tf_op jit(solution)/shard_map/ppermute | solution.py:524
  73.5 6.5 %collective-permute-start.28 = (f32[4,96,128]{2,1,0:T(8,128)S(1)}, f32[4,96,128]{2,1,0:T(8,128)S(1)}, u32[]{:S(2)}, u32[]{:S(2)}) collective-permute-start(f32[4,96,128]{2,1,0:T(8,128)S(1)} %get-tuple-element.57), channel_id=1, source_target_pairs={{0,48},{8,56},{16,0},{24,8},{32,16},{40,24},{48,32},{56,40},{64,11... | collective-permute-start | bytes 589832 | tf_op jit(solution)/shard_map/ppermute | solution.py:522
  75.8 7.0 %collective-permute-start.26 = (f32[4,96,128]{2,1,0:T(8,128)S(1)}, f32[4,96,128]{2,1,0:T(8,128)S(1)}, u32[]{:S(2)}, u32[]{:S(2)}) collective-permute-start(f32[4,96,128]{2,1,0:T(8,128)S(1)} %get-tuple-element.47.refs_1_), channel_id=1, source_target_pairs={{0,16},{8,24},{16,32},{24,40},{32,48},{40,56},{48,0},{56,8},{64,80... | collective-permute-start | bytes 589832 | tf_op jit(solution)/shard_map/ppermute | solution.py:522
  82.8 12.2 %collective-permute-start.29 = (f32[96,128]{1,0:T(8,128)S(1)}, f32[96,128]{1,0:T(8,128)S(1)}, u32[]{:S(2)}, u32[]{:S(2)}) collective-permute-start(f32[96,128]{1,0:T(8,128)S(1)} %get-tuple-element.59), channel_id=1, source_target_pairs={{0,64},{8,72},{16,80},{24,88},{32,96},{40,104},{48,112},{56,120},{... | collective-permute-start | bytes 147464 | tf_op jit(solution)/shard_map/ppermute | solution.py:526
  85.6 9.4 %collective-permute-start.30 = (f32[96,128]{1,0:T(8,128)S(1)}, f32[96,128]{1,0:T(8,128)S(1)}, u32[]{:S(2)}, u32[]{:S(2)}) collective-permute-start(f32[96,128]{1,0:T(8,128)S(1)} %get-tuple-element.60), channel_id=1, source_target_pairs={{0,128},{8,136},{16,144},{24,152},{32,160},{40,168},{48,176},{56,1... | collective-permute-start | bytes 147464 | tf_op jit(solution)/shard_map/ppermute | solution.py:526
  90.1 6.2 %collective-permute-start.31 = (f32[96,128]{1,0:T(8,128)S(1)}, f32[96,128]{1,0:T(8,128)S(1)}, u32[]{:S(2)}, u32[]{:S(2)}) collective-permute-start(f32[96,128]{1,0:T(8,128)S(1)} %get-tuple-element.61), channel_id=1, source_target_pairs={{0,192},{8,200},{16,208},{24,216},{32,224},{40,232},{48,240},{56,2... | collective-permute-start | bytes 147464 | tf_op jit(solution)/shard_map/ppermute | solution.py:526
  94.2 6.2 %collective-permute-start.24 = (f32[384,128]{1,0:T(8,128)S(1)}, f32[384,128]{1,0:T(8,128)S(1)}, u32[]{:S(2)}, u32[]{:S(2)}) collective-permute-start(f32[384,128]{1,0:T(8,128)S(1)} %get-tuple-element.53), channel_id=1, source_target_pairs={{0,1},{1,0},{2,3},{3,2},{4,5},{5,4},{6,7},{7,6},{8,9},{9,8},{10,11... | collective-permute-start | bytes 589832 | tf_op jit(solution)/shard_map/ppermute | solution.py:487
  97.0 9.8 %all-to-all-start.1 = ((f32[8,24,128]{2,1,0:T(8,128)}), f32[8,24,128]{2,1,0:T(8,128)S(1)}, u32[]{:S(2)}, u32[]{:S(2)}) async-start(f32[8,24,128]{2,1,0:T(8,128)} %shard_map.106), calls=%async_computation.1 | async-start | bytes 196608 | tf_op jit(solution)/shard_map/all_to_all | solution.py:537
  (9 other events, 343.3 us)

commit v7 on v6

--- a/solution.py
+++ b/solution.py
@@ -94,30 +94,24 @@
 
 
 def pick(index, choices):
-    value = choices[0]
-    for d in range(1, len(choices)):
-        value = jnp.where(index == d, choices[d], value)
-    return value
+    tiles = [c.reshape(-1, 8, LANES) for c in choices]
+    value = tiles[0]
+    for d in range(1, len(tiles)):
+        value = jnp.where(index[None] == d, tiles[d], value)
+    return value.reshape(choices[0].shape)
 
 
 def shape(*dims):
     return jax.ShapeDtypeStruct(dims, F32)
 
 
-def call(kernel, out_shape, owner, *arrays, after=(), scratch=(), flops=0, vmem=8):
+def call(kernel, out_shape, *arrays, after=(), scratch=(), flops=0, vmem=8):
     specs = [pl.BlockSpec(memory_space=pltpu.VMEM) for _ in arrays]
     specs += [pl.BlockSpec(memory_space=pl.ANY) for _ in after]
     size = sum(a.size for a in arrays) * 4
-    operands = [*arrays, *after]
-    if owner is not None:
-        specs = [pl.BlockSpec(memory_space=pltpu.SMEM)] + specs
-        operands = [owner] + operands
 
     def body(*refs):
-        if owner is None:
-            kernel(scalars(), *refs)
-        else:
-            kernel(scalars(refs[0]), *refs[1:])
+        kernel(scalars(), *refs)
 
     return pl.pallas_call(
         body,
@@ -126,27 +120,16 @@
         scratch_shapes=list(scratch),
         compiler_params=pltpu.CompilerParams(vmem_limit_bytes=vmem * 2**20),
         cost_estimate=pl.CostEstimate(flops=flops, bytes_accessed=2 * size, transcendentals=0),
-    )(*operands)
-
-
-MY_X, MY_C, MY_Z, X_STEP, C_OWN, Z_STEP, MY_Y, MY_PAIR = 0, 1, 2, 3, 5, 7, 9, 10
-
-
-def divide_grid():
-    me = lax.axis_index("grid")
-    return me // 2, lax.rem(me, 2)
-
-
-def scalars(owner=None):
-    me = lax.axis_index("band")
-    x, c, z = lax.rem(me // 2, 4), lax.rem(me, 2), me // 8
-    values = [x, c, z, 0, 0, 0, 0, 0, 0, *divide_grid()]
-    for step in range(2 if owner is not None else 0):
-        band = jnp.clip(owner[step], 0, BAND - 1)
-        values[X_STEP + step] = lax.rem(x + 4 - lax.rem(band // 2, 4), 4)
-        values[C_OWN + step] = (c == lax.rem(band, 2)).astype(jnp.int32)
-        values[Z_STEP + step] = lax.rem(z + 4 - band // 8, 4)
-    return values
+    )(*arrays, *after)
+
+
+MY_X, MY_C, MY_Z, MY_Y, MY_PAIR = range(5)
+
+
+def scalars():
+    band, grid = lax.axis_index("band"), lax.axis_index("grid")
+    x, c, z = lax.rem(band // 2, 4), lax.rem(band, 2), band // 8
+    return [x, c, z, grid // 2, lax.rem(grid, 2)]
 
 
 def pack_kernel(info, orb_ref, stay_ref, cross_ref, q0, q1, q2, q3, out_ref):
@@ -172,24 +155,26 @@
     out_ref[1] = got_ref[...]
 
 
-def pick_x_kernel(info, q0, q1, q2, q3, keep_ref, give_ref):
+def pick_x_kernel(info, owner_ref, q0, q1, q2, q3, keep_ref, give_ref):
     for ref, half in ((keep_ref, info[MY_C]), (give_ref, 1 - info[MY_C])):
         rows = pl.ds(pl.multiple_of(half * PIECE, PIECE), PIECE)
         for step in range(2):
+            away = (info[MY_X] - (owner_ref[step] >> 1)) & 3
             for m in range(2):
                 choices = [q[m, rows, :] for q in (q0, q1, q2, q3)]
-                ref[2 * step + m] = pick(info[X_STEP + step], choices)
-
-
-def pick_core_kernel(info, keep_ref, got_ref, out_ref):
+                ref[2 * step + m] = pick(away, choices)
+
+
+def pick_core_kernel(info, owner_ref, keep_ref, got_ref, out_ref):
     for b in range(4):
-        out_ref[b] = jnp.where(info[C_OWN + b // 2] == 1, keep_ref[b], got_ref[b])
-
-
-def pick_z_kernel(info, z0, z1, z2, z3, *refs):
-    out_ref = refs[-1]
+        away = (info[MY_C] - owner_ref[b // 2]) & 1
+        out_ref[b] = pick(away, [keep_ref[b], got_ref[b]])
+
+
+def pick_z_kernel(info, owner_ref, z0, z1, z2, z3, out_ref):
     for b in range(4):
-        value = pick(info[Z_STEP + b // 2], [z[b] for z in (z0, z1, z2, z3)])
+        away = (info[MY_Z] - (owner_ref[b // 2] >> 3)) & 3
+        value = pick(away, [z[b] for z in (z0, z1, z2, z3)])
         out_ref[2 * b] = value
         out_ref[2 * b + 1] = value
 
@@ -393,7 +378,6 @@
     return call(
         body,
         [shape(8, ROWS, LANES)] + [shape(4, PACK, LANES)] * 8,
-        None,
         *slabs,
         *pieces,
         *[jnp.asarray(t) for t in tables()],
@@ -493,24 +477,24 @@
 
 def on_device(orbitals, block_owner):
     scale = math.sqrt(GRID**3 / (2 * BAND))
+    owner = jnp.broadcast_to(block_owner[:, None, None], (2, 8, LANES))
     slab = shape(ROWS, LANES)
     stay, cross, *quarters = call(
         pack_kernel,
         [slab, slab] + [shape(2, QUARTER, LANES)] * 4,
-        None,
         orbitals,
         scratch=[pltpu.VMEM((2, ROWS, LANES), F32)],
     )
-    pair = call(join_kernel, shape(2, ROWS, LANES), None, stay, other_slab(cross))
+    pair = call(join_kernel, shape(2, ROWS, LANES), stay, other_slab(cross))
     slabs = [pair] + [lax.ppermute(pair, "grid", shift_y(d)) for d in (1, 3)]
     slabs.insert(2, lax.ppermute(slabs[1], "grid", shift_y(1)))
 
     quarters = quarters[:1] + [lax.ppermute(quarters[d], "band", shift_x(d)) for d in (1, 2, 3)]
     half = shape(4, PIECE, LANES)
-    keep, give = call(pick_x_kernel, [half, half], block_owner, *quarters)
-    mine = call(pick_core_kernel, half, block_owner, keep, other_core(give))
+    keep, give = call(pick_x_kernel, [half, half], owner, *quarters)
+    mine = call(pick_core_kernel, half, owner, keep, other_core(give))
     along = [mine] + [lax.ppermute(mine, "band", shift_z(d)) for d in (1, 2, 3)]
-    mine = call(pick_z_kernel, shape(8, PIECE, LANES), block_owner, *along)
+    mine = call(pick_z_kernel, shape(8, PIECE, LANES), owner, *along)
     piece = lax.all_to_all(mine, "grid", 0, 0)
     pieces = [piece] + [lax.ppermute(piece, "band", shift_x(d)) for d in (1, 2, 3)]
     pieces = pieces + [other_core(p) for p in pieces]
@@ -518,25 +502,24 @@
     own, *shares = fields(slabs, pieces, scale)
     kept, got = shares[:4], [other_core(g) for g in shares[4:]]
     part = shape(4, PACK, LANES)
-    added = call(add_core_kernel, [part] * 3, None, *kept[1:], *got[1:])
+    added = call(add_core_kernel, [part] * 3, *kept[1:], *got[1:])
     moved = [lax.ppermute(added[d - 1], "band", shift_x(d)) for d in (1, 2, 3)]
-    sent = call(send_kernel, [shape(2, ROWS, LANES)] * 4, None, own, after=added[:1])
+    sent = call(send_kernel, [shape(2, ROWS, LANES)] * 4, own, after=added[:1])
     sent = [sent[0]] + [lax.ppermute(sent[d], "grid", shift_y(d)) for d in (1, 2, 3)]
-    sums = call(add_x_kernel, [shape(PACK, LANES)] * 4, None, kept[0], got[0], *moved)
+    sums = call(add_x_kernel, [shape(PACK, LANES)] * 4, kept[0], got[0], *moved)
     moved = [lax.ppermute(sums[d], "band", shift_z(d)) for d in (1, 2, 3)]
     slabs = call(
         add_z_kernel,
         shape(8, PART, LANES),
-        None,
         sums[0],
         *moved,
         scratch=[pltpu.VMEM((PACK, LANES), F32)],
     )
-    stay, cross = call(add_y_kernel, [slab, slab], None, *sent)
-    field = call(own_kernel, shape(2, SLAB, PLANE), None, stay, other_slab(cross))
+    stay, cross = call(add_y_kernel, [slab, slab], *sent)
+    field = call(own_kernel, shape(2, SLAB, PLANE), stay, other_slab(cross))
     slabs = lax.all_to_all(slabs, "grid", 0, 0)
     block_field = call(
-        share_kernel, shape(2, 2, SLAB, SHARE), None, slabs, after=[field]
+        share_kernel, shape(2, 2, SLAB, SHARE), slabs, after=[field]
     )
     return field, block_field
 

time: 109 us -> 108 us (level)
  Pallas kernels: 11.9 us -> 10.2 us
    pallas_call x13, Pallas kernels: 11.9 us -> 10.2 us  [call(): pl.pallas_call(body, in_specs=specs, out_shape=out_shape, scratch_shapes=...]
  transfers between devices with their start and end apart: 34 -> 34, of which waited for: 19 -> 19; matrix products, arithmetic and copies ran while one was open for 1% -> 1% of each run, Pallas kernels for 3% -> 2%
where the time goes in v7:
time: 108 us; the launch traced here: 106 us
  starting transfers between devices  56.5 us (52%)
  waiting for transfers between devices  35.6 us (33%)
  Pallas kernels  10.2 us (9%)
  local copies, waits for them, and re-layouts  2.75 us (3%)
    ppermute x3, starting transfers between devices, on_device(): moved = [lax.ppermute(sums[d], 'band', shift_z(d)) for d in (1, 2, 3)]  10.6 us
    pallas_call x13, Pallas kernels, call(): pl.pallas_call(body, in_specs=specs, out_shape=out_shape, scratch_shapes=...  10.2 us
    ppermute x3, starting transfers between devices, on_device(): along = [mine] + [lax.ppermute(mine, 'band', shift_z(d)) for d in (1, 2, 3)]  9.51 us
    ppermute x3, waiting for transfers between devices, on_device(): along = [mine] + [lax.ppermute(mine, 'band', shift_z(d)) for d in (1, 2, 3)]  6.7 us
    ppermute x3, waiting for transfers between devices, on_device(): moved = [lax.ppermute(added[d - 1], 'band', shift_x(d)) for d in (1, 2, 3)]  5.95 us
    ppermute x3, starting transfers between devices, on_device(): moved = [lax.ppermute(added[d - 1], 'band', shift_x(d)) for d in (1, 2, 3)]  5.52 us
    all_to_all x1, waiting for transfers between devices, on_device(): slabs = lax.all_to_all(slabs, 'grid', 0, 0)  5.46 us
    ppermute x3, waiting for transfers between devices, on_device(): lax.ppermute(piece, 'band', shift_x(d))  5.24 us
  transfers between devices with their start and end apart: 34, of which 19 were waited for; matrix products, arithmetic and copies ran while one was open for 1% of the time, Pallas kernels for 2%

profile of v7, /device:TPU:2, one launch (start us, length us, event | category | flops | bytes accessed | tf_op | source)
XLA Modules:
  0.0 105.9 jit_solution(121596739331256012)
XLA Ops:
  1.9 1.6 %collective-permute-start.4 = (f32[2,96,128]{2,1,0:T(8,128)S(1)}, f32[2,96,128]{2,1,0:T(8,128)S(1)}, u32[]{:S(2)}, u32[]{:S(2)}) collective-permute-start(f32[2,96,128]{2,1,0:T(8,128)S(1)} %get-tuple-element.35), channel_id=1, source_target_pairs={{0,16},{8,24},{16,32},{24,40},{32,48},{40,56},{48,0},{56,8},{64,80... | collective-permute-start | bytes 294920 | tf_op jit(solution)/shard_map/ppermute | solution.py:492
  3.5 2.8 %collective-permute-start.5 = (f32[2,96,128]{2,1,0:T(8,128)S(1)}, f32[2,96,128]{2,1,0:T(8,128)S(1)}, u32[]{:S(2)}, u32[]{:S(2)}) collective-permute-start(f32[2,96,128]{2,1,0:T(8,128)S(1)} %get-tuple-element.36), channel_id=1, source_target_pairs={{0,32},{8,40},{16,48},{24,56},{32,0},{40,8},{48,16},{56,24},{64,96... | collective-permute-start | bytes 294920 | tf_op jit(solution)/shard_map/ppermute | solution.py:492
  6.7 1.9 %collective-permute-start = (f32[384,128]{1,0:T(8,128)S(1)}, f32[384,128]{1,0:T(8,128)S(1)}, u32[]{:S(2)}, u32[]{:S(2)}) collective-permute-start(f32[384,128]{1,0:T(8,128)S(1)} %get-tuple-element.33), channel_id=1, source_target_pairs={{0,1},{1,0},{2,3},{3,2},{4,5},{5,4},{6,7},{7,6},{8,9},{9,8},{10,11... | collective-permute-start | bytes 589832 | tf_op jit(solution)/shard_map/ppermute | solution.py:471
  8.6 1.7 %collective-permute-done.5.refs_3_ = f32[2,96,128]{2,1,0:T(8,128)S(1)} collective-permute-done((f32[2,96,128]{2,1,0:T(8,128)S(1)}, f32[2,96,128]{2,1,0:T(8,128)S(1)}, u32[]{:S(2)}, u32[]{:S(2)}) %collective-permute-start.5) | collective-permute-done | bytes 98336 | tf_op jit(solution)/shard_map/ppermute | solution.py:492
  11.5 1.3 %collective-permute-done.7.refs_2_ = f32[4,48,128]{2,1,0:T(8,128)S(1)} collective-permute-done((f32[4,48,128]{2,1,0:T(8,128)S(1)}, f32[4,48,128]{2,1,0:T(8,128)S(1)}, u32[]{:S(2)}, u32[]{:S(2)}) %collective-permute-start.7) | collective-permute-done | bytes 98336 | tf_op jit(solution)/shard_map/ppermute | solution.py:475
  12.9 5.7 %collective-permute-start.10 = (f32[4,48,128]{2,1,0:T(8,128)S(1)}, f32[4,48,128]{2,1,0:T(8,128)S(1)}, u32[]{:S(2)}, u32[]{:S(2)}) collective-permute-start(f32[4,48,128]{2,1,0:T(8,128)S(1)} %shard_map.98.refs_1_), channel_id=1, source_target_pairs={{0,192},{8,200},{16,208},{24,216},{32,224},{40,232},{48,240},{56,2... | collective-permute-start | bytes 294920 | tf_op jit(solution)/shard_map/ppermute | solution.py:496
  19.5 2.8 %collective-permute-start.8 = (f32[4,48,128]{2,1,0:T(8,128)S(1)}, f32[4,48,128]{2,1,0:T(8,128)S(1)}, u32[]{:S(2)}, u32[]{:S(2)}) collective-permute-start(f32[4,48,128]{2,1,0:T(8,128)S(1)} %shard_map.98.refs_1_), channel_id=1, source_target_pairs={{0,64},{8,72},{16,80},{24,88},{32,96},{40,104},{48,112},{56,120},{... | collective-permute-start | bytes 294920 | tf_op jit(solution)/shard_map/ppermute | solution.py:496
  22.4 1.7 %collective-permute-start.1 = (f32[2,384,128]{2,1,0:T(8,128)S(1)}, f32[2,384,128]{2,1,0:T(8,128)S(1)}, u32[]{:S(2)}, u32[]{:S(2)}) collective-permute-start(f32[2,384,128]{2,1,0:T(8,128)S(1)} %shard_map.96.refs_0_), channel_id=1, source_target_pairs={{0,2},{1,3},{2,4},{3,5},{4,6},{5,7},{6,0},{7,1},{8,10},{9,11},{10,... | collective-permute-start | bytes 1179656 | tf_op jit(solution)/shard_map/ppermute | solution.py:489
  24.1 3.2 %collective-permute-done.10.refs_4_ = f32[4,48,128]{2,1,0:T(8,128)S(1)} collective-permute-done((f32[4,48,128]{2,1,0:T(8,128)S(1)}, f32[4,48,128]{2,1,0:T(8,128)S(1)}, u32[]{:S(2)}, u32[]{:S(2)}) %collective-permute-start.10) | collective-permute-done | bytes 98336 | tf_op jit(solution)/shard_map/ppermute | solution.py:496
  27.3 3.5 %collective-permute-done.9.refs_3_ = f32[4,48,128]{2,1,0:T(8,128)S(1)} collective-permute-done((f32[4,48,128]{2,1,0:T(8,128)S(1)}, f32[4,48,128]{2,1,0:T(8,128)S(1)}, u32[]{:S(2)}, u32[]{:S(2)}) %collective-permute-start.9) | collective-permute-done | bytes 98336 | tf_op jit(solution)/shard_map/ppermute | solution.py:496
  31.5 4.5 %all-to-all-start = ((f32[8,48,128]{2,1,0:T(8,128)}), f32[8,48,128]{2,1,0:T(8,128)S(1)}, u32[]{:S(2)}, u32[]{:S(2)}) async-start(f32[8,48,128]{2,1,0:T(8,128)} %shard_map.99), calls=%async_computation | async-start | bytes 393216 | tf_op jit(solution)/shard_map/all_to_all | solution.py:498
  35.9 3.2 %collective-permute-start.3 = (f32[2,384,128]{2,1,0:T(8,128)S(1)}, f32[2,384,128]{2,1,0:T(8,128)S(1)}, u32[]{:S(2)}, u32[]{:S(2)}) collective-permute-start(f32[2,384,128]{2,1,0:T(8,128)S(1)} %shard_map.96.refs_0_), channel_id=1, source_target_pairs={{0,6},{1,7},{2,0},{3,1},{4,2},{5,3},{6,4},{7,5},{8,14},{9,15},{10,... | collective-permute-start | bytes 1179656 | tf_op jit(solution)/shard_map/ppermute | solution.py:489
  39.2 3.7 %all-to-all-done.refs_4_ = f32[8,48,128]{2,1,0:T(8,128)S(1)} async-done(((f32[8,48,128]{2,1,0:T(8,128)}), f32[8,48,128]{2,1,0:T(8,128)S(1)}, u32[]{:S(2)}, u32[]{:S(2)}) %all-to-all-start) | async-done | bytes 196640 | tf_op jit(solution)/shard_map/all_to_all | solution.py:498
  43.6 2.1 %collective-permute-start.12 = (f32[8,48,128]{2,1,0:T(8,128)S(1)}, f32[8,48,128]{2,1,0:T(8,128)S(1)}, u32[]{:S(2)}, u32[]{:S(2)}) collective-permute-start(f32[8,48,128]{2,1,0:T(8,128)S(1)} %all-to-all-done.refs_4_), channel_id=1, source_target_pairs={{0,32},{8,40},{16,48},{24,56},{32,0},{40,8},{48,16},{56,24},{64,96... | collective-permute-start | bytes 589832 | tf_op jit(solution)/shard_map/ppermute | solution.py:499
  46.1 2.1 %collective-permute-start.11 = (f32[8,48,128]{2,1,0:T(8,128)S(1)}, f32[8,48,128]{2,1,0:T(8,128)S(1)}, u32[]{:S(2)}, u32[]{:S(2)}) collective-permute-start(f32[8,48,128]{2,1,0:T(8,128)S(1)} %all-to-all-done.refs_4_), channel_id=1, source_target_pairs={{0,16},{8,24},{16,32},{24,40},{32,48},{40,56},{48,0},{56,8},{64,80... | collective-permute-start | bytes 589832 | tf_op jit(solution)/shard_map/ppermute | solution.py:499
  48.2 2.1 %collective-permute-done.13.refs_7_ = f32[8,48,128]{2,1,0:T(8,128)S(1)} collective-permute-done((f32[8,48,128]{2,1,0:T(8,128)S(1)}, f32[8,48,128]{2,1,0:T(8,128)S(1)}, u32[]{:S(2)}, u32[]{:S(2)}) %collective-permute-start.13) | collective-permute-done | bytes 196640 | tf_op jit(solution)/shard_map/ppermute | solution.py:499
  50.3 2.1 %collective-permute-done.12.refs_6_ = f32[8,48,128]{2,1,0:T(8,128)S(1)} collective-permute-done((f32[8,48,128]{2,1,0:T(8,128)S(1)}, f32[8,48,128]{2,1,0:T(8,128)S(1)}, u32[]{:S(2)}, u32[]{:S(2)}) %collective-permute-start.12) | collective-permute-done | bytes 196640 | tf_op jit(solution)/shard_map/ppermute | solution.py:499
  53.4 1.6 %collective-permute-done.2.refs_2_ = f32[2,384,128]{2,1,0:T(8,128)S(1)} collective-permute-done((f32[2,384,128]{2,1,0:T(8,128)S(1)}, f32[2,384,128]{2,1,0:T(8,128)S(1)}, u32[]{:S(2)}, u32[]{:S(2)}) %collective-permute-start.2) | collective-permute-done | bytes 393248 | tf_op jit(solution)/shard_map/ppermute | solution.py:490
  55.1 8.2 %shard_map.100 = (f32[8,384,128]{2,1,0:T(8,128)S(1)}, f32[4,96,128]{2,1,0:T(8,128)S(1)}, f32[4,96,128]{2,1,0:T(8,128)S(1)}, f32[4,96,128]{2,1,0:T(8,128)S(1)}, f...) custom-call(f32[2,384,128]{2,1,0:T(8,128)S(1)} %shard_map.96.refs_0_, ...), custom_call_target="tpu_custom_call" | custom-call | flops 10000000000 | bytes 8454144 | tf_op jit(solution)/shard_map/pallas_call | solution.py:116
  65.5 2.1 %collective-permute-start.27 = (f32[4,96,128]{2,1,0:T(8,128)S(1)}, f32[4,96,128]{2,1,0:T(8,128)S(1)}, u32[]{:S(2)}, u32[]{:S(2)}) collective-permute-start(f32[4,96,128]{2,1,0:T(8,128)S(1)} %get-tuple-element.56), channel_id=1, source_target_pairs={{0,32},{8,40},{16,48},{24,56},{32,0},{40,8},{48,16},{56,24},{64,96... | collective-permute-start | bytes 589832 | tf_op jit(solution)/shard_map/ppermute | solution.py:506
  68.2 2.1 %collective-permute-start.22 = (f32[2,384,128]{2,1,0:T(8,128)S(1)}, f32[2,384,128]{2,1,0:T(8,128)S(1)}, u32[]{:S(2)}, u32[]{:S(2)}) collective-permute-start(f32[2,384,128]{2,1,0:T(8,128)S(1)} %get-tuple-element.50), channel_id=1, source_target_pairs={{0,4},{1,5},{2,6},{3,7},{4,0},{5,1},{6,2},{7,3},{8,12},{9,13},{10,... | collective-permute-start | bytes 1179656 | tf_op jit(solution)/shard_map/ppermute | solution.py:508
  70.3 1.6 %collective-permute-start.23 = (f32[2,384,128]{2,1,0:T(8,128)S(1)}, f32[2,384,128]{2,1,0:T(8,128)S(1)}, u32[]{:S(2)}, u32[]{:S(2)}) collective-permute-start(f32[2,384,128]{2,1,0:T(8,128)S(1)} %get-tuple-element.51), channel_id=1, source_target_pairs={{0,6},{1,7},{2,0},{3,1},{4,2},{5,3},{6,4},{7,5},{8,14},{9,15},{10,... | collective-permute-start | bytes 1179656 | tf_op jit(solution)/shard_map/ppermute | solution.py:508
  71.9 1.4 %collective-permute-start.28 = (f32[4,96,128]{2,1,0:T(8,128)S(1)}, f32[4,96,128]{2,1,0:T(8,128)S(1)}, u32[]{:S(2)}, u32[]{:S(2)}) collective-permute-start(f32[4,96,128]{2,1,0:T(8,128)S(1)} %get-tuple-element.57), channel_id=1, source_target_pairs={{0,48},{8,56},{16,0},{24,8},{32,16},{40,24},{48,32},{56,40},{64,11... | collective-permute-start | bytes 589832 | tf_op jit(solution)/shard_map/ppermute | solution.py:506
  74.2 2.0 %collective-permute-start.26 = (f32[4,96,128]{2,1,0:T(8,128)S(1)}, f32[4,96,128]{2,1,0:T(8,128)S(1)}, u32[]{:S(2)}, u32[]{:S(2)}) collective-permute-start(f32[4,96,128]{2,1,0:T(8,128)S(1)} %get-tuple-element.47.refs_1_), channel_id=1, source_target_pairs={{0,16},{8,24},{16,32},{24,40},{32,48},{40,56},{48,0},{56,8},{64,80... | collective-permute-start | bytes 589832 | tf_op jit(solution)/shard_map/ppermute | solution.py:506
  76.2 2.2 %collective-permute-done.28.refs_4_ = f32[4,96,128]{2,1,0:T(8,128)S(1)} collective-permute-done((f32[4,96,128]{2,1,0:T(8,128)S(1)}, f32[4,96,128]{2,1,0:T(8,128)S(1)}, u32[]{:S(2)}, u32[]{:S(2)}) %collective-permute-start.28) | collective-permute-done | bytes 196640 | tf_op jit(solution)/shard_map/ppermute | solution.py:506
  78.4 2.8 %collective-permute-done.26.refs_2_ = f32[4,96,128]{2,1,0:T(8,128)S(1)} collective-permute-done((f32[4,96,128]{2,1,0:T(8,128)S(1)}, f32[4,96,128]{2,1,0:T(8,128)S(1)}, u32[]{:S(2)}, u32[]{:S(2)}) %collective-permute-start.26) | collective-permute-done | bytes 196640 | tf_op jit(solution)/shard_map/ppermute | solution.py:506
  81.3 2.8 %collective-permute-start.29 = (f32[96,128]{1,0:T(8,128)S(1)}, f32[96,128]{1,0:T(8,128)S(1)}, u32[]{:S(2)}, u32[]{:S(2)}) collective-permute-start(f32[96,128]{1,0:T(8,128)S(1)} %get-tuple-element.59), channel_id=1, source_target_pairs={{0,64},{8,72},{16,80},{24,88},{32,96},{40,104},{48,112},{56,120},{... | collective-permute-start | bytes 147464 | tf_op jit(solution)/shard_map/ppermute | solution.py:510
  84.0 3.8 %collective-permute-start.30 = (f32[96,128]{1,0:T(8,128)S(1)}, f32[96,128]{1,0:T(8,128)S(1)}, u32[]{:S(2)}, u32[]{:S(2)}) collective-permute-start(f32[96,128]{1,0:T(8,128)S(1)} %get-tuple-element.60), channel_id=1, source_target_pairs={{0,128},{8,136},{16,144},{24,152},{32,160},{40,168},{48,176},{56,1... | collective-permute-start | bytes 147464 | tf_op jit(solution)/shard_map/ppermute | solution.py:510
  88.4 4.1 %collective-permute-start.31 = (f32[96,128]{1,0:T(8,128)S(1)}, f32[96,128]{1,0:T(8,128)S(1)}, u32[]{:S(2)}, u32[]{:S(2)}) collective-permute-start(f32[96,128]{1,0:T(8,128)S(1)} %get-tuple-element.61), channel_id=1, source_target_pairs={{0,192},{8,200},{16,208},{24,216},{32,224},{40,232},{48,240},{56,2... | collective-permute-start | bytes 147464 | tf_op jit(solution)/shard_map/ppermute | solution.py:510
  93.4 1.2 %collective-permute-done.31.refs_3_ = f32[96,128]{1,0:T(8,128)S(1)} collective-permute-done((f32[96,128]{1,0:T(8,128)S(1)}, f32[96,128]{1,0:T(8,128)S(1)}, u32[]{:S(2)}, u32[]{:S(2)}) %collective-permute-start.31) | collective-permute-done | bytes 49184 | tf_op jit(solution)/shard_map/ppermute | solution.py:510
  95.4 3.4 %all-to-all-start.1 = ((f32[8,24,128]{2,1,0:T(8,128)}), f32[8,24,128]{2,1,0:T(8,128)S(1)}, u32[]{:S(2)}, u32[]{:S(2)}) async-start(f32[8,24,128]{2,1,0:T(8,128)} %shard_map.106), calls=%async_computation.1 | async-start | bytes 196608 | tf_op jit(solution)/shard_map/all_to_all | solution.py:520
  99.8 5.5 %all-to-all-done.1.refs_0_ = f32[8,24,128]{2,1,0:T(8,128)S(1)} async-done(((f32[8,24,128]{2,1,0:T(8,128)}), f32[8,24,128]{2,1,0:T(8,128)S(1)}, u32[]{:S(2)}, u32[]{:S(2)}) %all-to-all-start.1) | async-done | bytes 98336 | tf_op jit(solution)/shard_map/all_to_all | solution.py:520
  (67 shorter events, 14.4 us)
Async XLA Ops:
  1.9 6.8 %collective-permute-start.4 = (f32[2,96,128]{2,1,0:T(8,128)S(1)}, f32[2,96,128]{2,1,0:T(8,128)S(1)}, u32[]{:S(2)}, u32[]{:S(2)}) collective-permute-start(f32[2,96,128]{2,1,0:T(8,128)S(1)} %get-tuple-element.35), channel_id=1, source_target_pairs={{0,16},{8,24},{16,32},{24,40},{32,48},{40,56},{48,0},{56,8},{64,80... | collective-permute-start | bytes 294920 | tf_op jit(solution)/shard_map/ppermute | solution.py:492
  3.5 6.9 %collective-permute-start.5 = (f32[2,96,128]{2,1,0:T(8,128)S(1)}, f32[2,96,128]{2,1,0:T(8,128)S(1)}, u32[]{:S(2)}, u32[]{:S(2)}) collective-permute-start(f32[2,96,128]{2,1,0:T(8,128)S(1)} %get-tuple-element.36), channel_id=1, source_target_pairs={{0,32},{8,40},{16,48},{24,56},{32,0},{40,8},{48,16},{56,24},{64,96... | collective-permute-start | bytes 294920 | tf_op jit(solution)/shard_map/ppermute | solution.py:492
  6.3 5.0 %collective-permute-start.6 = (f32[2,96,128]{2,1,0:T(8,128)S(1)}, f32[2,96,128]{2,1,0:T(8,128)S(1)}, u32[]{:S(2)}, u32[]{:S(2)}) collective-permute-start(f32[2,96,128]{2,1,0:T(8,128)S(1)} %get-tuple-element.37), channel_id=1, source_target_pairs={{0,48},{8,56},{16,0},{24,8},{32,16},{40,24},{48,32},{56,40},{64,11... | collective-permute-start | bytes 294920 | tf_op jit(solution)/shard_map/ppermute | solution.py:492
  6.7 15.7 %collective-permute-start = (f32[384,128]{1,0:T(8,128)S(1)}, f32[384,128]{1,0:T(8,128)S(1)}, u32[]{:S(2)}, u32[]{:S(2)}) collective-permute-start(f32[384,128]{1,0:T(8,128)S(1)} %get-tuple-element.33), channel_id=1, source_target_pairs={{0,1},{1,0},{2,3},{3,2},{4,5},{5,4},{6,7},{7,6},{8,9},{9,8},{10,11... | collective-permute-start | bytes 589832 | tf_op jit(solution)/shard_map/ppermute | solution.py:471
  12.9 14.4 %collective-permute-start.10 = (f32[4,48,128]{2,1,0:T(8,128)S(1)}, f32[4,48,128]{2,1,0:T(8,128)S(1)}, u32[]{:S(2)}, u32[]{:S(2)}) collective-permute-start(f32[4,48,128]{2,1,0:T(8,128)S(1)} %shard_map.98.refs_1_), channel_id=1, source_target_pairs={{0,192},{8,200},{16,208},{24,216},{32,224},{40,232},{48,240},{56,2... | collective-permute-start | bytes 294920 | tf_op jit(solution)/shard_map/ppermute | solution.py:496
  18.6 12.2 %collective-permute-start.9 = (f32[4,48,128]{2,1,0:T(8,128)S(1)}, f32[4,48,128]{2,1,0:T(8,128)S(1)}, u32[]{:S(2)}, u32[]{:S(2)}) collective-permute-start(f32[4,48,128]{2,1,0:T(8,128)S(1)} %shard_map.98.refs_1_), channel_id=1, source_target_pairs={{0,128},{8,136},{16,144},{24,152},{32,160},{40,168},{48,176},{56,1... | collective-permute-start | bytes 294920 | tf_op jit(solution)/shard_map/ppermute | solution.py:496
  19.5 11.2 %collective-permute-start.8 = (f32[4,48,128]{2,1,0:T(8,128)S(1)}, f32[4,48,128]{2,1,0:T(8,128)S(1)}, u32[]{:S(2)}, u32[]{:S(2)}) collective-permute-start(f32[4,48,128]{2,1,0:T(8,128)S(1)} %shard_map.98.refs_1_), channel_id=1, source_target_pairs={{0,64},{8,72},{16,80},{24,88},{32,96},{40,104},{48,112},{56,120},{... | collective-permute-start | bytes 294920 | tf_op jit(solution)/shard_map/ppermute | solution.py:496
  22.4 23.2 %collective-permute-start.1 = (f32[2,384,128]{2,1,0:T(8,128)S(1)}, f32[2,384,128]{2,1,0:T(8,128)S(1)}, u32[]{:S(2)}, u32[]{:S(2)}) collective-permute-start(f32[2,384,128]{2,1,0:T(8,128)S(1)} %shard_map.96.refs_0_), channel_id=1, source_target_pairs={{0,2},{1,3},{2,4},{3,5},{4,6},{5,7},{6,0},{7,1},{8,10},{9,11},{10,... | collective-permute-start | bytes 1179656 | tf_op jit(solution)/shard_map/ppermute | solution.py:489
  31.5 11.4 %all-to-all-start = ((f32[8,48,128]{2,1,0:T(8,128)}), f32[8,48,128]{2,1,0:T(8,128)S(1)}, u32[]{:S(2)}, u32[]{:S(2)}) async-start(f32[8,48,128]{2,1,0:T(8,128)} %shard_map.99), calls=%async_computation | async-start | bytes 393216 | tf_op jit(solution)/shard_map/all_to_all | solution.py:498
  35.9 12.2 %collective-permute-start.3 = (f32[2,384,128]{2,1,0:T(8,128)S(1)}, f32[2,384,128]{2,1,0:T(8,128)S(1)}, u32[]{:S(2)}, u32[]{:S(2)}) collective-permute-start(f32[2,384,128]{2,1,0:T(8,128)S(1)} %shard_map.96.refs_0_), channel_id=1, source_target_pairs={{0,6},{1,7},{2,0},{3,1},{4,2},{5,3},{6,4},{7,5},{8,14},{9,15},{10,... | collective-permute-start | bytes 1179656 | tf_op jit(solution)/shard_map/ppermute | solution.py:489
  42.9 7.4 %collective-permute-start.13 = (f32[8,48,128]{2,1,0:T(8,128)S(1)}, f32[8,48,128]{2,1,0:T(8,128)S(1)}, u32[]{:S(2)}, u32[]{:S(2)}) collective-permute-start(f32[8,48,128]{2,1,0:T(8,128)S(1)} %all-to-all-done.refs_4_), channel_id=1, source_target_pairs={{0,48},{8,56},{16,0},{24,8},{32,16},{40,24},{48,32},{56,40},{64,11... | collective-permute-start | bytes 589832 | tf_op jit(solution)/shard_map/ppermute | solution.py:499
  43.6 8.8 %collective-permute-start.12 = (f32[8,48,128]{2,1,0:T(8,128)S(1)}, f32[8,48,128]{2,1,0:T(8,128)S(1)}, u32[]{:S(2)}, u32[]{:S(2)}) collective-permute-start(f32[8,48,128]{2,1,0:T(8,128)S(1)} %all-to-all-done.refs_4_), channel_id=1, source_target_pairs={{0,32},{8,40},{16,48},{24,56},{32,0},{40,8},{48,16},{56,24},{64,96... | collective-permute-start | bytes 589832 | tf_op jit(solution)/shard_map/ppermute | solution.py:499
  45.7 9.4 %collective-permute-start.2 = (f32[2,384,128]{2,1,0:T(8,128)S(1)}, f32[2,384,128]{2,1,0:T(8,128)S(1)}, u32[]{:S(2)}, u32[]{:S(2)}) collective-permute-start(f32[2,384,128]{2,1,0:T(8,128)S(1)} %collective-permute-done.1.refs_1_), channel_id=1, source_target_pairs={{0,2},{1,3},{2,4},{3,5},{4,6},{5,7},{6,0},{7,1},{8,10},{9,11},{10,... | collective-permute-start | bytes 1179656 | tf_op jit(solution)/shard_map/ppermute | solution.py:490
  46.1 7.3 %collective-permute-start.11 = (f32[8,48,128]{2,1,0:T(8,128)S(1)}, f32[8,48,128]{2,1,0:T(8,128)S(1)}, u32[]{:S(2)}, u32[]{:S(2)}) collective-permute-start(f32[8,48,128]{2,1,0:T(8,128)S(1)} %all-to-all-done.refs_4_), channel_id=1, source_target_pairs={{0,16},{8,24},{16,32},{24,40},{32,48},{40,56},{48,0},{56,8},{64,80... | collective-permute-start | bytes 589832 | tf_op jit(solution)/shard_map/ppermute | solution.py:499
  48.2 5.3 %collective-permute-start.14 = (f32[8,48,128]{2,1,0:T(8,128)S(1)}, f32[8,48,128]{2,1,0:T(8,128)S(1)}, u32[]{:S(2)}, u32[]{:S(2)}) collective-permute-start(f32[8,48,128]{2,1,0:T(8,128)S(1)} %all-to-all-done.refs_4_), channel_id=1, source_target_pairs={{0,8},{8,0},{16,24},{24,16},{32,40},{40,32},{48,56},{56,48},{64,72... | collective-permute-start | bytes 589832 | tf_op jit(solution)/shard_map/ppermute | solution.py:475
  50.3 4.8 %collective-permute-start.17 = (f32[8,48,128]{2,1,0:T(8,128)S(1)}, f32[8,48,128]{2,1,0:T(8,128)S(1)}, u32[]{:S(2)}, u32[]{:S(2)}) collective-permute-start(f32[8,48,128]{2,1,0:T(8,128)S(1)} %collective-permute-done.13.refs_7_), channel_id=1, source_target_pairs={{0,8},{8,0},{16,24},{24,16},{32,40},{40,32},{48,56},{56,48},{64,72... | collective-permute-start | bytes 589832 | tf_op jit(solution)/shard_map/ppermute | solution.py:475
  52.4 2.7 %collective-permute-start.16 = (f32[8,48,128]{2,1,0:T(8,128)S(1)}, f32[8,48,128]{2,1,0:T(8,128)S(1)}, u32[]{:S(2)}, u32[]{:S(2)}) collective-permute-start(f32[8,48,128]{2,1,0:T(8,128)S(1)} %collective-permute-done.12.refs_6_), channel_id=1, source_target_pairs={{0,8},{8,0},{16,24},{24,16},{32,40},{40,32},{48,56},{56,48},{64,72... | collective-permute-start | bytes 589832 | tf_op jit(solution)/shard_map/ppermute | solution.py:475
  53.4 1.6 %collective-permute-start.15 = (f32[8,48,128]{2,1,0:T(8,128)S(1)}, f32[8,48,128]{2,1,0:T(8,128)S(1)}, u32[]{:S(2)}, u32[]{:S(2)}) collective-permute-start(f32[8,48,128]{2,1,0:T(8,128)S(1)} %collective-permute-done.11.refs_5_), channel_id=1, source_target_pairs={{0,8},{8,0},{16,24},{24,16},{32,40},{40,32},{48,56},{56,48},{64,72... | collective-permute-start | bytes 589832 | tf_op jit(solution)/shard_map/ppermute | solution.py:475
  63.4 1.5 %collective-permute-start.18 = (f32[4,96,128]{2,1,0:T(8,128)S(1)}, f32[4,96,128]{2,1,0:T(8,128)S(1)}, u32[]{:S(2)}, u32[]{:S(2)}) collective-permute-start(f32[4,96,128]{2,1,0:T(8,128)S(1)} %get-tuple-element.44), channel_id=1, source_target_pairs={{0,8},{8,0},{16,24},{24,16},{32,40},{40,32},{48,56},{56,48},{64,72... | collective-permute-start | bytes 589832 | tf_op jit(solution)/shard_map/ppermute | solution.py:475
  63.5 1.7 %collective-permute-start.19 = (f32[4,96,128]{2,1,0:T(8,128)S(1)}, f32[4,96,128]{2,1,0:T(8,128)S(1)}, u32[]{:S(2)}, u32[]{:S(2)}) collective-permute-start(f32[4,96,128]{2,1,0:T(8,128)S(1)} %get-tuple-element.45), channel_id=1, source_target_pairs={{0,8},{8,0},{16,24},{24,16},{32,40},{40,32},{48,56},{56,48},{64,72... | collective-permute-start | bytes 589832 | tf_op jit(solution)/shard_map/ppermute | solution.py:475
  64.1 7.8 %collective-permute-start.25 = (f32[4,96,128]{2,1,0:T(8,128)S(1)}, f32[4,96,128]{2,1,0:T(8,128)S(1)}, u32[]{:S(2)}, u32[]{:S(2)}) collective-permute-start(f32[4,96,128]{2,1,0:T(8,128)S(1)} %get-tuple-element.55), channel_id=1, source_target_pairs={{0,8},{8,0},{16,24},{24,16},{32,40},{40,32},{48,56},{56,48},{64,72... | collective-permute-start | bytes 589832 | tf_op jit(solution)/shard_map/ppermute | solution.py:475
  65.5 8.6 %collective-permute-start.27 = (f32[4,96,128]{2,1,0:T(8,128)S(1)}, f32[4,96,128]{2,1,0:T(8,128)S(1)}, u32[]{:S(2)}, u32[]{:S(2)}) collective-permute-start(f32[4,96,128]{2,1,0:T(8,128)S(1)} %get-tuple-element.56), channel_id=1, source_target_pairs={{0,32},{8,40},{16,48},{24,56},{32,0},{40,8},{48,16},{56,24},{64,96... | collective-permute-start | bytes 589832 | tf_op jit(solution)/shard_map/ppermute | solution.py:506
  67.8 20.7 %collective-permute-start.21 = (f32[2,384,128]{2,1,0:T(8,128)S(1)}, f32[2,384,128]{2,1,0:T(8,128)S(1)}, u32[]{:S(2)}, u32[]{:S(2)}) collective-permute-start(f32[2,384,128]{2,1,0:T(8,128)S(1)} %get-tuple-element.49), channel_id=1, source_target_pairs={{0,2},{1,3},{2,4},{3,5},{4,6},{5,7},{6,0},{7,1},{8,10},{9,11},{10,... | collective-permute-start | bytes 1179656 | tf_op jit(solution)/shard_map/ppermute | solution.py:508
  68.2 24.3 %collective-permute-start.22 = (f32[2,384,128]{2,1,0:T(8,128)S(1)}, f32[2,384,128]{2,1,0:T(8,128)S(1)}, u32[]{:S(2)}, u32[]{:S(2)}) collective-permute-start(f32[2,384,128]{2,1,0:T(8,128)S(1)} %get-tuple-element.50), channel_id=1, source_target_pairs={{0,4},{1,5},{2,6},{3,7},{4,0},{5,1},{6,2},{7,3},{8,12},{9,13},{10,... | collective-permute-start | bytes 1179656 | tf_op jit(solution)/shard_map/ppermute | solution.py:508
  70.3 22.2 %collective-permute-start.23 = (f32[2,384,128]{2,1,0:T(8,128)S(1)}, f32[2,384,128]{2,1,0:T(8,128)S(1)}, u32[]{:S(2)}, u32[]{:S(2)}) collective-permute-start(f32[2,384,128]{2,1,0:T(8,128)S(1)} %get-tuple-element.51), channel_id=1, source_target_pairs={{0,6},{1,7},{2,0},{3,1},{4,2},{5,3},{6,4},{7,5},{8,14},{9,15},{10,... | collective-permute-start | bytes 1179656 | tf_op jit(solution)/shard_map/ppermute | solution.py:508
  71.9 6.5 %collective-permute-start.28 = (f32[4,96,128]{2,1,0:T(8,128)S(1)}, f32[4,96,128]{2,1,0:T(8,128)S(1)}, u32[]{:S(2)}, u32[]{:S(2)}) collective-permute-start(f32[4,96,128]{2,1,0:T(8,128)S(1)} %get-tuple-element.57), channel_id=1, source_target_pairs={{0,48},{8,56},{16,0},{24,8},{32,16},{40,24},{48,32},{56,40},{64,11... | collective-permute-start | bytes 589832 | tf_op jit(solution)/shard_map/ppermute | solution.py:506
  74.2 7.0 %collective-permute-start.26 = (f32[4,96,128]{2,1,0:T(8,128)S(1)}, f32[4,96,128]{2,1,0:T(8,128)S(1)}, u32[]{:S(2)}, u32[]{:S(2)}) collective-permute-start(f32[4,96,128]{2,1,0:T(8,128)S(1)} %get-tuple-element.47.refs_1_), channel_id=1, source_target_pairs={{0,16},{8,24},{16,32},{24,40},{32,48},{40,56},{48,0},{56,8},{64,80... | collective-permute-start | bytes 589832 | tf_op jit(solution)/shard_map/ppermute | solution.py:506
  81.3 12.2 %collective-permute-start.29 = (f32[96,128]{1,0:T(8,128)S(1)}, f32[96,128]{1,0:T(8,128)S(1)}, u32[]{:S(2)}, u32[]{:S(2)}) collective-permute-start(f32[96,128]{1,0:T(8,128)S(1)} %get-tuple-element.59), channel_id=1, source_target_pairs={{0,64},{8,72},{16,80},{24,88},{32,96},{40,104},{48,112},{56,120},{... | collective-permute-start | bytes 147464 | tf_op jit(solution)/shard_map/ppermute | solution.py:510
  84.0 9.4 %collective-permute-start.30 = (f32[96,128]{1,0:T(8,128)S(1)}, f32[96,128]{1,0:T(8,128)S(1)}, u32[]{:S(2)}, u32[]{:S(2)}) collective-permute-start(f32[96,128]{1,0:T(8,128)S(1)} %get-tuple-element.60), channel_id=1, source_target_pairs={{0,128},{8,136},{16,144},{24,152},{32,160},{40,168},{48,176},{56,1... | collective-permute-start | bytes 147464 | tf_op jit(solution)/shard_map/ppermute | solution.py:510
  88.4 6.2 %collective-permute-start.31 = (f32[96,128]{1,0:T(8,128)S(1)}, f32[96,128]{1,0:T(8,128)S(1)}, u32[]{:S(2)}, u32[]{:S(2)}) collective-permute-start(f32[96,128]{1,0:T(8,128)S(1)} %get-tuple-element.61), channel_id=1, source_target_pairs={{0,192},{8,200},{16,208},{24,216},{32,224},{40,232},{48,240},{56,2... | collective-permute-start | bytes 147464 | tf_op jit(solution)/shard_map/ppermute | solution.py:510
  92.6 6.2 %collective-permute-start.24 = (f32[384,128]{1,0:T(8,128)S(1)}, f32[384,128]{1,0:T(8,128)S(1)}, u32[]{:S(2)}, u32[]{:S(2)}) collective-permute-start(f32[384,128]{1,0:T(8,128)S(1)} %get-tuple-element.53), channel_id=1, source_target_pairs={{0,1},{1,0},{2,3},{3,2},{4,5},{5,4},{6,7},{7,6},{8,9},{9,8},{10,11... | collective-permute-start | bytes 589832 | tf_op jit(solution)/shard_map/ppermute | solution.py:471
  95.4 9.8 %all-to-all-start.1 = ((f32[8,24,128]{2,1,0:T(8,128)}), f32[8,24,128]{2,1,0:T(8,128)S(1)}, u32[]{:S(2)}, u32[]{:S(2)}) async-start(f32[8,24,128]{2,1,0:T(8,128)} %shard_map.106), calls=%async_computation.1 | async-start | bytes 196608 | tf_op jit(solution)/shard_map/all_to_all | solution.py:520
  (9 other events, 333.8 us)

commit v8 on v7

--- a/solution.py
+++ b/solution.py
@@ -119,7 +119,9 @@
         out_shape=out_shape,
         scratch_shapes=list(scratch),
         compiler_params=pltpu.CompilerParams(vmem_limit_bytes=vmem * 2**20),
-        cost_estimate=pl.CostEstimate(flops=flops, bytes_accessed=2 * size, transcendentals=0),
+        cost_estimate=pl.CostEstimate(
+            flops=flops, bytes_accessed=2 * size if flops else 0, transcendentals=0
+        ),
     )(*arrays, *after)
 
 

time: 108 us -> 108 us (level)
  no operation moved by 1% of the time
where the time goes in v8:
time: 108 us; the launch traced here: 106 us
  starting transfers between devices  56.5 us (52%)
  waiting for transfers between devices  35.6 us (33%)
  Pallas kernels  10.2 us (9%)
  local copies, waits for them, and re-layouts  2.75 us (3%)
    ppermute x3, starting transfers between devices, on_device(): moved = [lax.ppermute(sums[d], 'band', shift_z(d)) for d in (1, 2, 3)]  10.6 us
    pallas_call x13, Pallas kernels, call(): pl.pallas_call(body, in_specs=specs, out_shape=out_shape, scratch_shapes=...  10.2 us
    ppermute x3, starting transfers between devices, on_device(): along = [mine] + [lax.ppermute(mine, 'band', shift_z(d)) for d in (1, 2, 3)]  9.51 us
    ppermute x3, waiting for transfers between devices, on_device(): along = [mine] + [lax.ppermute(mine, 'band', shift_z(d)) for d in (1, 2, 3)]  6.7 us
    ppermute x3, waiting for transfers between devices, on_device(): moved = [lax.ppermute(added[d - 1], 'band', shift_x(d)) for d in (1, 2, 3)]  5.95 us
    ppermute x3, starting transfers between devices, on_device(): moved = [lax.ppermute(added[d - 1], 'band', shift_x(d)) for d in (1, 2, 3)]  5.52 us
    all_to_all x1, waiting for transfers between devices, on_device(): slabs = lax.all_to_all(slabs, 'grid', 0, 0)  5.46 us
    ppermute x3, waiting for transfers between devices, on_device(): lax.ppermute(piece, 'band', shift_x(d))  5.24 us
  transfers between devices with their start and end apart: 34, of which 19 were waited for; matrix products, arithmetic and copies ran while one was open for 1% of the time, Pallas kernels for 2%

profile of v8, /device:TPU:2, one launch (start us, length us, event | category | flops | bytes accessed | tf_op | source)
XLA Modules:
  0.0 105.9 jit_solution(121596739331256012)
XLA Ops:
  1.9 1.6 %collective-permute-start.4 = (f32[2,96,128]{2,1,0:T(8,128)S(1)}, f32[2,96,128]{2,1,0:T(8,128)S(1)}, u32[]{:S(2)}, u32[]{:S(2)}) collective-permute-start(f32[2,96,128]{2,1,0:T(8,128)S(1)} %get-tuple-element.35), channel_id=1, source_target_pairs={{0,16},{8,24},{16,32},{24,40},{32,48},{40,56},{48,0},{56,8},{64,80... | collective-permute-start | bytes 294920 | tf_op jit(solution)/shard_map/ppermute | solution.py:494
  3.5 2.8 %collective-permute-start.5 = (f32[2,96,128]{2,1,0:T(8,128)S(1)}, f32[2,96,128]{2,1,0:T(8,128)S(1)}, u32[]{:S(2)}, u32[]{:S(2)}) collective-permute-start(f32[2,96,128]{2,1,0:T(8,128)S(1)} %get-tuple-element.36), channel_id=1, source_target_pairs={{0,32},{8,40},{16,48},{24,56},{32,0},{40,8},{48,16},{56,24},{64,96... | collective-permute-start | bytes 294920 | tf_op jit(solution)/shard_map/ppermute | solution.py:494
  6.7 1.9 %collective-permute-start = (f32[384,128]{1,0:T(8,128)S(1)}, f32[384,128]{1,0:T(8,128)S(1)}, u32[]{:S(2)}, u32[]{:S(2)}) collective-permute-start(f32[384,128]{1,0:T(8,128)S(1)} %get-tuple-element.33), channel_id=1, source_target_pairs={{0,1},{1,0},{2,3},{3,2},{4,5},{5,4},{6,7},{7,6},{8,9},{9,8},{10,11... | collective-permute-start | bytes 589832 | tf_op jit(solution)/shard_map/ppermute | solution.py:473
  8.6 1.7 %collective-permute-done.5.refs_3_ = f32[2,96,128]{2,1,0:T(8,128)S(1)} collective-permute-done((f32[2,96,128]{2,1,0:T(8,128)S(1)}, f32[2,96,128]{2,1,0:T(8,128)S(1)}, u32[]{:S(2)}, u32[]{:S(2)}) %collective-permute-start.5) | collective-permute-done | bytes 98336 | tf_op jit(solution)/shard_map/ppermute | solution.py:494
  11.5 1.3 %collective-permute-done.7.refs_2_ = f32[4,48,128]{2,1,0:T(8,128)S(1)} collective-permute-done((f32[4,48,128]{2,1,0:T(8,128)S(1)}, f32[4,48,128]{2,1,0:T(8,128)S(1)}, u32[]{:S(2)}, u32[]{:S(2)}) %collective-permute-start.7) | collective-permute-done | bytes 98336 | tf_op jit(solution)/shard_map/ppermute | solution.py:477
  12.9 5.7 %collective-permute-start.10 = (f32[4,48,128]{2,1,0:T(8,128)S(1)}, f32[4,48,128]{2,1,0:T(8,128)S(1)}, u32[]{:S(2)}, u32[]{:S(2)}) collective-permute-start(f32[4,48,128]{2,1,0:T(8,128)S(1)} %shard_map.98.refs_1_), channel_id=1, source_target_pairs={{0,192},{8,200},{16,208},{24,216},{32,224},{40,232},{48,240},{56,2... | collective-permute-start | bytes 294920 | tf_op jit(solution)/shard_map/ppermute | solution.py:498
  19.5 2.8 %collective-permute-start.8 = (f32[4,48,128]{2,1,0:T(8,128)S(1)}, f32[4,48,128]{2,1,0:T(8,128)S(1)}, u32[]{:S(2)}, u32[]{:S(2)}) collective-permute-start(f32[4,48,128]{2,1,0:T(8,128)S(1)} %shard_map.98.refs_1_), channel_id=1, source_target_pairs={{0,64},{8,72},{16,80},{24,88},{32,96},{40,104},{48,112},{56,120},{... | collective-permute-start | bytes 294920 | tf_op jit(solution)/shard_map/ppermute | solution.py:498
  22.4 1.7 %collective-permute-start.1 = (f32[2,384,128]{2,1,0:T(8,128)S(1)}, f32[2,384,128]{2,1,0:T(8,128)S(1)}, u32[]{:S(2)}, u32[]{:S(2)}) collective-permute-start(f32[2,384,128]{2,1,0:T(8,128)S(1)} %shard_map.96.refs_0_), channel_id=1, source_target_pairs={{0,2},{1,3},{2,4},{3,5},{4,6},{5,7},{6,0},{7,1},{8,10},{9,11},{10,... | collective-permute-start | bytes 1179656 | tf_op jit(solution)/shard_map/ppermute | solution.py:491
  24.1 3.2 %collective-permute-done.10.refs_4_ = f32[4,48,128]{2,1,0:T(8,128)S(1)} collective-permute-done((f32[4,48,128]{2,1,0:T(8,128)S(1)}, f32[4,48,128]{2,1,0:T(8,128)S(1)}, u32[]{:S(2)}, u32[]{:S(2)}) %collective-permute-start.10) | collective-permute-done | bytes 98336 | tf_op jit(solution)/shard_map/ppermute | solution.py:498
  27.3 3.5 %collective-permute-done.9.refs_3_ = f32[4,48,128]{2,1,0:T(8,128)S(1)} collective-permute-done((f32[4,48,128]{2,1,0:T(8,128)S(1)}, f32[4,48,128]{2,1,0:T(8,128)S(1)}, u32[]{:S(2)}, u32[]{:S(2)}) %collective-permute-start.9) | collective-permute-done | bytes 98336 | tf_op jit(solution)/shard_map/ppermute | solution.py:498
  31.5 4.5 %all-to-all-start = ((f32[8,48,128]{2,1,0:T(8,128)}), f32[8,48,128]{2,1,0:T(8,128)S(1)}, u32[]{:S(2)}, u32[]{:S(2)}) async-start(f32[8,48,128]{2,1,0:T(8,128)} %shard_map.99), calls=%async_computation | async-start | bytes 393216 | tf_op jit(solution)/shard_map/all_to_all | solution.py:500
  35.9 3.2 %collective-permute-start.3 = (f32[2,384,128]{2,1,0:T(8,128)S(1)}, f32[2,384,128]{2,1,0:T(8,128)S(1)}, u32[]{:S(2)}, u32[]{:S(2)}) collective-permute-start(f32[2,384,128]{2,1,0:T(8,128)S(1)} %shard_map.96.refs_0_), channel_id=1, source_target_pairs={{0,6},{1,7},{2,0},{3,1},{4,2},{5,3},{6,4},{7,5},{8,14},{9,15},{10,... | collective-permute-start | bytes 1179656 | tf_op jit(solution)/shard_map/ppermute | solution.py:491
  39.2 3.7 %all-to-all-done.refs_4_ = f32[8,48,128]{2,1,0:T(8,128)S(1)} async-done(((f32[8,48,128]{2,1,0:T(8,128)}), f32[8,48,128]{2,1,0:T(8,128)S(1)}, u32[]{:S(2)}, u32[]{:S(2)}) %all-to-all-start) | async-done | bytes 196640 | tf_op jit(solution)/shard_map/all_to_all | solution.py:500
  43.6 2.1 %collective-permute-start.12 = (f32[8,48,128]{2,1,0:T(8,128)S(1)}, f32[8,48,128]{2,1,0:T(8,128)S(1)}, u32[]{:S(2)}, u32[]{:S(2)}) collective-permute-start(f32[8,48,128]{2,1,0:T(8,128)S(1)} %all-to-all-done.refs_4_), channel_id=1, source_target_pairs={{0,32},{8,40},{16,48},{24,56},{32,0},{40,8},{48,16},{56,24},{64,96... | collective-permute-start | bytes 589832 | tf_op jit(solution)/shard_map/ppermute | solution.py:501
  46.1 2.1 %collective-permute-start.11 = (f32[8,48,128]{2,1,0:T(8,128)S(1)}, f32[8,48,128]{2,1,0:T(8,128)S(1)}, u32[]{:S(2)}, u32[]{:S(2)}) collective-permute-start(f32[8,48,128]{2,1,0:T(8,128)S(1)} %all-to-all-done.refs_4_), channel_id=1, source_target_pairs={{0,16},{8,24},{16,32},{24,40},{32,48},{40,56},{48,0},{56,8},{64,80... | collective-permute-start | bytes 589832 | tf_op jit(solution)/shard_map/ppermute | solution.py:501
  48.2 2.1 %collective-permute-done.13.refs_7_ = f32[8,48,128]{2,1,0:T(8,128)S(1)} collective-permute-done((f32[8,48,128]{2,1,0:T(8,128)S(1)}, f32[8,48,128]{2,1,0:T(8,128)S(1)}, u32[]{:S(2)}, u32[]{:S(2)}) %collective-permute-start.13) | collective-permute-done | bytes 196640 | tf_op jit(solution)/shard_map/ppermute | solution.py:501
  50.3 2.1 %collective-permute-done.12.refs_6_ = f32[8,48,128]{2,1,0:T(8,128)S(1)} collective-permute-done((f32[8,48,128]{2,1,0:T(8,128)S(1)}, f32[8,48,128]{2,1,0:T(8,128)S(1)}, u32[]{:S(2)}, u32[]{:S(2)}) %collective-permute-start.12) | collective-permute-done | bytes 196640 | tf_op jit(solution)/shard_map/ppermute | solution.py:501
  53.4 1.6 %collective-permute-done.2.refs_2_ = f32[2,384,128]{2,1,0:T(8,128)S(1)} collective-permute-done((f32[2,384,128]{2,1,0:T(8,128)S(1)}, f32[2,384,128]{2,1,0:T(8,128)S(1)}, u32[]{:S(2)}, u32[]{:S(2)}) %collective-permute-start.2) | collective-permute-done | bytes 393248 | tf_op jit(solution)/shard_map/ppermute | solution.py:492
  55.1 8.2 %shard_map.100 = (f32[8,384,128]{2,1,0:T(8,128)S(1)}, f32[4,96,128]{2,1,0:T(8,128)S(1)}, f32[4,96,128]{2,1,0:T(8,128)S(1)}, f32[4,96,128]{2,1,0:T(8,128)S(1)}, f...) custom-call(f32[2,384,128]{2,1,0:T(8,128)S(1)} %shard_map.96.refs_0_, ...), custom_call_target="tpu_custom_call" | custom-call | flops 10000000000 | bytes 8454144 | tf_op jit(solution)/shard_map/pallas_call | solution.py:116
  65.5 2.1 %collective-permute-start.27 = (f32[4,96,128]{2,1,0:T(8,128)S(1)}, f32[4,96,128]{2,1,0:T(8,128)S(1)}, u32[]{:S(2)}, u32[]{:S(2)}) collective-permute-start(f32[4,96,128]{2,1,0:T(8,128)S(1)} %get-tuple-element.56), channel_id=1, source_target_pairs={{0,32},{8,40},{16,48},{24,56},{32,0},{40,8},{48,16},{56,24},{64,96... | collective-permute-start | bytes 589832 | tf_op jit(solution)/shard_map/ppermute | solution.py:508
  68.2 2.1 %collective-permute-start.22 = (f32[2,384,128]{2,1,0:T(8,128)S(1)}, f32[2,384,128]{2,1,0:T(8,128)S(1)}, u32[]{:S(2)}, u32[]{:S(2)}) collective-permute-start(f32[2,384,128]{2,1,0:T(8,128)S(1)} %get-tuple-element.50), channel_id=1, source_target_pairs={{0,4},{1,5},{2,6},{3,7},{4,0},{5,1},{6,2},{7,3},{8,12},{9,13},{10,... | collective-permute-start | bytes 1179656 | tf_op jit(solution)/shard_map/ppermute | solution.py:510
  70.3 1.6 %collective-permute-start.23 = (f32[2,384,128]{2,1,0:T(8,128)S(1)}, f32[2,384,128]{2,1,0:T(8,128)S(1)}, u32[]{:S(2)}, u32[]{:S(2)}) collective-permute-start(f32[2,384,128]{2,1,0:T(8,128)S(1)} %get-tuple-element.51), channel_id=1, source_target_pairs={{0,6},{1,7},{2,0},{3,1},{4,2},{5,3},{6,4},{7,5},{8,14},{9,15},{10,... | collective-permute-start | bytes 1179656 | tf_op jit(solution)/shard_map/ppermute | solution.py:510
  71.9 1.4 %collective-permute-start.28 = (f32[4,96,128]{2,1,0:T(8,128)S(1)}, f32[4,96,128]{2,1,0:T(8,128)S(1)}, u32[]{:S(2)}, u32[]{:S(2)}) collective-permute-start(f32[4,96,128]{2,1,0:T(8,128)S(1)} %get-tuple-element.57), channel_id=1, source_target_pairs={{0,48},{8,56},{16,0},{24,8},{32,16},{40,24},{48,32},{56,40},{64,11... | collective-permute-start | bytes 589832 | tf_op jit(solution)/shard_map/ppermute | solution.py:508
  74.2 2.0 %collective-permute-start.26 = (f32[4,96,128]{2,1,0:T(8,128)S(1)}, f32[4,96,128]{2,1,0:T(8,128)S(1)}, u32[]{:S(2)}, u32[]{:S(2)}) collective-permute-start(f32[4,96,128]{2,1,0:T(8,128)S(1)} %get-tuple-element.47.refs_1_), channel_id=1, source_target_pairs={{0,16},{8,24},{16,32},{24,40},{32,48},{40,56},{48,0},{56,8},{64,80... | collective-permute-start | bytes 589832 | tf_op jit(solution)/shard_map/ppermute | solution.py:508
  76.2 2.2 %collective-permute-done.28.refs_4_ = f32[4,96,128]{2,1,0:T(8,128)S(1)} collective-permute-done((f32[4,96,128]{2,1,0:T(8,128)S(1)}, f32[4,96,128]{2,1,0:T(8,128)S(1)}, u32[]{:S(2)}, u32[]{:S(2)}) %collective-permute-start.28) | collective-permute-done | bytes 196640 | tf_op jit(solution)/shard_map/ppermute | solution.py:508
  78.4 2.8 %collective-permute-done.26.refs_2_ = f32[4,96,128]{2,1,0:T(8,128)S(1)} collective-permute-done((f32[4,96,128]{2,1,0:T(8,128)S(1)}, f32[4,96,128]{2,1,0:T(8,128)S(1)}, u32[]{:S(2)}, u32[]{:S(2)}) %collective-permute-start.26) | collective-permute-done | bytes 196640 | tf_op jit(solution)/shard_map/ppermute | solution.py:508
  81.3 2.8 %collective-permute-start.29 = (f32[96,128]{1,0:T(8,128)S(1)}, f32[96,128]{1,0:T(8,128)S(1)}, u32[]{:S(2)}, u32[]{:S(2)}) collective-permute-start(f32[96,128]{1,0:T(8,128)S(1)} %get-tuple-element.59), channel_id=1, source_target_pairs={{0,64},{8,72},{16,80},{24,88},{32,96},{40,104},{48,112},{56,120},{... | collective-permute-start | bytes 147464 | tf_op jit(solution)/shard_map/ppermute | solution.py:512
  84.0 3.8 %collective-permute-start.30 = (f32[96,128]{1,0:T(8,128)S(1)}, f32[96,128]{1,0:T(8,128)S(1)}, u32[]{:S(2)}, u32[]{:S(2)}) collective-permute-start(f32[96,128]{1,0:T(8,128)S(1)} %get-tuple-element.60), channel_id=1, source_target_pairs={{0,128},{8,136},{16,144},{24,152},{32,160},{40,168},{48,176},{56,1... | collective-permute-start | bytes 147464 | tf_op jit(solution)/shard_map/ppermute | solution.py:512
  88.4 4.1 %collective-permute-start.31 = (f32[96,128]{1,0:T(8,128)S(1)}, f32[96,128]{1,0:T(8,128)S(1)}, u32[]{:S(2)}, u32[]{:S(2)}) collective-permute-start(f32[96,128]{1,0:T(8,128)S(1)} %get-tuple-element.61), channel_id=1, source_target_pairs={{0,192},{8,200},{16,208},{24,216},{32,224},{40,232},{48,240},{56,2... | collective-permute-start | bytes 147464 | tf_op jit(solution)/shard_map/ppermute | solution.py:512
  93.4 1.2 %collective-permute-done.31.refs_3_ = f32[96,128]{1,0:T(8,128)S(1)} collective-permute-done((f32[96,128]{1,0:T(8,128)S(1)}, f32[96,128]{1,0:T(8,128)S(1)}, u32[]{:S(2)}, u32[]{:S(2)}) %collective-permute-start.31) | collective-permute-done | bytes 49184 | tf_op jit(solution)/shard_map/ppermute | solution.py:512
  95.4 3.4 %all-to-all-start.1 = ((f32[8,24,128]{2,1,0:T(8,128)}), f32[8,24,128]{2,1,0:T(8,128)S(1)}, u32[]{:S(2)}, u32[]{:S(2)}) async-start(f32[8,24,128]{2,1,0:T(8,128)} %shard_map.106), calls=%async_computation.1 | async-start | bytes 196608 | tf_op jit(solution)/shard_map/all_to_all | solution.py:522
  99.8 5.5 %all-to-all-done.1.refs_0_ = f32[8,24,128]{2,1,0:T(8,128)S(1)} async-done(((f32[8,24,128]{2,1,0:T(8,128)}), f32[8,24,128]{2,1,0:T(8,128)S(1)}, u32[]{:S(2)}, u32[]{:S(2)}) %all-to-all-start.1) | async-done | bytes 98336 | tf_op jit(solution)/shard_map/all_to_all | solution.py:522
  (67 shorter events, 14.4 us)
Async XLA Ops:
  1.9 6.8 %collective-permute-start.4 = (f32[2,96,128]{2,1,0:T(8,128)S(1)}, f32[2,96,128]{2,1,0:T(8,128)S(1)}, u32[]{:S(2)}, u32[]{:S(2)}) collective-permute-start(f32[2,96,128]{2,1,0:T(8,128)S(1)} %get-tuple-element.35), channel_id=1, source_target_pairs={{0,16},{8,24},{16,32},{24,40},{32,48},{40,56},{48,0},{56,8},{64,80... | collective-permute-start | bytes 294920 | tf_op jit(solution)/shard_map/ppermute | solution.py:494
  3.5 6.9 %collective-permute-start.5 = (f32[2,96,128]{2,1,0:T(8,128)S(1)}, f32[2,96,128]{2,1,0:T(8,128)S(1)}, u32[]{:S(2)}, u32[]{:S(2)}) collective-permute-start(f32[2,96,128]{2,1,0:T(8,128)S(1)} %get-tuple-element.36), channel_id=1, source_target_pairs={{0,32},{8,40},{16,48},{24,56},{32,0},{40,8},{48,16},{56,24},{64,96... | collective-permute-start | bytes 294920 | tf_op jit(solution)/shard_map/ppermute | solution.py:494
  6.3 5.0 %collective-permute-start.6 = (f32[2,96,128]{2,1,0:T(8,128)S(1)}, f32[2,96,128]{2,1,0:T(8,128)S(1)}, u32[]{:S(2)}, u32[]{:S(2)}) collective-permute-start(f32[2,96,128]{2,1,0:T(8,128)S(1)} %get-tuple-element.37), channel_id=1, source_target_pairs={{0,48},{8,56},{16,0},{24,8},{32,16},{40,24},{48,32},{56,40},{64,11... | collective-permute-start | bytes 294920 | tf_op jit(solution)/shard_map/ppermute | solution.py:494
  6.7 15.7 %collective-permute-start = (f32[384,128]{1,0:T(8,128)S(1)}, f32[384,128]{1,0:T(8,128)S(1)}, u32[]{:S(2)}, u32[]{:S(2)}) collective-permute-start(f32[384,128]{1,0:T(8,128)S(1)} %get-tuple-element.33), channel_id=1, source_target_pairs={{0,1},{1,0},{2,3},{3,2},{4,5},{5,4},{6,7},{7,6},{8,9},{9,8},{10,11... | collective-permute-start | bytes 589832 | tf_op jit(solution)/shard_map/ppermute | solution.py:473
  12.9 14.4 %collective-permute-start.10 = (f32[4,48,128]{2,1,0:T(8,128)S(1)}, f32[4,48,128]{2,1,0:T(8,128)S(1)}, u32[]{:S(2)}, u32[]{:S(2)}) collective-permute-start(f32[4,48,128]{2,1,0:T(8,128)S(1)} %shard_map.98.refs_1_), channel_id=1, source_target_pairs={{0,192},{8,200},{16,208},{24,216},{32,224},{40,232},{48,240},{56,2... | collective-permute-start | bytes 294920 | tf_op jit(solution)/shard_map/ppermute | solution.py:498
  18.6 12.2 %collective-permute-start.9 = (f32[4,48,128]{2,1,0:T(8,128)S(1)}, f32[4,48,128]{2,1,0:T(8,128)S(1)}, u32[]{:S(2)}, u32[]{:S(2)}) collective-permute-start(f32[4,48,128]{2,1,0:T(8,128)S(1)} %shard_map.98.refs_1_), channel_id=1, source_target_pairs={{0,128},{8,136},{16,144},{24,152},{32,160},{40,168},{48,176},{56,1... | collective-permute-start | bytes 294920 | tf_op jit(solution)/shard_map/ppermute | solution.py:498
  19.5 11.2 %collective-permute-start.8 = (f32[4,48,128]{2,1,0:T(8,128)S(1)}, f32[4,48,128]{2,1,0:T(8,128)S(1)}, u32[]{:S(2)}, u32[]{:S(2)}) collective-permute-start(f32[4,48,128]{2,1,0:T(8,128)S(1)} %shard_map.98.refs_1_), channel_id=1, source_target_pairs={{0,64},{8,72},{16,80},{24,88},{32,96},{40,104},{48,112},{56,120},{... | collective-permute-start | bytes 294920 | tf_op jit(solution)/shard_map/ppermute | solution.py:498
  22.4 23.2 %collective-permute-start.1 = (f32[2,384,128]{2,1,0:T(8,128)S(1)}, f32[2,384,128]{2,1,0:T(8,128)S(1)}, u32[]{:S(2)}, u32[]{:S(2)}) collective-permute-start(f32[2,384,128]{2,1,0:T(8,128)S(1)} %shard_map.96.refs_0_), channel_id=1, source_target_pairs={{0,2},{1,3},{2,4},{3,5},{4,6},{5,7},{6,0},{7,1},{8,10},{9,11},{10,... | collective-permute-start | bytes 1179656 | tf_op jit(solution)/shard_map/ppermute | solution.py:491
  31.5 11.4 %all-to-all-start = ((f32[8,48,128]{2,1,0:T(8,128)}), f32[8,48,128]{2,1,0:T(8,128)S(1)}, u32[]{:S(2)}, u32[]{:S(2)}) async-start(f32[8,48,128]{2,1,0:T(8,128)} %shard_map.99), calls=%async_computation | async-start | bytes 393216 | tf_op jit(solution)/shard_map/all_to_all | solution.py:500
  35.9 12.2 %collective-permute-start.3 = (f32[2,384,128]{2,1,0:T(8,128)S(1)}, f32[2,384,128]{2,1,0:T(8,128)S(1)}, u32[]{:S(2)}, u32[]{:S(2)}) collective-permute-start(f32[2,384,128]{2,1,0:T(8,128)S(1)} %shard_map.96.refs_0_), channel_id=1, source_target_pairs={{0,6},{1,7},{2,0},{3,1},{4,2},{5,3},{6,4},{7,5},{8,14},{9,15},{10,... | collective-permute-start | bytes 1179656 | tf_op jit(solution)/shard_map/ppermute | solution.py:491
  42.9 7.4 %collective-permute-start.13 = (f32[8,48,128]{2,1,0:T(8,128)S(1)}, f32[8,48,128]{2,1,0:T(8,128)S(1)}, u32[]{:S(2)}, u32[]{:S(2)}) collective-permute-start(f32[8,48,128]{2,1,0:T(8,128)S(1)} %all-to-all-done.refs_4_), channel_id=1, source_target_pairs={{0,48},{8,56},{16,0},{24,8},{32,16},{40,24},{48,32},{56,40},{64,11... | collective-permute-start | bytes 589832 | tf_op jit(solution)/shard_map/ppermute | solution.py:501
  43.6 8.8 %collective-permute-start.12 = (f32[8,48,128]{2,1,0:T(8,128)S(1)}, f32[8,48,128]{2,1,0:T(8,128)S(1)}, u32[]{:S(2)}, u32[]{:S(2)}) collective-permute-start(f32[8,48,128]{2,1,0:T(8,128)S(1)} %all-to-all-done.refs_4_), channel_id=1, source_target_pairs={{0,32},{8,40},{16,48},{24,56},{32,0},{40,8},{48,16},{56,24},{64,96... | collective-permute-start | bytes 589832 | tf_op jit(solution)/shard_map/ppermute | solution.py:501
  45.7 9.4 %collective-permute-start.2 = (f32[2,384,128]{2,1,0:T(8,128)S(1)}, f32[2,384,128]{2,1,0:T(8,128)S(1)}, u32[]{:S(2)}, u32[]{:S(2)}) collective-permute-start(f32[2,384,128]{2,1,0:T(8,128)S(1)} %collective-permute-done.1.refs_1_), channel_id=1, source_target_pairs={{0,2},{1,3},{2,4},{3,5},{4,6},{5,7},{6,0},{7,1},{8,10},{9,11},{10,... | collective-permute-start | bytes 1179656 | tf_op jit(solution)/shard_map/ppermute | solution.py:492
  46.1 7.3 %collective-permute-start.11 = (f32[8,48,128]{2,1,0:T(8,128)S(1)}, f32[8,48,128]{2,1,0:T(8,128)S(1)}, u32[]{:S(2)}, u32[]{:S(2)}) collective-permute-start(f32[8,48,128]{2,1,0:T(8,128)S(1)} %all-to-all-done.refs_4_), channel_id=1, source_target_pairs={{0,16},{8,24},{16,32},{24,40},{32,48},{40,56},{48,0},{56,8},{64,80... | collective-permute-start | bytes 589832 | tf_op jit(solution)/shard_map/ppermute | solution.py:501
  48.2 5.3 %collective-permute-start.14 = (f32[8,48,128]{2,1,0:T(8,128)S(1)}, f32[8,48,128]{2,1,0:T(8,128)S(1)}, u32[]{:S(2)}, u32[]{:S(2)}) collective-permute-start(f32[8,48,128]{2,1,0:T(8,128)S(1)} %all-to-all-done.refs_4_), channel_id=1, source_target_pairs={{0,8},{8,0},{16,24},{24,16},{32,40},{40,32},{48,56},{56,48},{64,72... | collective-permute-start | bytes 589832 | tf_op jit(solution)/shard_map/ppermute | solution.py:477
  50.3 4.8 %collective-permute-start.17 = (f32[8,48,128]{2,1,0:T(8,128)S(1)}, f32[8,48,128]{2,1,0:T(8,128)S(1)}, u32[]{:S(2)}, u32[]{:S(2)}) collective-permute-start(f32[8,48,128]{2,1,0:T(8,128)S(1)} %collective-permute-done.13.refs_7_), channel_id=1, source_target_pairs={{0,8},{8,0},{16,24},{24,16},{32,40},{40,32},{48,56},{56,48},{64,72... | collective-permute-start | bytes 589832 | tf_op jit(solution)/shard_map/ppermute | solution.py:477
  52.4 2.7 %collective-permute-start.16 = (f32[8,48,128]{2,1,0:T(8,128)S(1)}, f32[8,48,128]{2,1,0:T(8,128)S(1)}, u32[]{:S(2)}, u32[]{:S(2)}) collective-permute-start(f32[8,48,128]{2,1,0:T(8,128)S(1)} %collective-permute-done.12.refs_6_), channel_id=1, source_target_pairs={{0,8},{8,0},{16,24},{24,16},{32,40},{40,32},{48,56},{56,48},{64,72... | collective-permute-start | bytes 589832 | tf_op jit(solution)/shard_map/ppermute | solution.py:477
  53.4 1.6 %collective-permute-start.15 = (f32[8,48,128]{2,1,0:T(8,128)S(1)}, f32[8,48,128]{2,1,0:T(8,128)S(1)}, u32[]{:S(2)}, u32[]{:S(2)}) collective-permute-start(f32[8,48,128]{2,1,0:T(8,128)S(1)} %collective-permute-done.11.refs_5_), channel_id=1, source_target_pairs={{0,8},{8,0},{16,24},{24,16},{32,40},{40,32},{48,56},{56,48},{64,72... | collective-permute-start | bytes 589832 | tf_op jit(solution)/shard_map/ppermute | solution.py:477
  63.4 1.5 %collective-permute-start.18 = (f32[4,96,128]{2,1,0:T(8,128)S(1)}, f32[4,96,128]{2,1,0:T(8,128)S(1)}, u32[]{:S(2)}, u32[]{:S(2)}) collective-permute-start(f32[4,96,128]{2,1,0:T(8,128)S(1)} %get-tuple-element.44), channel_id=1, source_target_pairs={{0,8},{8,0},{16,24},{24,16},{32,40},{40,32},{48,56},{56,48},{64,72... | collective-permute-start | bytes 589832 | tf_op jit(solution)/shard_map/ppermute | solution.py:477
  63.5 1.7 %collective-permute-start.19 = (f32[4,96,128]{2,1,0:T(8,128)S(1)}, f32[4,96,128]{2,1,0:T(8,128)S(1)}, u32[]{:S(2)}, u32[]{:S(2)}) collective-permute-start(f32[4,96,128]{2,1,0:T(8,128)S(1)} %get-tuple-element.45), channel_id=1, source_target_pairs={{0,8},{8,0},{16,24},{24,16},{32,40},{40,32},{48,56},{56,48},{64,72... | collective-permute-start | bytes 589832 | tf_op jit(solution)/shard_map/ppermute | solution.py:477
  64.1 7.8 %collective-permute-start.25 = (f32[4,96,128]{2,1,0:T(8,128)S(1)}, f32[4,96,128]{2,1,0:T(8,128)S(1)}, u32[]{:S(2)}, u32[]{:S(2)}) collective-permute-start(f32[4,96,128]{2,1,0:T(8,128)S(1)} %get-tuple-element.55), channel_id=1, source_target_pairs={{0,8},{8,0},{16,24},{24,16},{32,40},{40,32},{48,56},{56,48},{64,72... | collective-permute-start | bytes 589832 | tf_op jit(solution)/shard_map/ppermute | solution.py:477
  65.5 8.6 %collective-permute-start.27 = (f32[4,96,128]{2,1,0:T(8,128)S(1)}, f32[4,96,128]{2,1,0:T(8,128)S(1)}, u32[]{:S(2)}, u32[]{:S(2)}) collective-permute-start(f32[4,96,128]{2,1,0:T(8,128)S(1)} %get-tuple-element.56), channel_id=1, source_target_pairs={{0,32},{8,40},{16,48},{24,56},{32,0},{40,8},{48,16},{56,24},{64,96... | collective-permute-start | bytes 589832 | tf_op jit(solution)/shard_map/ppermute | solution.py:508
  67.8 20.7 %collective-permute-start.21 = (f32[2,384,128]{2,1,0:T(8,128)S(1)}, f32[2,384,128]{2,1,0:T(8,128)S(1)}, u32[]{:S(2)}, u32[]{:S(2)}) collective-permute-start(f32[2,384,128]{2,1,0:T(8,128)S(1)} %get-tuple-element.49), channel_id=1, source_target_pairs={{0,2},{1,3},{2,4},{3,5},{4,6},{5,7},{6,0},{7,1},{8,10},{9,11},{10,... | collective-permute-start | bytes 1179656 | tf_op jit(solution)/shard_map/ppermute | solution.py:510
  68.2 24.3 %collective-permute-start.22 = (f32[2,384,128]{2,1,0:T(8,128)S(1)}, f32[2,384,128]{2,1,0:T(8,128)S(1)}, u32[]{:S(2)}, u32[]{:S(2)}) collective-permute-start(f32[2,384,128]{2,1,0:T(8,128)S(1)} %get-tuple-element.50), channel_id=1, source_target_pairs={{0,4},{1,5},{2,6},{3,7},{4,0},{5,1},{6,2},{7,3},{8,12},{9,13},{10,... | collective-permute-start | bytes 1179656 | tf_op jit(solution)/shard_map/ppermute | solution.py:510
  70.3 22.2 %collective-permute-start.23 = (f32[2,384,128]{2,1,0:T(8,128)S(1)}, f32[2,384,128]{2,1,0:T(8,128)S(1)}, u32[]{:S(2)}, u32[]{:S(2)}) collective-permute-start(f32[2,384,128]{2,1,0:T(8,128)S(1)} %get-tuple-element.51), channel_id=1, source_target_pairs={{0,6},{1,7},{2,0},{3,1},{4,2},{5,3},{6,4},{7,5},{8,14},{9,15},{10,... | collective-permute-start | bytes 1179656 | tf_op jit(solution)/shard_map/ppermute | solution.py:510
  71.9 6.5 %collective-permute-start.28 = (f32[4,96,128]{2,1,0:T(8,128)S(1)}, f32[4,96,128]{2,1,0:T(8,128)S(1)}, u32[]{:S(2)}, u32[]{:S(2)}) collective-permute-start(f32[4,96,128]{2,1,0:T(8,128)S(1)} %get-tuple-element.57), channel_id=1, source_target_pairs={{0,48},{8,56},{16,0},{24,8},{32,16},{40,24},{48,32},{56,40},{64,11... | collective-permute-start | bytes 589832 | tf_op jit(solution)/shard_map/ppermute | solution.py:508
  74.2 7.0 %collective-permute-start.26 = (f32[4,96,128]{2,1,0:T(8,128)S(1)}, f32[4,96,128]{2,1,0:T(8,128)S(1)}, u32[]{:S(2)}, u32[]{:S(2)}) collective-permute-start(f32[4,96,128]{2,1,0:T(8,128)S(1)} %get-tuple-element.47.refs_1_), channel_id=1, source_target_pairs={{0,16},{8,24},{16,32},{24,40},{32,48},{40,56},{48,0},{56,8},{64,80... | collective-permute-start | bytes 589832 | tf_op jit(solution)/shard_map/ppermute | solution.py:508
  81.3 12.2 %collective-permute-start.29 = (f32[96,128]{1,0:T(8,128)S(1)}, f32[96,128]{1,0:T(8,128)S(1)}, u32[]{:S(2)}, u32[]{:S(2)}) collective-permute-start(f32[96,128]{1,0:T(8,128)S(1)} %get-tuple-element.59), channel_id=1, source_target_pairs={{0,64},{8,72},{16,80},{24,88},{32,96},{40,104},{48,112},{56,120},{... | collective-permute-start | bytes 147464 | tf_op jit(solution)/shard_map/ppermute | solution.py:512
  84.0 9.4 %collective-permute-start.30 = (f32[96,128]{1,0:T(8,128)S(1)}, f32[96,128]{1,0:T(8,128)S(1)}, u32[]{:S(2)}, u32[]{:S(2)}) collective-permute-start(f32[96,128]{1,0:T(8,128)S(1)} %get-tuple-element.60), channel_id=1, source_target_pairs={{0,128},{8,136},{16,144},{24,152},{32,160},{40,168},{48,176},{56,1... | collective-permute-start | bytes 147464 | tf_op jit(solution)/shard_map/ppermute | solution.py:512
  88.4 6.2 %collective-permute-start.31 = (f32[96,128]{1,0:T(8,128)S(1)}, f32[96,128]{1,0:T(8,128)S(1)}, u32[]{:S(2)}, u32[]{:S(2)}) collective-permute-start(f32[96,128]{1,0:T(8,128)S(1)} %get-tuple-element.61), channel_id=1, source_target_pairs={{0,192},{8,200},{16,208},{24,216},{32,224},{40,232},{48,240},{56,2... | collective-permute-start | bytes 147464 | tf_op jit(solution)/shard_map/ppermute | solution.py:512
  92.6 6.2 %collective-permute-start.24 = (f32[384,128]{1,0:T(8,128)S(1)}, f32[384,128]{1,0:T(8,128)S(1)}, u32[]{:S(2)}, u32[]{:S(2)}) collective-permute-start(f32[384,128]{1,0:T(8,128)S(1)} %get-tuple-element.53), channel_id=1, source_target_pairs={{0,1},{1,0},{2,3},{3,2},{4,5},{5,4},{6,7},{7,6},{8,9},{9,8},{10,11... | collective-permute-start | bytes 589832 | tf_op jit(solution)/shard_map/ppermute | solution.py:473
  95.4 9.8 %all-to-all-start.1 = ((f32[8,24,128]{2,1,0:T(8,128)}), f32[8,24,128]{2,1,0:T(8,128)S(1)}, u32[]{:S(2)}, u32[]{:S(2)}) async-start(f32[8,24,128]{2,1,0:T(8,128)} %shard_map.106), calls=%async_computation.1 | async-start | bytes 196608 | tf_op jit(solution)/shard_map/all_to_all | solution.py:522
  (9 other events, 333.8 us)
